TPU v7x, 32 devices: a whole 2x2x4 slice. The times are simulated.
32 devices in a mesh: xy: 16 (over z, x, core), gz: 2 (over y).
Axes of the slice: x: 2, y: 2, z: 4, core: 2. Of those that a mesh axis runs over, the one named last changes fastest.
Arguments:
- file_data: float32 [512, 64, 4096], P('gz', None, 'xy')
- factor: float32 [512, 256], P('gz'), may hold values from -0.25 to 0.25
- block_owner: int32 [32], replicated, may hold values from 0 to 15, as said below
- block_offset: int32 [32], replicated, may hold values from 0 to 128, as said below
Outputs:
- gram: float32 [512, 512], P('gz')
- core: float32 [256, 64, 4096], P('gz', None, 'xy')
Inputs may be any that keep to these rules, and one draw needn't show every extreme that they name: `block_owner`: block b of device d (b = d * 2 + j) is owned by d - 1, d or d + 1 modulo 16. Every index of xy owns exactly 2 blocks. `block_offset`: offsets are multiples of 128; the blocks of one owner take distinct offsets, so every file slot is named once.
All inputs are finite; a program needn't handle non-finite values.
Results may differ from a plain program's by a relative error of at most 0.00007.
Values sent between devices are 32-bit elements; how exact they have to be, the bound alone decides.
No kernel may reach another device: no remote copies, remote signals or barrier semaphores. Data moves between devices by JAX's collectives and lax.ppermute only.
A program may use at most 128 MiB of HBM per device.

v0:
```python
import jax
import jax.numpy as jnp
from jax import lax
from jax.sharding import PartitionSpec as P

BLOCKS_DEV = 2


def shifted(array, axis, by):
    length = lax.axis_size(axis)
    return lax.ppermute(array, axis, [(i, (i + by) % length) for i in range(length)])


def take_block(buffer, offset):
    return lax.dynamic_slice_in_dim(buffer, offset, 128, 2)


def rebalance(buffer, block_owner, block_offset):
    devices = lax.axis_size("xy")
    myself = lax.axis_index("xy")
    lower_peer = (myself + devices - 1) % devices
    upper_peer = (myself + 1) % devices
    blank = jnp.zeros(buffer.shape[:2] + (128,), buffer.dtype)

    def outgoing(target):
        pieces = []
        for j in range(BLOCKS_DEV):
            owner = block_owner[target * BLOCKS_DEV + j]
            offset = block_offset[target * BLOCKS_DEV + j]
            pieces.append(jnp.where(owner == myself, take_block(buffer, offset), blank))
        return jnp.concatenate(pieces, axis=2)

    from_lower = shifted(outgoing(upper_peer), "xy", 1)
    from_upper = shifted(outgoing(lower_peer), "xy", -1)
    blocks = []
    for j in range(BLOCKS_DEV):
        owner = block_owner[myself * BLOCKS_DEV + j]
        offset = block_offset[myself * BLOCKS_DEV + j]
        local_block = take_block(buffer, offset)
        lower_block = from_lower[:, :, j * 128 : (j + 1) * 128]
        upper_block = from_upper[:, :, j * 128 : (j + 1) * 128]
        remote = jnp.where(owner == lower_peer, lower_block, upper_block)
        blocks.append(jnp.where(owner == myself, local_block, remote))
    return jnp.concatenate(blocks, axis=2)


def used_slots(file_data, block_owner, block_offset):
    myself = lax.axis_index("xy")
    slot_count = file_data.shape[2] // 128
    hits = (block_owner[:, None] == myself) & (
        block_offset[:, None] // 128 == jnp.arange(slot_count, dtype=jnp.int32)[None, :]
    )
    used = jnp.any(hits, axis=0).astype(jnp.float32)
    return jnp.repeat(used, 128)


def local(file_data, factor, block_owner, block_offset):
    working = file_data * used_slots(file_data, block_owner, block_offset)[None, None, :]
    swapped = lax.all_to_all(working, "gz", split_axis=1, concat_axis=0, tiled=True)
    scale = 1.0 / (BLOCKS_DEV * 128 * lax.axis_size("xy") * file_data.shape[1])
    partial_gram = (
        jnp.einsum("zcs,wcs->zw", swapped, swapped, precision=lax.Precision.HIGHEST) * scale
    )
    z_local = file_data.shape[0]
    full_gram = lax.psum(partial_gram, ("xy", "gz"))
    gram = lax.dynamic_slice_in_dim(full_gram, lax.axis_index("gz") * z_local, z_local, 0)
    whole_factor = lax.all_gather(factor, "gz", axis=0, tiled=True)
    core_part = jnp.einsum("zr,zcs->rcs", whole_factor, swapped, precision=lax.Precision.HIGHEST)
    core = lax.all_to_all(core_part, "gz", split_axis=0, concat_axis=1, tiled=True)
    core = rebalance(core, block_owner, block_offset)
    return (gram, core)


def solution(mesh):
    return jax.shard_map(
        local,
        mesh=mesh,
        in_specs=(P("gz", None, "xy"), P("gz", None), P(), P()),
        out_specs=(P("gz", None), P("gz", None, "xy")),
        check_vma=False,
    )
```

profile of v0, /device:TPU:0, one launch (start us, length us, event | category | flops | bytes accessed | tf_op | source)
XLA Modules:
  0.0 640.3 jit_solution(5745485050651148054)
XLA Ops:
  7.2 0.7 and_select_fusion
  7.8 0.7 broadcast_compare_fusion
  8.5 0.1 and_reduce_fusion
  8.6 0.1 broadcast_bitcast_fusion
  8.7 17.9 %copy_multiply_fusion = f32[256,64,256]{2,0,1:T(8,128)} fusion(f32[256,64,256]{2,1,0:T(8,128)} %param.4, f32[256]{0:T(256)S(1)} %broadcast_bitcast_fusion), kind=kLoop, calls=%fused_computation | loop fusion | flops 4194304 | bytes 33555456 | tf_op jit(solution)/shard_map/mul | solution.py:58
  26.6 0.0 copy-start.1
  26.6 9.8 %all-to-all-start = ((f32[256,64,256]{2,0,1:T(8,128)}), f32[256,64,256]{2,0,1:T(8,128)}, u32[]{:S(2)}, u32[]{:S(2)}) async-start(f32[256,64,256]{2,0,1:T(8,128)} %copy_multiply_fusion), calls=%async_computation | async-start | bytes 33554432 | tf_op jit(solution)/shard_map/all_to_all | solution.py:59
  36.4 0.0 copy-done.1
  36.4 189.2 %all_gather.3 = f32[512,256]{1,0:T(8,128)S(1)} all-gather(f32[256,256]{1,0:T(8,128)S(1)} %copy-done.1), channel_id=1, replica_groups=mesh['xy'=16,'gz'=2] {'gz'}, dimensions={0}, use_global_device_ids=true | all-gather | bytes 786432 | tf_op jit(solution)/shard_map/all_gather | solution.py:67
  225.6 0.0 all-to-all-done
  225.7 6.8 %copy.15 = f32[256,2,32,256]{3,0,1,2:T(8,128)S(1)} copy(f32[256,2,32,256]{3,0,2,1:T(8,128)} %bitcast.1) | data formatting | bytes 33554432 | tf_op jit(solution)/shard_map/all_to_all | solution.py:59
  232.5 0.0 copy-start
  232.5 5.7 copy-done
  238.2 30.7 %convolution_bitcast_fusion = f32[256,32,256]{0,2,1:T(8,128)} fusion(f32[512,32,256]{2,0,1:T(8,128)S(1)} %bitcast.34, f32[512,256]{1,0:T(8,128)S(1)} %all_gather.3), kind=kOutput, calls=%fused_computation.12 | convolution fusion | flops 12884901888 | bytes 25690112 | tf_op jit(solution)/shard_map/zr,zcs->rcs/dot_general | solution.py:68
  269.0 10.3 %copy.17 = f32[256,32,256]{2,1,0:T(8,128)} copy(f32[256,32,256]{0,2,1:T(8,128)} %convolution_bitcast_fusion) | data formatting | bytes 16777216 | tf_op jit(solution)/shard_map/zr,zcs->rcs/dot_general | solution.py:68
  279.3 0.0 copy-start.2
  279.3 0.0 copy-start.3
  279.3 7.1 %all-to-all-start.1 = ((f32[256,32,256]{2,1,0:T(8,128)}), f32[256,32,256]{2,1,0:T(8,128)}, u32[]{:S(2)}, u32[]{:S(2)}) async-start(f32[256,32,256]{2,1,0:T(8,128)} %copy.17), calls=%async_computation.1 | async-start | bytes 16777216 | tf_op jit(solution)/shard_map/all_to_all | solution.py:69
  286.4 0.0 all-reduce.2.cloned.1.call-start
  286.4 0.0 copy-done.2
  286.5 0.0 copy-done.3
  286.5 0.7 fusion.4
  297.0 81.4 %all-to-all-done.1 = f32[256,32,256]{2,1,0:T(8,128)} async-done(((f32[256,32,256]{2,1,0:T(8,128)}), f32[256,32,256]{2,1,0:T(8,128)}, u32[]{:S(2)}, u32[]{:S(2)}) %all-to-all-start.1) | async-done | bytes 8388640 | tf_op jit(solution)/shard_map/all_to_all | solution.py:69
  378.4 8.4 %copy.18 = f32[128,2,32,256]{3,2,1,0:T(8,128)} copy(f32[128,2,32,256]{3,2,0,1:T(8,128)} %bitcast.10) | data formatting | bytes 16777216 | tf_op jit(solution)/shard_map/all_to_all | solution.py:69
  386.8 14.2 %dynamic-slice_select_fusion.3 = (f32[128,64,128]{2,1,0:T(8,128)S(1)}, f32[128,64,128]{2,1,0:T(8,128)}, f32[128,64,128]{2,1,0:T(8,128)}, f32[128,64,128]{2,1,0:T(8,128)}) fusion(f32[128,64,256]{2,1,0:T(8,128)} %bitcast.38, s32[]{:T(128)S(6)} %select_n.122, pred[]{:T(512)S(6)} %eq.54, s32[]{:T(128)S(6)} %select_n.134, pred[]{:T(512)S(6)} %eq.57, ...), kind=kLoop, calls=%fused_computation.11 | loop fusion | flops 4194304 | bytes 33554452 | tf_op jit(solution)/shard_map/jit(_where)/select_n | solution.py:30
  401.0 0.0 slice-start
  401.0 0.0 slice-start.1
  401.0 7.9 %pad_maximum_fusion.1 = f32[128,64,256]{2,1,0:T(8,128)} fusion(f32[128,64,128]{2,1,0:T(8,128)} %get-tuple-element.5, f32[128,64,128]{2,1,0:T(8,128)} %get-tuple-element.6), kind=kLoop, calls=%fused_computation.2 | loop fusion | flops 2097152 | bytes 16777216 | tf_op jit(solution)/shard_map/concatenate | solution.py:31
  408.9 2.1 collective-permute-start.1
  411.0 0.0 slice-start.2
  411.0 0.0 slice-start.3
  411.0 6.6 %pad_maximum_fusion = f32[128,64,256]{2,1,0:T(8,128)} fusion(f32[128,64,128]{2,1,0:T(8,128)} %get-tuple-element.7, f32[128,64,128]{2,1,0:T(8,128)S(1)} %get-tuple-element.4), kind=kLoop, calls=%fused_computation.1 | loop fusion | flops 2097152 | bytes 16777216 | tf_op jit(solution)/shard_map/concatenate | solution.py:31
  417.5 0.0 collective-permute-start
  417.5 0.0 slice-done
  417.5 0.0 slice-done.1
  417.6 0.0 slice-done.2
  417.6 0.0 slice-done.3
  417.6 28.7 %fusion.2 = f32[512,512]{1,0:T(8,128)} fusion(f32[512,32,256]{2,0,1:T(8,128)S(1)} %bitcast.37), kind=kOutput, calls=%fused_computation.14 | convolution fusion | flops 25770065920 | bytes 17825792 | tf_op jit(solution)/shard_map/zcs,wcs->zw/dot_general | solution.py:62
  446.3 0.0 all-reduce.2.cloned.1.call-update
  452.6 164.9 %all-reduce.2.cloned.1.call-done = f32[512,512]{1,0:T(8,128)} async-done(((f32[512,512]{1,0:T(8,128)}), f32[512,512]{1,0:T(8,128)}) %all-reduce.2.cloned.1.call-update) | async-done | bytes 1048592 | tf_op jit(solution)/shard_map/psum | solution.py:65
  617.5 1.9 constant_dynamic-slice_fusion
  619.4 0.0 collective-permute-done.1
  619.4 0.0 collective-permute-done
  619.4 9.7 %fusion.1 = (f32[128,64,128]{2,1,0:T(8,128)S(1)}, f32[128,64,128]{2,1,0:T(8,128)S(1)}) fusion(f32[128,64,256]{2,1,0:T(8,128)} %collective-permute-done.1, f32[128,64,256]{2,1,0:T(8,128)} %collective-permute-done, f32[128,64,256]{2,1,0:T(8,128)} %bitcast.39, s32[]{:T(128)S(6)} %select_n.116, pred[]{:T(512)S(6)} %eq.53, pred[]{:T(512)S(6)} %eq.52, pred[]{:T(512)S(6)} %eq.59, ...), kind=kLoop, calls=%fused_computation.7 | loop fusion | flops 4194304 | bytes 33554444 | tf_op jit(solution)/shard_map/jit(_where)/select_n | solution.py:43
  629.0 4.4 pad_maximum_fusion.2
  (2 shorter events, 0.0 us)
Async XLA Ops:
  26.6 9.8 %copy-start.1 = (f32[256,256]{1,0:T(8,128)S(1)}, f32[256,256]{1,0:T(8,128)}, u32[]{:S(2)}) copy-start(f32[256,256]{1,0:T(8,128)} %param.5) | copy-start | bytes 786436
  26.6 199.1 %all-to-all-start = ((f32[256,64,256]{2,0,1:T(8,128)}), f32[256,64,256]{2,0,1:T(8,128)}, u32[]{:S(2)}, u32[]{:S(2)}) async-start(f32[256,64,256]{2,0,1:T(8,128)} %copy_multiply_fusion), calls=%async_computation | async-start | bytes 33554432 | tf_op jit(solution)/shard_map/all_to_all | solution.py:59
  232.5 5.7 copy-start
  279.3 7.2 %copy-start.2 = (s32[32]{0:T(128)S(1)}, s32[32]{0:T(128)}, u32[]{:S(2)}) copy-start(s32[32]{0:T(128)} %param.6) | copy-start | bytes 388
  279.3 7.2 %copy-start.3 = (s32[32]{0:T(128)S(1)}, s32[32]{0:T(128)}, u32[]{:S(2)}) copy-start(s32[32]{0:T(128)} %param.7) | copy-start | bytes 388
  279.3 99.1 %all-to-all-start.1 = ((f32[256,32,256]{2,1,0:T(8,128)}), f32[256,32,256]{2,1,0:T(8,128)}, u32[]{:S(2)}, u32[]{:S(2)}) async-start(f32[256,32,256]{2,1,0:T(8,128)} %copy.17), calls=%async_computation.1 | async-start | bytes 16777216 | tf_op jit(solution)/shard_map/all_to_all | solution.py:69
  286.4 331.1 %all-reduce.2.cloned.1.call-start = ((), (), s32[]{:S(2)}) async-start(), calls=%async_computation.2 | async-start | bytes 2097152 | tf_op jit(solution)/shard_map/psum | solution.py:65
  401.0 16.5 %slice-start = ((s8[16777216]{0:T(1024)(128)(4,1)}), s8[4194304]{0:T(1024)(128)(4,1)S(1)}, s32[]{:S(2)}) async-start(s8[16777216]{0:T(1024)(128)(4,1)} %bitcast.35), calls=%async_computation.3 | async-start | bytes 8388608
  401.0 16.5 %slice-start.1 = ((s8[16777216]{0:T(1024)(128)(4,1)}), s8[4194304]{0:T(1024)(128)(4,1)S(1)}, s32[]{:S(2)}) async-start(s8[16777216]{0:T(1024)(128)(4,1)} %bitcast.35), calls=%async_computation.4 | async-start | bytes 8388608
  408.9 210.5 %collective-permute-start.1 = (f32[128,64,256]{2,1,0:T(8,128)}, f32[128,64,256]{2,1,0:T(8,128)}, u32[]{:S(2)}, u32[]{:S(2)}) collective-permute-start(f32[128,64,256]{2,1,0:T(8,128)} %pad_maximum_fusion.1), channel_id=1, source_target_pairs={{0,30},{2,0},{4,2},{6,4},{8,6},{10,8},{12,10},{14,12},{16,14},{18,... | collective-permute-start | bytes 25165832 | tf_op jit(solution)/shard_map/ppermute | solution.py:11
  411.0 6.6 %slice-start.2 = ((s8[16777216]{0:T(1024)(128)(4,1)}), s8[4194304]{0:T(1024)(128)(4,1)S(1)}, s32[]{:S(2)}) async-start(s8[16777216]{0:T(1024)(128)(4,1)} %bitcast.35), calls=%async_computation.5 | async-start | bytes 8388608
  411.0 6.6 %slice-start.3 = ((s8[16777216]{0:T(1024)(128)(4,1)}), s8[4194304]{0:T(1024)(128)(4,1)S(1)}, s32[]{:S(2)}) async-start(s8[16777216]{0:T(1024)(128)(4,1)} %bitcast.35), calls=%async_computation.6 | async-start | bytes 8388608
  417.5 201.8 %collective-permute-start = (f32[128,64,256]{2,1,0:T(8,128)}, f32[128,64,256]{2,1,0:T(8,128)}, u32[]{:S(2)}, u32[]{:S(2)}) collective-permute-start(f32[128,64,256]{2,1,0:T(8,128)} %pad_maximum_fusion), channel_id=1, source_target_pairs={{0,2},{2,4},{4,6},{6,8},{8,10},{10,12},{12,14},{14,16},{16,18},{18... | collective-permute-start | bytes 25165832 | tf_op jit(solution)/shard_map/ppermute | solution.py:11
Sparse Core Ops, SparseCore 0:
  446.4 171.0 all-reduce.1
where the time goes:
time: 645 us; the launch traced here: 640 us
  waiting for transfers between devices  246 us (38%)
  blocking collectives  189 us (29%)
  other arithmetic  62 us (10%)
  matrix products  59.4 us (9%)
  local copies, waits for them, and re-layouts  34 us (5%)
  between operations  30.3 us (5%)
  starting transfers between devices  19 us (3%)
    all_gather x1, blocking collectives, local(): whole_factor = lax.all_gather(factor, 'gz', axis=0, tiled=True)  189 us
    psum x1, waiting for transfers between devices, local(): full_gram = lax.psum(partial_gram, ('xy', 'gz'))  165 us
    all_to_all x1, waiting for transfers between devices, local(): lax.all_to_all(core_part, 'gz', split_axis=0, concat_axis=1, tiled=True)  81.4 us
    dot_general x1, matrix products, local(): jnp.einsum('zr,zcs->rcs', whole_factor, swapped, precision=lax.Precision....  30.7 us
    dot_general x1, matrix products, local(): jnp.einsum('zcs,wcs->zw', swapped, swapped, precision=lax.Precision.HIGHEST)  28.7 us
    mul x1, other arithmetic, local(): file_data * used_slots(file_data, block_owner, block_offset)[None, None, :]  17.9 us
    concatenate x2, other arithmetic, outgoing(): return jnp.concatenate(pieces, axis=2)  14.4 us
    select_n x1, other arithmetic, outgoing(): pieces.append(jnp.where(owner == myself, take_block(buffer, offset), blank))  14.2 us
  transfers between devices with their start and end apart: 5, of which 2 were waited for; matrix products, arithmetic and copies ran while one was open for 6% of the time, Pallas kernels for 0%

commit v1 on v0

v1 whole, which is shorter than its diff:
```python
import functools

import jax
import jax.numpy as jnp
from jax import lax
from jax.experimental import pallas as pl
from jax.experimental.pallas import tpu as pltpu
from jax.sharding import PartitionSpec as P

BLOCKS_DEV = 2
POINTS = 128
TILE = 8
VMEM_LIMIT = 60 * 1024 * 1024
COST = pl.CostEstimate(flops=3 * 10**10, bytes_accessed=0, transcendentals=0)
MINE, THEIRS, CORE, SOURCE, SLOT = 0, 1, 2, 3, 3 + BLOCKS_DEV


def shifted(array, axis, by):
    length = lax.axis_size(axis)
    return lax.ppermute(array, axis, [(i, (i + by) % length) for i in range(length)])


def halves(x):
    high = x.astype(jnp.bfloat16)
    return high, (x - high.astype(jnp.float32)).astype(jnp.bfloat16)


def dot(a, b):
    return lax.dot_general(a, b, (((1,), (0,)), ((), ())), preferred_element_type=jnp.float32)


def dot_nt(a, b):
    return lax.dot_general(a, b, (((1,), (1,)), ((), ())), preferred_element_type=jnp.float32)


def dot3(a, b, kind):
    return kind(a[0], b[0]) + (kind(a[0], b[1]) + kind(a[1], b[0]))


def species(ref, s):
    rows, tile, points = ref.shape
    flat = ref.reshape(rows * tile, points)
    return jnp.concatenate([flat[pl.ds(s + k, rows, stride=tile), :] for k in range(2)], axis=1)


def put_species(ref, s, value):
    rows, tile, points = ref.shape
    flat = ref.reshape(rows * tile, points)
    for k in range(2):
        flat[pl.ds(s + k, rows, stride=tile), :] = value[:, k * points : (k + 1) * points]


class Steps:
    def __init__(self, index):
        self.index = index
        self.last = []

    def call(self, kernel, name, grid, inputs, outputs, aliases=None, scratch=()):
        held = [array for array, _ in inputs]
        extra = [a for a in self.last if not any(a is h for h in held)]
        count = len(inputs)

        def body(index_ref, *refs):
            kernel(index_ref, *refs[:count], *refs[count + len(extra) :])

        result = pl.pallas_call(
            body,
            out_shape=[jax.ShapeDtypeStruct(shape, jnp.float32) for shape, _ in outputs],
            grid_spec=pltpu.PrefetchScalarGridSpec(
                num_scalar_prefetch=1,
                grid=grid,
                in_specs=[spec for _, spec in inputs] + [pl.BlockSpec(memory_space=pl.ANY)] * len(extra),
                out_specs=[spec for _, spec in outputs],
                scratch_shapes=list(scratch),
            ),
            input_output_aliases={k + 1: v for k, v in (aliases or {}).items()},
            compiler_params=pltpu.CompilerParams(vmem_limit_bytes=VMEM_LIMIT),
            cost_estimate=COST,
            name=name,
        )(self.index, *held, *extra)
        self.last = [result[0]]
        return result


def whole(shape):
    return pl.BlockSpec(shape, lambda *args: (0,) * len(shape))


def field_chunk(z, chunks, at, i):
    return pl.BlockSpec((z, TILE, POINTS), lambda p, w: (0, w[at] * chunks + i, p))


def core_chunk(rank):
    return pl.BlockSpec((rank, TILE, POINTS), lambda p, w: (0, 0, p))


def ranks(z, rank, at):
    return pl.BlockSpec((z, rank), lambda p, w: (0, w[at]))


def staged(sources, stages, targets, in_sems, out_sems):
    loads = [pltpu.make_async_copy(a, b, in_sems.at[k]) for k, (a, b) in enumerate(zip(sources, stages))]
    stores = [pltpu.make_async_copy(a, b, out_sems.at[k]) for k, (a, b) in enumerate(zip(stages, targets))]
    for load in loads:
        load.start()
    for load, store in zip(loads, stores):
        load.wait()
        store.start()
    for store in stores:
        store.wait()


def copy_field_kernel(i, index_ref, field_ref, out_ref, stage_ref, in_sems, out_sems):
    count = in_sems.shape[0]
    slab = out_ref.shape[0] // count
    first = pl.multiple_of((index_ref[THEIRS] * (field_ref.shape[1] // (2 * TILE)) + i) * TILE, TILE)
    slabs = [pl.ds(k * slab, slab) for k in range(count)]
    staged(
        [field_ref.at[at, pl.ds(first, TILE), :] for at in slabs],
        [stage_ref.at[at] for at in slabs],
        [out_ref.at[at] for at in slabs],
        in_sems,
        out_sems,
    )


def copy_kernel(index_ref, in_ref, out_ref):
    out_ref[...] = in_ref[...]


def add_kernel(index_ref, a_ref, b_ref, out_ref):
    out_ref[...] = a_ref[...] + b_ref[...]


def core_part_kernel(index_ref, factor_ref, field_ref, out_ref):
    at = halves(factor_ref[...].T)
    for s in range(0, TILE, 2):
        put_species(out_ref, s, dot3(at, halves(species(field_ref, s)), dot))


def core_finish_kernel(index_ref, factor_ref, field_ref, arrived_ref, out_ref):
    at = halves(factor_ref[...].T)
    for s in range(0, TILE, 2):
        put_species(out_ref, s, species(arrived_ref, s) + dot3(at, halves(species(field_ref, s)), dot))


def received_kernel(
    first, last, index_ref, factor_ref, cross_factor_ref, mine_ref, theirs_ref, *rest
):
    core_ref, cross_ref = rest[-2:]
    step = pl.program_id(0)

    @pl.when(step == 0)
    def _():
        cross_ref[...] = jnp.zeros_like(cross_ref) if first else rest[0][...]

    at = halves(jnp.concatenate([factor_ref[...].T, cross_factor_ref[...].T], axis=1))
    total = cross_ref[...]
    for s in range(0, TILE, 2):
        mine = halves(species(mine_ref, s))
        theirs = halves(species(theirs_ref, s))
        total = total + dot3(mine, theirs, dot_nt)
        both = tuple(jnp.concatenate([m, t], axis=0) for m, t in zip(mine, theirs))
        put_species(core_ref, s, dot3(at, both, dot))
    cross_ref[...] = total

    if last:
        @pl.when((step == pl.num_programs(0) - 1) & (index_ref[MINE] == 1))
        def _():
            cross_ref[...] = cross_ref[...].T


def diagonal_kernel(scale, index_ref, field_ref, keep_ref, send_ref, high_ref, mixed_ref):
    step = pl.program_id(0)

    @pl.when(step == 0)
    def _():
        high_ref[...] = jnp.zeros_like(high_ref)
        mixed_ref[...] = jnp.zeros_like(mixed_ref)

    high_sum, mixed_sum = high_ref[...], mixed_ref[...]
    for s in range(0, TILE, 2):
        high, low = halves(species(field_ref, s))
        high_sum = high_sum + dot_nt(high, high)
        mixed_sum = mixed_sum + dot_nt(high, low)
    high_ref[...] = high_sum
    mixed_ref[...] = mixed_sum

    @pl.when(step == pl.num_programs(0) - 1)
    def _():
        mixed = mixed_ref[...]
        high_ref[...] = (high_ref[...] + (mixed + mixed.T)) * scale
        half = keep_ref.shape[0]
        odd = index_ref[CORE]
        keep_ref[...] = high_ref[pl.ds(pl.multiple_of(odd * half, half), half), :]
        send_ref[...] = high_ref[pl.ds(pl.multiple_of((1 - odd) * half, half), half), :]


def sum_kernel(scale, index_ref, pieces_ref, out_ref):
    total = jnp.sum(pieces_ref[...], axis=0) * scale
    out_ref[...] = jnp.broadcast_to(total[None], out_ref.shape)


def gram_kernel(index_ref, diagonal_ref, cross_ref, out_ref):
    z = cross_ref.shape[0]

    @pl.when(index_ref[MINE] == 0)
    def _():
        out_ref[:, :z] = diagonal_ref[...]
        out_ref[:, z:] = cross_ref[...]

    @pl.when(index_ref[MINE] == 1)
    def _():
        out_ref[:, :z] = cross_ref[...].T
        out_ref[:, z:] = diagonal_ref[...]


def place_kernel(index_ref, here_ref, lower_ref, upper_ref, *rest):
    out_ref = rest[-1]
    source = index_ref[SOURCE + pl.program_id(0)]

    @pl.when(source == 0)
    def _():
        out_ref[...] = here_ref[...]

    @pl.when(source == 1)
    def _():
        out_ref[...] = lower_ref[...]

    @pl.when(source == 2)
    def _():
        out_ref[...] = upper_ref[...]


def put_kernel(i, index_ref, part_ref, old_ref, core_ref, stage_ref, in_sems, out_sems):
    count = in_sems.shape[0]
    slab = part_ref.shape[0] // count
    first = pl.multiple_of((index_ref[THEIRS] * (core_ref.shape[1] // (2 * TILE)) + i) * TILE, TILE)
    staged(
        [part_ref.at[pl.ds(k * slab, slab)] for k in range(count)],
        [stage_ref.at[pl.ds(k * slab, slab)] for k in range(count)],
        [core_ref.at[pl.ds(k * slab, slab), pl.ds(first, TILE), :] for k in range(count)],
        in_sems,
        out_sems,
    )


def join_kernel(axis, index_ref, keep_ref, other_ref, out_ref):
    half = keep_ref.shape[axis]
    odd = index_ref[CORE]
    for value_ref, first in ((keep_ref, odd * half), (other_ref, (1 - odd) * half)):
        part = pl.ds(pl.multiple_of(first, half), half)
        out_ref[(part, slice(None)) if axis == 0 else (slice(None), part)] = value_ref[...]


def block_sources(block_owner, block_offset):
    devices = lax.axis_size("xy")
    myself = lax.axis_index("xy")
    owner = lax.dynamic_slice_in_dim(block_owner, myself * BLOCKS_DEV, BLOCKS_DEV)
    offset = lax.dynamic_slice_in_dim(block_offset, myself * BLOCKS_DEV, BLOCKS_DEV)
    lower = (myself + devices - 1) % devices
    source = jnp.where(owner == myself, 0, jnp.where(owner == lower, 1, 2))
    return source.astype(jnp.int32), (offset // POINTS).astype(jnp.int32)


def local_pair(field, factor, block_owner, block_offset):
    z, count, points = field.shape
    mine = lax.axis_index("gz")
    group = count // 2
    rank = factor.shape[1] // 2
    chunks = group // TILE
    columns = points // POINTS
    scale = 1.0 / (count * points * lax.axis_size("xy"))
    source, slot = block_sources(block_owner, block_offset)
    along = lax.axis_index("xy")
    places = jnp.stack([mine, 1 - mine, along % 2]).astype(jnp.int32)
    steps = Steps(jnp.concatenate([places, source, slot]))
    any_space = pl.BlockSpec(memory_space=pl.ANY)
    whole_factor = whole(factor.shape)
    slabs = 4

    def staging(rows):
        return [pltpu.VMEM((rows, TILE, points), jnp.float32)] + [pltpu.SemaphoreType.DMA((slabs,))] * 2

    def neighbours(part):
        return part, shifted(part, "xy", 1), shifted(part, "xy", -1)

    def over_gz(part):
        return shifted(part, "gz", 1)

    def exchanged(part, bit):
        return lax.ppermute(part, "xy", [(i, i ^ bit) for i in range(lax.axis_size("xy"))])

    def send_field(i):
        kernel = functools.partial(copy_field_kernel, i)
        out = ((z, TILE, points), any_space)
        return over_gz(steps.call(kernel, "copy", (1,), [(field, any_space)], [out], None, staging(z))[0])

    def send_factor():
        out = ((z, rank), whole((z, rank)))
        half = over_gz(steps.call(copy_kernel, "copy", (1,), [(factor, ranks(z, rank, CORE))], [out])[0])
        return half, exchanged(half, 1)

    def core_send(i):
        inputs = [(factor, ranks(z, rank, THEIRS)), (field, field_chunk(z, chunks, MINE, i))]
        out = ((rank, TILE, points), core_chunk(rank))
        return steps.call(core_part_kernel, "core_send", (columns,), inputs, [out])[0]

    def core_finish(i, arrived):
        inputs = [
            (factor, ranks(z, rank, MINE)),
            (field, field_chunk(z, chunks, THEIRS, i)),
            (arrived, core_chunk(rank)),
        ]
        out = ((rank, TILE, points), core_chunk(rank))
        return steps.call(core_finish_kernel, "core_finish", (columns,), inputs, [out])[0]

    def received(i, theirs, cross_factor, cross, both):
        out_rank = 2 * rank if both else rank
        factor_spec = whole_factor if both else ranks(z, rank, MINE)
        inputs = [
            (factor, factor_spec),
            (cross_factor, factor_spec),
            (field, field_chunk(z, chunks, MINE, i)),
            (theirs, pl.BlockSpec((z, TILE, POINTS), lambda p, w: (0, 0, p))),
        ]
        if cross is not None:
            inputs.append((cross, whole((z, z))))
        outputs = [((out_rank, TILE, points), core_chunk(out_rank)), ((z, z), whole((z, z)))]
        kernel = functools.partial(received_kernel, cross is None, i == chunks - 1)
        return steps.call(kernel, "received", (columns,), inputs, outputs)

    def diagonal_gram():
        block = pl.BlockSpec((z, TILE, POINTS), lambda i, w: (0, i // columns, i % columns))
        scratch = [pltpu.VMEM((z, z), jnp.float32)] * 2
        grid = (count // TILE * columns,)
        half = ((z // 2, z), whole((z // 2, z)))
        kernel = functools.partial(diagonal_kernel, scale)
        return steps.call(kernel, "diagonal", grid, [(field, block)], [half, half], None, scratch)

    def small(kernel, *arrays):
        spec = whole(arrays[0].shape)
        return steps.call(kernel, "small", (1,), [(a, spec) for a in arrays], [(arrays[0].shape, spec)])[0]

    def joined(axis, keep, other):
        spec = whole(keep.shape)
        shape = tuple(n * 2 if k == axis else n for k, n in enumerate(keep.shape))
        kernel = functools.partial(join_kernel, axis)
        return steps.call(kernel, "join", (1,), [(keep, spec), (other, spec)], [(shape, whole(shape))])[0]

    def spread(matrix, axes):
        parts = lax.axis_size(axes)
        pieces = matrix.reshape(parts, z // parts, z)
        return lax.all_to_all(pieces, axes, split_axis=0, concat_axis=0, tiled=True)

    def summed(pieces, axes):
        spec = whole(pieces.shape)
        kernel = functools.partial(sum_kernel, scale)
        total = steps.call(kernel, "sum", (1,), [(pieces, spec)], [(pieces.shape, spec)])[0]
        return lax.all_to_all(total, axes, split_axis=0, concat_axis=0, tiled=True).reshape(z, z)

    def place(parts, half=None, core=None, at=MINE, i=0):
        rows = (lambda w: 0) if half is None else (lambda w: w[half])
        spec = pl.BlockSpec((rank, TILE, POINTS), lambda j, w: (rows(w), 0, w[SLOT + j]))
        inputs = [(part, spec) for part in parts]
        if core is None:
            return steps.call(place_kernel, "place", (BLOCKS_DEV,), inputs, [((rank, TILE, points), core_chunk(rank))])[0]
        out = ((rank, count, points), field_chunk(rank, chunks, at, i))
        if core is EMPTY:
            return steps.call(place_kernel, "place", (BLOCKS_DEV,), inputs, [out])[0]
        inputs.append((core, any_space))
        return steps.call(place_kernel, "place", (BLOCKS_DEV,), inputs, [out], {3: 0})[0]

    def put(part, core, i):
        out = ((rank, count, points), any_space)
        kernel = functools.partial(put_kernel, i)
        inputs = [(part, any_space), (core, any_space)]
        return steps.call(kernel, "put", (1,), inputs, [out], {1: 0}, staging(rank))[0]

    fields, ready, arrived = {}, {}, {}
    arrived[2] = over_gz(core_send(2))
    cross_half = send_factor()
    fields[0] = send_field(0)
    diagonal, half = diagonal_gram()
    half = exchanged(half, 1)
    fields[1] = send_field(1)
    diagonal = small(add_kernel, diagonal, half)
    half = exchanged(diagonal, 2)
    cross_factor = joined(1, *cross_half)
    diagonal = small(add_kernel, diagonal, half)
    half = exchanged(diagonal, 4)
    late2 = neighbours(core_finish(2, arrived[2]))
    diagonal = small(add_kernel, diagonal, half)
    half = exchanged(diagonal, 8)
    core = place(late2, None, EMPTY, THEIRS, 2)
    diagonal = small(add_kernel, diagonal, half)
    half = exchanged(diagonal, 1)
    part, cross = received(0, fields[0], cross_factor, None, True)
    ready[0] = neighbours(part)
    diagonal = joined(0, diagonal, half)
    fields[2] = send_field(2)
    part, cross = received(1, fields[1], cross_factor, cross, True)
    ready[1] = neighbours(part)
    core = place(ready[0], MINE, core, MINE, 0)
    fields[3] = send_field(3)
    part, cross = received(2, fields[2], cross_factor, cross, False)
    ready[2] = neighbours(part)
    core = place(ready[1], MINE, core, MINE, 1)
    arrived[3] = over_gz(core_send(3))
    core = place(ready[2], None, core, MINE, 2)
    part, cross = received(3, fields[3], cross_factor, cross, False)
    ready[3] = neighbours(part)
    cross = spread(cross, ("xy", "gz"))
    arrived[0] = over_gz(place(ready[0], THEIRS))
    late3 = neighbours(core_finish(3, arrived[3]))
    cross = summed(cross, ("xy", "gz"))
    core = place(ready[3], None, core, MINE, 3)
    arrived[1] = over_gz(place(ready[1], THEIRS))
    core = put(arrived[0], core, 0)
    gram_specs = [(diagonal, whole((z, z))), (cross, whole((z, z)))]
    gram = steps.call(gram_kernel, "gram", (1,), gram_specs, [((z, 2 * z), whole((z, 2 * z)))])[0]
    core = place(late3, None, core, THEIRS, 3)
    core = put(arrived[1], core, 1)
    return (gram, core)


EMPTY = object()


def local_many(field, factor, block_owner, block_offset):
    parts = lax.axis_size("gz")
    mine = lax.axis_index("gz")
    z, count, points = field.shape
    scale = 1.0 / (count * points * lax.axis_size("xy"))
    swapped = lax.all_to_all(field, "gz", split_axis=1, concat_axis=0, tiled=True)
    part = jnp.einsum("zcs,wcs->zw", swapped, swapped, precision=lax.Precision.HIGHEST)
    rows = lax.psum_scatter(part, "gz", scatter_dimension=0, tiled=True)
    gram = lax.psum(rows, "xy") * scale
    whole_factor = lax.all_gather(factor, "gz", axis=0, tiled=True)
    core_part = jnp.einsum("zr,zcs->rcs", whole_factor, swapped, precision=lax.Precision.HIGHEST)
    core = lax.all_to_all(core_part, "gz", split_axis=0, concat_axis=1, tiled=True)
    source, slot = block_sources(block_owner, block_offset)
    stack = (core, shifted(core, "xy", 1), shifted(core, "xy", -1))
    blocks = []
    for j in range(BLOCKS_DEV):
        here, lower, upper = (lax.dynamic_slice_in_dim(a, slot[j] * POINTS, POINTS, 2) for a in stack)
        blocks.append(jnp.where(source[j] == 0, here, jnp.where(source[j] == 1, lower, upper)))
    return (gram, jnp.concatenate(blocks, axis=2))


def solution(mesh):
    return jax.shard_map(
        local_pair if mesh.shape["gz"] == 2 else local_many,
        mesh=mesh,
        in_specs=(P("gz", None, "xy"), P("gz", None), P(), P()),
        out_specs=(P("gz", None), P("gz", None, "xy")),
        check_vma=False,
    )
```

time: 645 us -> 313 us (0.49)
  blocking collectives: 189 us -> 0 us
  waiting for transfers between devices: 246 us -> 97.4 us
  Pallas kernels: 0 us -> 120 us
  other arithmetic: 62 us -> 0.75 us
  matrix products: 59.4 us -> 0 us
  starting transfers between devices: 19 us -> 78.2 us
  between operations: 30.3 us -> 0.82 us
  local copies, waits for them, and re-layouts: 34 us -> 14.3 us
    all_gather x1 -> x0, blocking collectives: 189 us -> none  [local(): whole_factor = lax.all_gather(factor, 'gz', axis=0, tiled=True)]
    psum x1 -> x0, waiting for transfers between devices: 165 us -> none  [local(): full_gram = lax.psum(partial_gram, ('xy', 'gz'))]
    pallas_call x0 -> x32, Pallas kernels: none -> 120 us  [call(): pl.pallas_call(body, out_shape=[jax.ShapeDtypeStruct(shape, jnp.float32)...]
    ppermute x2 -> x21, waiting for transfers between devices: 0.01 us -> 82.5 us  [shifted(): lax.ppermute(array, axis, [(i, (i + by) % length) for i in range(length)])]
    all_to_all x2, waiting for transfers between devices: 81.4 us -> 13.6 us  [the longest x1 13.6 us: spread(): return lax.all_to_all(pieces, axes, split_axis=0, concat_axis=0, tiled=True)]
    dot_general x2 -> x0, matrix products: 59.4 us -> none  [the longest x1 30.7 us: local(): jnp.einsum('zr,zcs->rcs', whole_factor, swapped, precision=lax.Precision....]
    ppermute x2 -> x21, starting transfers between devices: 2.07 us -> 48.4 us  [shifted(): lax.ppermute(array, axis, [(i, (i + by) % length) for i in range(length)])]
    select_n x3 -> x1, other arithmetic: 24.5 us -> 0.75 us  [block_sources(): return (source.astype(jnp.int32), (offset // POINTS).astype(jnp.int32))]
  transfers between devices with their start and end apart: 5 -> 29, of which waited for: 2 -> 9; matrix products, arithmetic and copies ran while one was open for 6% -> 0% of each run, Pallas kernels for 0% -> 36%
where the time goes in v1:
time: 313 us; the launch traced here: 311 us
  Pallas kernels  120 us (38%)
  waiting for transfers between devices  97.4 us (31%)
  starting transfers between devices  78.2 us (25%)
  local copies, waits for them, and re-layouts  14.3 us (5%)
    pallas_call x32, Pallas kernels, call(): pl.pallas_call(body, out_shape=[jax.ShapeDtypeStruct(shape, jnp.float32)...  120 us
    ppermute x21, waiting for transfers between devices, shifted(): lax.ppermute(array, axis, [(i, (i + by) % length) for i in range(length)])  82.5 us
    ppermute x21, starting transfers between devices, shifted(): lax.ppermute(array, axis, [(i, (i + by) % length) for i in range(length)])  48.4 us
    unnamed x34, local copies, waits for them, and re-layouts  13.6 us
    all_to_all x1, waiting for transfers between devices, spread(): return lax.all_to_all(pieces, axes, split_axis=0, concat_axis=0, tiled=True)  13.6 us
    ppermute x6, starting transfers between devices, exchanged(): lax.ppermute(part, 'xy', [(i, i ^ bit) for i in range(lax.axis_size('xy'))])  12.6 us
    all_to_all x1, starting transfers between devices, summed(): lax.all_to_all(total, axes, split_axis=0, concat_axis=0, tiled=True)  11 us
  transfers between devices with their start and end apart: 29, of which 9 were waited for; matrix products, arithmetic and copies ran while one was open for 0% of the time, Pallas kernels for 36%

profile of v1, /device:TPU:0, one launch (start us, length us, event | category | flops | bytes accessed | tf_op | source)
XLA Modules:
  0.0 311.2 jit_solution(4052346653025093443)
XLA Ops:
  2.1 3.8 %core_send.2.refs_1_ = f32[128,8,256]{2,1,0:T(8,128)} custom-call(s32[7]{0:T(128)} %concatenate.3.index_ref, f32[256,256]{1,0:T(8,128)} %refs_0_.27, f32[256,64,256]{2,1,0:T(8,128)} %refs_1_.7), custom_call_target="tpu_custom_call" | custom-call | flops 30000001024 | tf_op jit(solution)/shard_map/core_send/pallas_call | solution.py:66
  5.9 3.0 collective-permute-start.5
  11.1 3.1 %copy.26.refs_1_ = f32[256,8,256]{2,1,0:T(8,128)} custom-call(s32[7]{0:T(128)} %concatenate.3.index_ref, f32[256,64,256]{2,1,0:T(8,128)} %refs_1_.7, f32[256,128]{1,0:T(8,128)} %copy.25.refs_1_), custom_call_target="tpu_custom_call" | custom-call | flops 30000001024 | tf_op jit(solution)/shard_map/copy/pallas_call | solution.py:66
  16.3 16.5 %diagonal.1 = (f32[128,256]{1,0:T(8,128)}, f32[128,256]{1,0:T(8,128)}) custom-call(s32[7]{0:T(128)} %concatenate.3.index_ref, f32[256,64,256]{2,1,0:T(8,128)} %refs_1_.7, f32[256,8,256]{2,1,0:T(8,128)} %copy.26.refs_1_), custom_call_target="tpu_custom_call" | custom-call | flops 30000001024 | tf_op jit(solution)/shard_map/diagonal/pallas_call | solution.py:66
  32.8 3.1 copy.27.refs_2_
  37.2 2.3 small.4.refs_2_.refs_0_
  41.8 2.4 join.2.refs_2_.refs_1_
  45.9 2.3 small.5.refs_3_.refs_0_
  50.0 4.0 %core_finish.2.refs_2_.refs_0_ = f32[128,8,256]{2,1,0:T(8,128)} custom-call(s32[7]{0:T(128)} %concatenate.3.index_ref, f32[256,256]{1,0:T(8,128)} %refs_0_.27, f32[256,64,256]{2,1,0:T(8,128)} %refs_1_.7, f32[128,8,256]{2,1,0:T(8,128)} %collective-permute-done.5.refs_2_, f32[128,256]{1,0:T(8,128)} %small.5.refs_3_.refs_0_), custom_call_target="tpu_custom_call" | custom-call | flops 30000001024 | tf_op jit(solution)/shard_map/core_finish/pallas_call | solution.py:66
  54.1 4.4 %collective-permute-start.8 = (f32[128,8,256]{2,1,0:T(8,128)}, f32[128,8,256]{2,1,0:T(8,128)S(1)}, u32[]{:S(2)}, u32[]{:S(2)}) collective-permute-start(f32[128,8,256]{2,1,0:T(8,128)} %core_finish.2.refs_2_.refs_0_), channel_id=1, source_target_pairs={{0,30},{2,0},{4,2},{6,4},{8,6},{10,8},{12,10},{14,12},{16,14},{18,... | collective-permute-start | bytes 3145736 | tf_op jit(solution)/shard_map/ppermute | solution.py:20
  59.2 2.3 small.6.refs_3_.refs_0_
  62.2 10.5 %collective-permute-done.7.refs_1_ = f32[128,8,256]{2,1,0:T(8,128)S(1)} collective-permute-done((f32[128,8,256]{2,1,0:T(8,128)}, f32[128,8,256]{2,1,0:T(8,128)S(1)}, u32[]{:S(2)}, u32[]{:S(2)}) %collective-permute-start.7) | collective-permute-done | bytes 1048608 | tf_op jit(solution)/shard_map/ppermute | solution.py:20
  74.7 3.1 place.8.refs_2_.refs_3_
  78.6 2.3 small.7.refs_4_.refs_0_
  80.9 7.8 %collective-permute-start.9 = (f32[128,256]{1,0:T(8,128)}, f32[128,256]{1,0:T(8,128)S(1)}, u32[]{:S(2)}, u32[]{:S(2)}) collective-permute-start(f32[128,256]{1,0:T(8,128)} %small.7.refs_4_.refs_0_), channel_id=1, source_target_pairs={{0,2},{2,0},{4,6},{6,4},{8,10},{10,8},{12,14},{14,12},{16,18},{18,... | collective-permute-start | bytes 393224 | tf_op jit(solution)/shard_map/ppermute | solution.py:292
  88.7 6.5 %received.4 = (f32[256,8,256]{2,1,0:T(8,128)}, f32[256,256]{1,0:T(8,128)}) custom-call(s32[7]{0:T(128)} %concatenate.3.index_ref, f32[256,256]{1,0:T(8,128)} %refs_0_.27, f32[256,256]{1,0:T(8,128)} %join.2.refs_2_.refs_1_, f32[256,64,256]{2,1,0:T(8,128)} %refs_1_.7, f32[256,8,256]{2,1,0:T(8,128)} %collective-permute-done.10.refs_3_, ...), custom_call_target="tpu_custom_call" | custom-call | flops 30000001024 | tf_op jit(solution)/shard_map/received/pallas_call | solution.py:66
  95.2 4.4 %collective-permute-start.12 = (f32[256,8,256]{2,1,0:T(8,128)}, f32[256,8,256]{2,1,0:T(8,128)}, u32[]{:S(2)}, u32[]{:S(2)}) collective-permute-start(f32[256,8,256]{2,1,0:T(8,128)} %get-tuple-element.14.refs_2_.refs_0_), channel_id=1, source_target_pairs={{0,30},{2,0},{4,2},{6,4},{8,6},{10,8},{12,10},{14,12},{16,14},{18,... | collective-permute-start | bytes 6291464 | tf_op jit(solution)/shard_map/ppermute | solution.py:20
  100.3 2.3 join.3.refs_1_.refs_0_
  102.6 3.1 copy.28.refs_5_
  107.3 18.5 %collective-permute-done.13.refs_3_ = f32[256,8,256]{2,1,0:T(8,128)} collective-permute-done((f32[256,8,256]{2,1,0:T(8,128)}, f32[256,8,256]{2,1,0:T(8,128)}, u32[]{:S(2)}, u32[]{:S(2)}) %collective-permute-start.13) | collective-permute-done | bytes 2097184 | tf_op jit(solution)/shard_map/ppermute | solution.py:20
  125.8 6.6 %received.5 = (f32[256,8,256]{2,1,0:T(8,128)}, f32[256,256]{1,0:T(8,128)}) custom-call(s32[7]{0:T(128)} %concatenate.3.index_ref, f32[256,256]{1,0:T(8,128)} %refs_0_.27, f32[256,256]{1,0:T(8,128)} %join.2.refs_2_.refs_1_, f32[256,64,256]{2,1,0:T(8,128)} %refs_1_.7, f32[256,8,256]{2,1,0:T(8,128)} %collective-permute-done.13.refs_3_, ...), custom_call_target="tpu_custom_call" | custom-call | flops 30000001024 | tf_op jit(solution)/shard_map/received/pallas_call | solution.py:66
  132.4 4.4 %collective-permute-start.19 = (f32[256,8,256]{2,1,0:T(8,128)}, f32[256,8,256]{2,1,0:T(8,128)}, u32[]{:S(2)}, u32[]{:S(2)}) collective-permute-start(f32[256,8,256]{2,1,0:T(8,128)} %get-tuple-element.16.refs_4_.refs_0_), channel_id=1, source_target_pairs={{0,30},{2,0},{4,2},{6,4},{8,6},{10,8},{12,10},{14,12},{16,14},{18,... | collective-permute-start | bytes 6291464 | tf_op jit(solution)/shard_map/ppermute | solution.py:20
  136.9 3.1 place.9.refs_1_.refs_3_
  139.9 3.1 copy.29.refs_5_
  145.1 24.8 %collective-permute-done.15.refs_3_ = f32[256,8,256]{2,1,0:T(8,128)} collective-permute-done((f32[256,8,256]{2,1,0:T(8,128)}, f32[256,8,256]{2,1,0:T(8,128)}, u32[]{:S(2)}, u32[]{:S(2)}) %collective-permute-start.15) | collective-permute-done | bytes 2097184 | tf_op jit(solution)/shard_map/ppermute | solution.py:20
  169.9 5.7 %received.6 = (f32[128,8,256]{2,1,0:T(8,128)}, f32[256,256]{1,0:T(8,128)}) custom-call(s32[7]{0:T(128)} %concatenate.3.index_ref, f32[256,256]{1,0:T(8,128)} %refs_0_.27, f32[256,256]{1,0:T(8,128)} %join.2.refs_2_.refs_1_, f32[256,64,256]{2,1,0:T(8,128)} %refs_1_.7, f32[256,8,256]{2,1,0:T(8,128)} %collective-permute-done.15.refs_3_, ...), custom_call_target="tpu_custom_call" | custom-call | flops 30000001024 | tf_op jit(solution)/shard_map/received/pallas_call | solution.py:66
  175.6 4.3 %collective-permute-start.16 = (f32[128,8,256]{2,1,0:T(8,128)}, f32[128,8,256]{2,1,0:T(8,128)S(1)}, u32[]{:S(2)}, u32[]{:S(2)}) collective-permute-start(f32[128,8,256]{2,1,0:T(8,128)} %get-tuple-element.19.refs_4_.refs_0_), channel_id=1, source_target_pairs={{0,2},{2,4},{4,6},{6,8},{8,10},{10,12},{12,14},{14,16},{16,18},{18... | collective-permute-start | bytes 3145736 | tf_op jit(solution)/shard_map/ppermute | solution.py:20
  181.5 3.1 place.10.refs_2_.refs_3_
  184.5 3.8 %core_send.3.refs_4_ = f32[128,8,256]{2,1,0:T(8,128)} custom-call(s32[7]{0:T(128)} %concatenate.3.index_ref, f32[256,256]{1,0:T(8,128)} %refs_0_.27, f32[256,64,256]{2,1,0:T(8,128)} %refs_1_.7, f32[128,64,256]{2,1,0:T(8,128)} %place.10.refs_2_.refs_3_), custom_call_target="tpu_custom_call" | custom-call | flops 30000001024 | tf_op jit(solution)/shard_map/core_send/pallas_call | solution.py:66
  190.1 2.8 collective-permute-done.16.refs_1_
  193.8 3.1 place.11.refs_5_.refs_3_
  196.9 12.0 %collective-permute-done.14.refs_3_ = f32[256,8,256]{2,1,0:T(8,128)} collective-permute-done((f32[256,8,256]{2,1,0:T(8,128)}, f32[256,8,256]{2,1,0:T(8,128)}, u32[]{:S(2)}, u32[]{:S(2)}) %collective-permute-start.14) | collective-permute-done | bytes 2097184 | tf_op jit(solution)/shard_map/ppermute | solution.py:20
  208.9 5.7 %received.7 = (f32[128,8,256]{2,1,0:T(8,128)}, f32[256,256]{1,0:T(8,128)}) custom-call(s32[7]{0:T(128)} %concatenate.3.index_ref, f32[256,256]{1,0:T(8,128)} %refs_0_.27, f32[256,256]{1,0:T(8,128)} %join.2.refs_2_.refs_1_, f32[256,64,256]{2,1,0:T(8,128)} %refs_1_.7, f32[256,8,256]{2,1,0:T(8,128)} %collective-permute-done.14.refs_3_, ...), custom_call_target="tpu_custom_call" | custom-call | flops 30000001024 | tf_op jit(solution)/shard_map/received/pallas_call | solution.py:66
  214.6 12.1 %collective-permute-start.22 = (f32[128,8,256]{2,1,0:T(8,128)}, f32[128,8,256]{2,1,0:T(8,128)S(1)}, u32[]{:S(2)}, u32[]{:S(2)}) collective-permute-start(f32[128,8,256]{2,1,0:T(8,128)} %get-tuple-element.21.refs_3_.refs_0_), channel_id=1, source_target_pairs={{0,2},{2,4},{4,6},{6,8},{8,10},{10,12},{12,14},{14,16},{16,18},{18... | collective-permute-start | bytes 3145736 | tf_op jit(solution)/shard_map/ppermute | solution.py:20
  226.7 6.2 %all-to-all-start = ((f32[32,8,256]{2,1,0:T(8,128)}), f32[32,8,256]{2,1,0:T(8,128)S(1)}, u32[]{:S(2)}, u32[]{:S(2)}) async-start(f32[32,8,256]{2,1,0:T(8,128)} %bitcast.5), calls=%async_computation | async-start | bytes 524288 | tf_op jit(solution)/shard_map/all_to_all | solution.py:354
  232.8 3.1 place.12.refs_3_
  237.7 4.0 %core_finish.3.refs_1_.refs_0_ = f32[128,8,256]{2,1,0:T(8,128)} custom-call(s32[7]{0:T(128)} %concatenate.3.index_ref, f32[256,256]{1,0:T(8,128)} %refs_0_.27, f32[256,64,256]{2,1,0:T(8,128)} %refs_1_.7, f32[128,8,256]{2,1,0:T(8,128)} %collective-permute-done.20.refs_2_, f32[128,8,256]{2,1,0:T(8,128)} %place.12.refs_3_), custom_call_target="tpu_custom_call" | custom-call | flops 30000001024 | tf_op jit(solution)/shard_map/core_finish/pallas_call | solution.py:66
  241.7 4.4 %collective-permute-start.26 = (f32[128,8,256]{2,1,0:T(8,128)}, f32[128,8,256]{2,1,0:T(8,128)}, u32[]{:S(2)}, u32[]{:S(2)}) collective-permute-start(f32[128,8,256]{2,1,0:T(8,128)} %core_finish.3.refs_1_.refs_0_), channel_id=1, source_target_pairs={{0,30},{2,0},{4,2},{6,4},{8,6},{10,8},{12,10},{14,12},{16,14},{18,... | collective-permute-start | bytes 3145736 | tf_op jit(solution)/shard_map/ppermute | solution.py:20
  246.1 13.6 %all-to-all-done.refs_0_ = f32[32,8,256]{2,1,0:T(8,128)S(1)} async-done(((f32[32,8,256]{2,1,0:T(8,128)}), f32[32,8,256]{2,1,0:T(8,128)S(1)}, u32[]{:S(2)}, u32[]{:S(2)}) %all-to-all-start) | async-done | bytes 262176 | tf_op jit(solution)/shard_map/all_to_all | solution.py:354
  260.4 2.4 sum.1.refs_4_
  262.8 11.0 %all-to-all-start.1 = ((f32[32,8,256]{2,1,0:T(8,128)}), f32[32,8,256]{2,1,0:T(8,128)S(1)}, u32[]{:S(2)}, u32[]{:S(2)}) async-start(f32[32,8,256]{2,1,0:T(8,128)} %sum.1.refs_4_), calls=%async_computation.1 | async-start | bytes 524288 | tf_op jit(solution)/shard_map/all_to_all | solution.py:360
  275.8 3.1 place.13.refs_3_.refs_1_
  278.9 3.1 %place.14.refs_2_ = f32[128,8,256]{2,1,0:T(8,128)} custom-call(s32[7]{0:T(128)} %concatenate.3.index_ref, f32[256,8,256]{2,1,0:T(8,128)} %get-tuple-element.16.refs_4_.refs_0_, f32[256,8,256]{2,1,0:T(8,128)} %copy-done.2, f32[256,8,256]{2,1,0:T(8,128)} %collective-permute-done.19.refs_2_, f32[128,64,256]{2,1,0:T(8,128)} %place.13.refs_3_.refs_1_), custom_call_target="tpu_custom_call" | custom-call | flops 30000001024 | tf_op jit(solution)/shard_map/place/pallas_call | solution.py:66
  284.8 2.6 put.2.refs_2_.refs_3_
  288.1 2.5 gram.1.refs_4_
  290.7 3.1 place.15.refs_1_
  293.7 13.8 %collective-permute-done.24.refs_0_ = f32[128,8,256]{2,1,0:T(8,128)S(1)} collective-permute-done((f32[128,8,256]{2,1,0:T(8,128)}, f32[128,8,256]{2,1,0:T(8,128)S(1)}, u32[]{:S(2)}, u32[]{:S(2)}) %collective-permute-start.24) | collective-permute-done | bytes 1048608 | tf_op jit(solution)/shard_map/ppermute | solution.py:20
  308.5 2.6 put.3
  (78 shorter events, 35.0 us)
Async XLA Ops:
  5.9 44.2 %collective-permute-start.5 = (f32[128,8,256]{2,1,0:T(8,128)}, f32[128,8,256]{2,1,0:T(8,128)}, u32[]{:S(2)}, u32[]{:S(2)}) collective-permute-start(f32[128,8,256]{2,1,0:T(8,128)} %core_send.2.refs_1_), channel_id=1, source_target_pairs={{0,1},{1,0},{2,3},{3,2},{4,5},{5,4},{6,7},{7,6},{8,9},{9,8},{10,11... | collective-permute-start | bytes 3145736 | tf_op jit(solution)/shard_map/ppermute | solution.py:20
  11.1 24.9 %collective-permute-start.2 = (f32[256,128]{1,0:T(8,128)}, f32[256,128]{1,0:T(8,128)S(1)}, u32[]{:S(2)}, u32[]{:S(2)}) collective-permute-start(f32[256,128]{1,0:T(8,128)} %copy.25.refs_1_), channel_id=1, source_target_pairs={{0,1},{1,0},{2,3},{3,2},{4,5},{5,4},{6,7},{7,6},{8,9},{9,8},{10,11... | collective-permute-start | bytes 393224 | tf_op jit(solution)/shard_map/ppermute | solution.py:20
  14.2 74.5 %collective-permute-start.10 = (f32[256,8,256]{2,1,0:T(8,128)}, f32[256,8,256]{2,1,0:T(8,128)}, u32[]{:S(2)}, u32[]{:S(2)}) collective-permute-start(f32[256,8,256]{2,1,0:T(8,128)} %copy.26.refs_1_), channel_id=1, source_target_pairs={{0,1},{1,0},{2,3},{3,2},{4,5},{5,4},{6,7},{7,6},{8,9},{9,8},{10,11... | collective-permute-start | bytes 6291464 | tf_op jit(solution)/shard_map/ppermute | solution.py:20
  32.8 3.8 %collective-permute-start = (f32[128,256]{1,0:T(8,128)}, f32[128,256]{1,0:T(8,128)S(1)}, u32[]{:S(2)}, u32[]{:S(2)}) collective-permute-start(f32[128,256]{1,0:T(8,128)} %get-tuple-element.13), channel_id=1, source_target_pairs={{0,2},{2,0},{4,6},{6,4},{8,10},{10,8},{12,14},{14,12},{16,18},{18,... | collective-permute-start | bytes 393224 | tf_op jit(solution)/shard_map/ppermute | solution.py:292
  35.9 90.0 %collective-permute-start.13 = (f32[256,8,256]{2,1,0:T(8,128)}, f32[256,8,256]{2,1,0:T(8,128)}, u32[]{:S(2)}, u32[]{:S(2)}) collective-permute-start(f32[256,8,256]{2,1,0:T(8,128)} %copy.27.refs_2_), channel_id=1, source_target_pairs={{0,1},{1,0},{2,3},{3,2},{4,5},{5,4},{6,7},{7,6},{8,9},{9,8},{10,11... | collective-permute-start | bytes 6291464 | tf_op jit(solution)/shard_map/ppermute | solution.py:20
  36.0 3.5 %copy-start.10 = (f32[256,128]{1,0:T(8,128)}, f32[256,128]{1,0:T(8,128)S(1)}, u32[]{:S(2)}) copy-start(f32[256,128]{1,0:T(8,128)S(1)} %collective-permute-done.2.refs_0_) | copy-start | bytes 393220
  36.0 5.2 %collective-permute-start.3 = (f32[256,128]{1,0:T(8,128)S(1)}, f32[256,128]{1,0:T(8,128)S(1)}, u32[]{:S(2)}, u32[]{:S(2)}) collective-permute-start(f32[256,128]{1,0:T(8,128)S(1)} %collective-permute-done.2.refs_0_), channel_id=1, source_target_pairs={{0,2},{2,0},{4,6},{6,4},{8,10},{10,8},{12,14},{14,12},{16,18},{18,... | collective-permute-start | bytes 393224 | tf_op jit(solution)/shard_map/ppermute | solution.py:292
  36.5 0.7 copy-start.12
  39.5 5.8 %collective-permute-start.1 = (f32[128,256]{1,0:T(8,128)}, f32[128,256]{1,0:T(8,128)S(1)}, u32[]{:S(2)}, u32[]{:S(2)}) collective-permute-start(f32[128,256]{1,0:T(8,128)} %small.4.refs_2_.refs_0_), channel_id=1, source_target_pairs={{0,4},{2,6},{4,0},{6,2},{8,12},{10,14},{12,8},{14,10},{16,20},{18,... | collective-permute-start | bytes 393224 | tf_op jit(solution)/shard_map/ppermute | solution.py:292
  41.1 0.6 copy-start.14
  45.3 0.6 copy-start.16
  48.2 10.3 %collective-permute-start.4 = (f32[128,256]{1,0:T(8,128)}, f32[128,256]{1,0:T(8,128)S(1)}, u32[]{:S(2)}, u32[]{:S(2)}) collective-permute-start(f32[128,256]{1,0:T(8,128)} %small.5.refs_3_.refs_0_), channel_id=1, source_target_pairs={{0,8},{2,10},{4,12},{6,14},{8,0},{10,2},{12,4},{14,6},{16,24},{18,... | collective-permute-start | bytes 393224 | tf_op jit(solution)/shard_map/ppermute | solution.py:292
  54.0 18.7 %collective-permute-start.7 = (f32[128,8,256]{2,1,0:T(8,128)}, f32[128,8,256]{2,1,0:T(8,128)S(1)}, u32[]{:S(2)}, u32[]{:S(2)}) collective-permute-start(f32[128,8,256]{2,1,0:T(8,128)} %core_finish.2.refs_2_.refs_0_), channel_id=1, source_target_pairs={{0,2},{2,4},{4,6},{6,8},{8,10},{10,12},{12,14},{14,16},{16,18},{18... | collective-permute-start | bytes 3145736 | tf_op jit(solution)/shard_map/ppermute | solution.py:20
  54.1 18.7 %collective-permute-start.8 = (f32[128,8,256]{2,1,0:T(8,128)}, f32[128,8,256]{2,1,0:T(8,128)S(1)}, u32[]{:S(2)}, u32[]{:S(2)}) collective-permute-start(f32[128,8,256]{2,1,0:T(8,128)} %core_finish.2.refs_2_.refs_0_), channel_id=1, source_target_pairs={{0,30},{2,0},{4,2},{6,4},{8,6},{10,8},{12,10},{14,12},{16,14},{18,... | collective-permute-start | bytes 3145736 | tf_op jit(solution)/shard_map/ppermute | solution.py:20
  58.5 0.7 copy-start.13
  61.5 16.5 %collective-permute-start.6 = (f32[128,256]{1,0:T(8,128)}, f32[128,256]{1,0:T(8,128)S(1)}, u32[]{:S(2)}, u32[]{:S(2)}) collective-permute-start(f32[128,256]{1,0:T(8,128)} %small.6.refs_3_.refs_0_), channel_id=1, source_target_pairs={{0,16},{2,18},{4,20},{6,22},{8,24},{10,26},{12,28},{14,30},{16,0},... | collective-permute-start | bytes 393224 | tf_op jit(solution)/shard_map/ppermute | solution.py:292
  72.7 1.0 copy-start.8
  73.7 1.0 copy-start.9
  78.0 0.7 copy-start.15
  80.9 18.7 %collective-permute-start.9 = (f32[128,256]{1,0:T(8,128)}, f32[128,256]{1,0:T(8,128)S(1)}, u32[]{:S(2)}, u32[]{:S(2)}) collective-permute-start(f32[128,256]{1,0:T(8,128)} %small.7.refs_4_.refs_0_), channel_id=1, source_target_pairs={{0,2},{2,0},{4,6},{6,4},{8,10},{10,8},{12,14},{14,12},{16,18},{18,... | collective-permute-start | bytes 393224 | tf_op jit(solution)/shard_map/ppermute | solution.py:292
  95.2 41.7 %collective-permute-start.11 = (f32[256,8,256]{2,1,0:T(8,128)}, f32[256,8,256]{2,1,0:T(8,128)}, u32[]{:S(2)}, u32[]{:S(2)}) collective-permute-start(f32[256,8,256]{2,1,0:T(8,128)} %get-tuple-element.14.refs_2_.refs_0_), channel_id=1, source_target_pairs={{0,2},{2,4},{4,6},{6,8},{8,10},{10,12},{12,14},{14,16},{16,18},{18... | collective-permute-start | bytes 6291464 | tf_op jit(solution)/shard_map/ppermute | solution.py:20
  95.2 41.7 %collective-permute-start.12 = (f32[256,8,256]{2,1,0:T(8,128)}, f32[256,8,256]{2,1,0:T(8,128)}, u32[]{:S(2)}, u32[]{:S(2)}) collective-permute-start(f32[256,8,256]{2,1,0:T(8,128)} %get-tuple-element.14.refs_2_.refs_0_), channel_id=1, source_target_pairs={{0,30},{2,0},{4,2},{6,4},{8,6},{10,8},{12,10},{14,12},{16,14},{18,... | collective-permute-start | bytes 6291464 | tf_op jit(solution)/shard_map/ppermute | solution.py:20
  99.6 0.6 copy-start.11
  105.7 64.2 %collective-permute-start.15 = (f32[256,8,256]{2,1,0:T(8,128)}, f32[256,8,256]{2,1,0:T(8,128)}, u32[]{:S(2)}, u32[]{:S(2)}) collective-permute-start(f32[256,8,256]{2,1,0:T(8,128)} %copy.28.refs_5_), channel_id=1, source_target_pairs={{0,1},{1,0},{2,3},{3,2},{4,5},{5,4},{6,7},{7,6},{8,9},{9,8},{10,11... | collective-permute-start | bytes 6291464 | tf_op jit(solution)/shard_map/ppermute | solution.py:20
  132.4 47.6 %collective-permute-start.18 = (f32[256,8,256]{2,1,0:T(8,128)}, f32[256,8,256]{2,1,0:T(8,128)S(1)}, u32[]{:S(2)}, u32[]{:S(2)}) collective-permute-start(f32[256,8,256]{2,1,0:T(8,128)} %get-tuple-element.16.refs_4_.refs_0_), channel_id=1, source_target_pairs={{0,2},{2,4},{4,6},{6,8},{8,10},{10,12},{12,14},{14,16},{16,18},{18... | collective-permute-start | bytes 6291464 | tf_op jit(solution)/shard_map/ppermute | solution.py:20
  132.4 47.6 %collective-permute-start.19 = (f32[256,8,256]{2,1,0:T(8,128)}, f32[256,8,256]{2,1,0:T(8,128)}, u32[]{:S(2)}, u32[]{:S(2)}) collective-permute-start(f32[256,8,256]{2,1,0:T(8,128)} %get-tuple-element.16.refs_4_.refs_0_), channel_id=1, source_target_pairs={{0,30},{2,0},{4,2},{6,4},{8,6},{10,8},{12,10},{14,12},{16,14},{18,... | collective-permute-start | bytes 6291464 | tf_op jit(solution)/shard_map/ppermute | solution.py:20
  143.0 65.9 %collective-permute-start.14 = (f32[256,8,256]{2,1,0:T(8,128)}, f32[256,8,256]{2,1,0:T(8,128)}, u32[]{:S(2)}, u32[]{:S(2)}) collective-permute-start(f32[256,8,256]{2,1,0:T(8,128)} %copy.29.refs_5_), channel_id=1, source_target_pairs={{0,1},{1,0},{2,3},{3,2},{4,5},{5,4},{6,7},{7,6},{8,9},{9,8},{10,11... | collective-permute-start | bytes 6291464 | tf_op jit(solution)/shard_map/ppermute | solution.py:20
  175.6 17.2 %collective-permute-start.16 = (f32[128,8,256]{2,1,0:T(8,128)}, f32[128,8,256]{2,1,0:T(8,128)S(1)}, u32[]{:S(2)}, u32[]{:S(2)}) collective-permute-start(f32[128,8,256]{2,1,0:T(8,128)} %get-tuple-element.19.refs_4_.refs_0_), channel_id=1, source_target_pairs={{0,2},{2,4},{4,6},{6,8},{8,10},{10,12},{12,14},{14,16},{16,18},{18... | collective-permute-start | bytes 3145736 | tf_op jit(solution)/shard_map/ppermute | solution.py:20
  179.9 13.0 %collective-permute-start.17 = (f32[128,8,256]{2,1,0:T(8,128)}, f32[128,8,256]{2,1,0:T(8,128)}, u32[]{:S(2)}, u32[]{:S(2)}) collective-permute-start(f32[128,8,256]{2,1,0:T(8,128)} %get-tuple-element.19.refs_4_.refs_0_), channel_id=1, source_target_pairs={{0,30},{2,0},{4,2},{6,4},{8,6},{10,8},{12,10},{14,12},{16,14},{18,... | collective-permute-start | bytes 3145736 | tf_op jit(solution)/shard_map/ppermute | solution.py:20
  180.1 1.4 copy-start.2
  188.3 49.3 %collective-permute-start.20 = (f32[128,8,256]{2,1,0:T(8,128)}, f32[128,8,256]{2,1,0:T(8,128)}, u32[]{:S(2)}, u32[]{:S(2)}) collective-permute-start(f32[128,8,256]{2,1,0:T(8,128)} %core_send.3.refs_4_), channel_id=1, source_target_pairs={{0,1},{1,0},{2,3},{3,2},{4,5},{5,4},{6,7},{7,6},{8,9},{9,8},{10,11... | collective-permute-start | bytes 3145736 | tf_op jit(solution)/shard_map/ppermute | solution.py:20
  192.8 1.0 copy-start.7
  214.6 59.2 %collective-permute-start.22 = (f32[128,8,256]{2,1,0:T(8,128)}, f32[128,8,256]{2,1,0:T(8,128)S(1)}, u32[]{:S(2)}, u32[]{:S(2)}) collective-permute-start(f32[128,8,256]{2,1,0:T(8,128)} %get-tuple-element.21.refs_3_.refs_0_), channel_id=1, source_target_pairs={{0,2},{2,4},{4,6},{6,8},{8,10},{10,12},{12,14},{14,16},{16,18},{18... | collective-permute-start | bytes 3145736 | tf_op jit(solution)/shard_map/ppermute | solution.py:20
  226.7 47.2 %collective-permute-start.23 = (f32[128,8,256]{2,1,0:T(8,128)}, f32[128,8,256]{2,1,0:T(8,128)S(1)}, u32[]{:S(2)}, u32[]{:S(2)}) collective-permute-start(f32[128,8,256]{2,1,0:T(8,128)} %get-tuple-element.21.refs_3_.refs_0_), channel_id=1, source_target_pairs={{0,30},{2,0},{4,2},{6,4},{8,6},{10,8},{12,10},{14,12},{16,14},{18,... | collective-permute-start | bytes 3145736 | tf_op jit(solution)/shard_map/ppermute | solution.py:20
  226.7 33.0 %all-to-all-start = ((f32[32,8,256]{2,1,0:T(8,128)}), f32[32,8,256]{2,1,0:T(8,128)S(1)}, u32[]{:S(2)}, u32[]{:S(2)}) async-start(f32[32,8,256]{2,1,0:T(8,128)} %bitcast.5), calls=%async_computation | async-start | bytes 524288 | tf_op jit(solution)/shard_map/all_to_all | solution.py:354
  235.9 47.9 %collective-permute-start.21 = (f32[128,8,256]{2,1,0:T(8,128)}, f32[128,8,256]{2,1,0:T(8,128)S(1)}, u32[]{:S(2)}, u32[]{:S(2)}) collective-permute-start(f32[128,8,256]{2,1,0:T(8,128)} %place.12.refs_3_), channel_id=1, source_target_pairs={{0,1},{1,0},{2,3},{3,2},{4,5},{5,4},{6,7},{7,6},{8,9},{9,8},{10,11... | collective-permute-start | bytes 3145736 | tf_op jit(solution)/shard_map/ppermute | solution.py:20
  241.7 49.0 %collective-permute-start.25 = (f32[128,8,256]{2,1,0:T(8,128)}, f32[128,8,256]{2,1,0:T(8,128)}, u32[]{:S(2)}, u32[]{:S(2)}) collective-permute-start(f32[128,8,256]{2,1,0:T(8,128)} %core_finish.3.refs_1_.refs_0_), channel_id=1, source_target_pairs={{0,2},{2,4},{4,6},{6,8},{8,10},{10,12},{12,14},{14,16},{16,18},{18... | collective-permute-start | bytes 3145736 | tf_op jit(solution)/shard_map/ppermute | solution.py:20
  241.7 48.9 %collective-permute-start.26 = (f32[128,8,256]{2,1,0:T(8,128)}, f32[128,8,256]{2,1,0:T(8,128)}, u32[]{:S(2)}, u32[]{:S(2)}) collective-permute-start(f32[128,8,256]{2,1,0:T(8,128)} %core_finish.3.refs_1_.refs_0_), channel_id=1, source_target_pairs={{0,30},{2,0},{4,2},{6,4},{8,6},{10,8},{12,10},{14,12},{16,14},{18,... | collective-permute-start | bytes 3145736 | tf_op jit(solution)/shard_map/ppermute | solution.py:20
  259.7 0.7 copy-start.1
  262.8 24.7 %all-to-all-start.1 = ((f32[32,8,256]{2,1,0:T(8,128)}), f32[32,8,256]{2,1,0:T(8,128)S(1)}, u32[]{:S(2)}, u32[]{:S(2)}) async-start(f32[32,8,256]{2,1,0:T(8,128)} %sum.1.refs_4_), calls=%async_computation.1 | async-start | bytes 524288 | tf_op jit(solution)/shard_map/all_to_all | solution.py:360
  273.8 1.0 copy-start.3
  274.8 1.0 copy-start.4
  282.0 25.5 %collective-permute-start.24 = (f32[128,8,256]{2,1,0:T(8,128)}, f32[128,8,256]{2,1,0:T(8,128)S(1)}, u32[]{:S(2)}, u32[]{:S(2)}) collective-permute-start(f32[128,8,256]{2,1,0:T(8,128)} %place.14.refs_2_), channel_id=1, source_target_pairs={{0,1},{1,0},{2,3},{3,2},{4,5},{5,4},{6,7},{7,6},{8,9},{9,8},{10,11... | collective-permute-start | bytes 3145736 | tf_op jit(solution)/shard_map/ppermute | solution.py:20
  283.8 1.0 copy-start.5
  287.4 0.7 copy-start
  307.5 1.0 copy-start.6

commit v2 on v1

--- a/solution.py
+++ b/solution.py
@@ -11,7 +11,8 @@
 POINTS = 128
 TILE = 8
 VMEM_LIMIT = 60 * 1024 * 1024
-COST = pl.CostEstimate(flops=3 * 10**10, bytes_accessed=0, transcendentals=0)
+HEAVY = 3 * 10**10
+WEIGHTS = {15: 0.3, 16: 0.3, 19: 0, 21: 0, 22: 0, 26: 0, 28: 0.1, 29: 0.1, 30: 3, 31: 3, 32: 3}
 MINE, THEIRS, CORE, SOURCE, SLOT = 0, 1, 2, 3, 3 + BLOCKS_DEV
 
 
@@ -54,8 +55,11 @@
     def __init__(self, index):
         self.index = index
         self.last = []
-
-    def call(self, kernel, name, grid, inputs, outputs, aliases=None, scratch=()):
+        self.count = 0
+
+    def call(self, kernel, name, grid, inputs, outputs, aliases=None, scratch=(), index=None):
+        weight = WEIGHTS.get(self.count, 1)
+        self.count += 1
         held = [array for array, _ in inputs]
         extra = [a for a in self.last if not any(a is h for h in held)]
         count = len(inputs)
@@ -75,9 +79,9 @@
             ),
             input_output_aliases={k + 1: v for k, v in (aliases or {}).items()},
             compiler_params=pltpu.CompilerParams(vmem_limit_bytes=VMEM_LIMIT),
-            cost_estimate=COST,
+            cost_estimate=pl.CostEstimate(flops=int(HEAVY * weight), bytes_accessed=0, transcendentals=0),
             name=name,
-        )(self.index, *held, *extra)
+        )(self.index if index is None else index, *held, *extra)
         self.last = [result[0]]
         return result
 
@@ -144,30 +148,36 @@
         put_species(out_ref, s, species(arrived_ref, s) + dot3(at, halves(species(field_ref, s)), dot))
 
 
-def received_kernel(
-    first, last, index_ref, factor_ref, cross_factor_ref, mine_ref, theirs_ref, *rest
-):
-    core_ref, cross_ref = rest[-2:]
+def cross_kernel(first, last, index_ref, mine_ref, theirs_ref, *rest):
+    out_ref = rest[-1]
     step = pl.program_id(0)
 
     @pl.when(step == 0)
     def _():
-        cross_ref[...] = jnp.zeros_like(cross_ref) if first else rest[0][...]
-
-    at = halves(jnp.concatenate([factor_ref[...].T, cross_factor_ref[...].T], axis=1))
-    total = cross_ref[...]
+        out_ref[...] = jnp.zeros_like(out_ref) if first else rest[0][...]
+
+    total = out_ref[...]
     for s in range(0, TILE, 2):
-        mine = halves(species(mine_ref, s))
-        theirs = halves(species(theirs_ref, s))
-        total = total + dot3(mine, theirs, dot_nt)
-        both = tuple(jnp.concatenate([m, t], axis=0) for m, t in zip(mine, theirs))
-        put_species(core_ref, s, dot3(at, both, dot))
-    cross_ref[...] = total
+        total = total + dot3(halves(species(mine_ref, s)), halves(species(theirs_ref, s)), dot_nt)
+    out_ref[...] = total
 
     if last:
         @pl.when((step == pl.num_programs(0) - 1) & (index_ref[MINE] == 1))
         def _():
-            cross_ref[...] = cross_ref[...].T
+            out_ref[...] = out_ref[...].T
+
+
+def core_kernel(index_ref, factor_ref, cross_factor_ref, mine_ref, theirs_ref, out_ref):
+    at = halves(jnp.concatenate([factor_ref[...].T, cross_factor_ref[...].T], axis=1))
+    for s in range(0, TILE, 2):
+        both = jnp.concatenate([species(mine_ref, s), species(theirs_ref, s)], axis=0)
+        put_species(out_ref, s, dot3(at, halves(both), dot))
+
+
+def received_kernel(first, index_ref, factor_ref, cross_factor_ref, mine_ref, theirs_ref, *rest):
+    core_ref, cross_ref = rest[-2:]
+    core_kernel(index_ref, factor_ref, cross_factor_ref, mine_ref, theirs_ref, core_ref)
+    cross_kernel(first, False, index_ref, mine_ref, theirs_ref, *rest[:-2], cross_ref)
 
 
 def diagonal_kernel(scale, index_ref, field_ref, keep_ref, send_ref, high_ref, mixed_ref):
@@ -278,6 +288,7 @@
     any_space = pl.BlockSpec(memory_space=pl.ANY)
     whole_factor = whole(factor.shape)
     slabs = 4
+    late = (2, 3)
 
     def staging(rows):
         return [pltpu.VMEM((rows, TILE, points), jnp.float32)] + [pltpu.SemaphoreType.DMA((slabs,))] * 2
@@ -294,17 +305,20 @@
     def send_field(i):
         kernel = functools.partial(copy_field_kernel, i)
         out = ((z, TILE, points), any_space)
-        return over_gz(steps.call(kernel, "copy", (1,), [(field, any_space)], [out], None, staging(z))[0])
+        index = places if i == 0 else None
+        return over_gz(steps.call(kernel, "copy", (1,), [(field, any_space)], [out], None, staging(z), index)[0])
 
     def send_factor():
         out = ((z, rank), whole((z, rank)))
-        half = over_gz(steps.call(copy_kernel, "copy", (1,), [(factor, ranks(z, rank, CORE))], [out])[0])
+        half = steps.call(copy_kernel, "copy", (1,), [(factor, ranks(z, rank, CORE))], [out], index=places)[0]
+        half = over_gz(half)
         return half, exchanged(half, 1)
 
     def core_send(i):
         inputs = [(factor, ranks(z, rank, THEIRS)), (field, field_chunk(z, chunks, MINE, i))]
         out = ((rank, TILE, points), core_chunk(rank))
-        return steps.call(core_part_kernel, "core_send", (columns,), inputs, [out])[0]
+        index = places if i == late[0] else None
+        return steps.call(core_part_kernel, "core_send", (columns,), inputs, [out], index=index)[0]
 
     def core_finish(i, arrived):
         inputs = [
@@ -315,19 +329,26 @@
         out = ((rank, TILE, points), core_chunk(rank))
         return steps.call(core_finish_kernel, "core_finish", (columns,), inputs, [out])[0]
 
-    def received(i, theirs, cross_factor, cross, both):
-        out_rank = 2 * rank if both else rank
-        factor_spec = whole_factor if both else ranks(z, rank, MINE)
-        inputs = [
-            (factor, factor_spec),
-            (cross_factor, factor_spec),
-            (field, field_chunk(z, chunks, MINE, i)),
-            (theirs, pl.BlockSpec((z, TILE, POINTS), lambda p, w: (0, 0, p))),
-        ]
+    def both_halves(i, theirs):
+        received = pl.BlockSpec((z, TILE, POINTS), lambda p, w: (0, 0, p))
+        return [(field, field_chunk(z, chunks, MINE, i)), (theirs, received)]
+
+    def add_cross(i, theirs, cross):
+        inputs = both_halves(i, theirs) + ([] if cross is None else [(cross, whole((z, z)))])
+        kernel = functools.partial(cross_kernel, cross is None, i == chunks - 1)
+        return steps.call(kernel, "cross", (columns,), inputs, [((z, z), whole((z, z)))])[0]
+
+    def core_of(i, theirs, cross_factor, ranks_spec, out_rank):
+        inputs = [(factor, ranks_spec), (cross_factor, ranks_spec)] + both_halves(i, theirs)
+        out = ((out_rank, TILE, points), core_chunk(out_rank))
+        return steps.call(core_kernel, "core", (columns,), inputs, [out])[0]
+
+    def received(i, theirs, cross_factor, cross, ranks_spec, out_rank):
+        inputs = [(factor, ranks_spec), (cross_factor, ranks_spec)] + both_halves(i, theirs)
         if cross is not None:
             inputs.append((cross, whole((z, z))))
         outputs = [((out_rank, TILE, points), core_chunk(out_rank)), ((z, z), whole((z, z)))]
-        kernel = functools.partial(received_kernel, cross is None, i == chunks - 1)
+        kernel = functools.partial(received_kernel, cross is None)
         return steps.call(kernel, "received", (columns,), inputs, outputs)
 
     def diagonal_gram():
@@ -364,7 +385,8 @@
         spec = pl.BlockSpec((rank, TILE, POINTS), lambda j, w: (rows(w), 0, w[SLOT + j]))
         inputs = [(part, spec) for part in parts]
         if core is None:
-            return steps.call(place_kernel, "place", (BLOCKS_DEV,), inputs, [((rank, TILE, points), core_chunk(rank))])[0]
+            out = ((rank, TILE, points), core_chunk(rank))
+            return steps.call(place_kernel, "place", (BLOCKS_DEV,), inputs, [out])[0]
         out = ((rank, count, points), field_chunk(rank, chunks, at, i))
         if core is EMPTY:
             return steps.call(place_kernel, "place", (BLOCKS_DEV,), inputs, [out])[0]
@@ -378,6 +400,7 @@
         return steps.call(kernel, "put", (1,), inputs, [out], {1: 0}, staging(rank))[0]
 
     fields, ready, arrived = {}, {}, {}
+    own_ranks = ranks(z, rank, MINE)
     arrived[2] = over_gz(core_send(2))
     cross_half = send_factor()
     fields[0] = send_field(0)
@@ -387,40 +410,40 @@
     diagonal = small(add_kernel, diagonal, half)
     half = exchanged(diagonal, 2)
     cross_factor = joined(1, *cross_half)
+    late2 = neighbours(core_finish(2, arrived[2]))
     diagonal = small(add_kernel, diagonal, half)
     half = exchanged(diagonal, 4)
-    late2 = neighbours(core_finish(2, arrived[2]))
+    core = place(late2, None, EMPTY, THEIRS, 2)
     diagonal = small(add_kernel, diagonal, half)
     half = exchanged(diagonal, 8)
-    core = place(late2, None, EMPTY, THEIRS, 2)
+    part, cross = received(0, fields[0], cross_factor, None, whole_factor, 2 * rank)
+    ready[0] = neighbours(part)
     diagonal = small(add_kernel, diagonal, half)
-    half = exchanged(diagonal, 1)
-    part, cross = received(0, fields[0], cross_factor, None, True)
-    ready[0] = neighbours(part)
-    diagonal = joined(0, diagonal, half)
     fields[2] = send_field(2)
-    part, cross = received(1, fields[1], cross_factor, cross, True)
+    part, cross = received(1, fields[1], cross_factor, cross, whole_factor, 2 * rank)
     ready[1] = neighbours(part)
     core = place(ready[0], MINE, core, MINE, 0)
     fields[3] = send_field(3)
-    part, cross = received(2, fields[2], cross_factor, cross, False)
+    part, cross = received(2, fields[2], cross_factor, cross, own_ranks, rank)
     ready[2] = neighbours(part)
     core = place(ready[1], MINE, core, MINE, 1)
+    diagonal = small(copy_kernel, diagonal)
+    half = exchanged(diagonal, 1)
     arrived[3] = over_gz(core_send(3))
+    diagonal = joined(0, diagonal, half)
     core = place(ready[2], None, core, MINE, 2)
-    part, cross = received(3, fields[3], cross_factor, cross, False)
-    ready[3] = neighbours(part)
-    cross = spread(cross, ("xy", "gz"))
+    ready[3] = neighbours(core_of(3, fields[3], cross_factor, own_ranks, rank))
+    cross = spread(add_cross(3, fields[3], cross), ("xy", "gz"))
     arrived[0] = over_gz(place(ready[0], THEIRS))
+    arrived[1] = over_gz(place(ready[1], THEIRS))
     late3 = neighbours(core_finish(3, arrived[3]))
+    core = place(ready[3], None, core, MINE, 3)
     cross = summed(cross, ("xy", "gz"))
-    core = place(ready[3], None, core, MINE, 3)
-    arrived[1] = over_gz(place(ready[1], THEIRS))
     core = put(arrived[0], core, 0)
+    core = place(late3, None, core, THEIRS, 3)
+    core = put(arrived[1], core, 1)
     gram_specs = [(diagonal, whole((z, z))), (cross, whole((z, z)))]
     gram = steps.call(gram_kernel, "gram", (1,), gram_specs, [((z, 2 * z), whole((z, 2 * z)))])[0]
-    core = place(late3, None, core, THEIRS, 3)
-    core = put(arrived[1], core, 1)
     return (gram, core)
 
 

time: 313 us -> 295 us (0.942)
  waiting for transfers between devices: 97.4 us -> 79.2 us
  Pallas kernels: 120 us -> 130 us
  starting transfers between devices: 78.2 us -> 71.7 us
  local copies, waits for them, and re-layouts: 14.3 us -> 11 us
    ppermute x21, starting transfers between devices: 48.4 us -> 30 us  [shifted(): lax.ppermute(array, axis, [(i, (i + by) % length) for i in range(length)])]
    all_to_all x1, waiting for transfers between devices: 13.6 us -> 0.01 us  [spread(): return lax.all_to_all(pieces, axes, split_axis=0, concat_axis=0, tiled=True)]
    pallas_call x32 -> x34, Pallas kernels: 120 us -> 130 us  [call(): pl.pallas_call(body, out_shape=[jax.ShapeDtypeStruct(shape, jnp.float32)...]
    ppermute x6, starting transfers between devices: 12.6 us -> 20.8 us  [exchanged(): lax.ppermute(part, 'xy', [(i, i ^ bit) for i in range(lax.axis_size('xy'))])]
    all_to_all x1, starting transfers between devices: 11 us -> 15 us  [summed(): lax.all_to_all(total, axes, split_axis=0, concat_axis=0, tiled=True)]
    ppermute x21, waiting for transfers between devices: 82.5 us -> 79.2 us  [shifted(): lax.ppermute(array, axis, [(i, (i + by) % length) for i in range(length)])]
    unnamed x34, local copies, waits for them, and re-layouts: 13.6 us -> 10.4 us
  transfers between devices with their start and end apart: 29 -> 29, of which waited for: 9 -> 6; matrix products, arithmetic and copies ran while one was open for 0% -> 0% of each run, Pallas kernels for 36% -> 42%
where the time goes in v2:
time: 295 us; the launch traced here: 294 us
  Pallas kernels  130 us (44%)
  waiting for transfers between devices  79.2 us (27%)
  starting transfers between devices  71.7 us (24%)
  local copies, waits for them, and re-layouts  11 us (4%)
    pallas_call x34, Pallas kernels, call(): pl.pallas_call(body, out_shape=[jax.ShapeDtypeStruct(shape, jnp.float32)...  130 us
    ppermute x21, waiting for transfers between devices, shifted(): lax.ppermute(array, axis, [(i, (i + by) % length) for i in range(length)])  79.2 us
    ppermute x21, starting transfers between devices, shifted(): lax.ppermute(array, axis, [(i, (i + by) % length) for i in range(length)])  30 us
    ppermute x6, starting transfers between devices, exchanged(): lax.ppermute(part, 'xy', [(i, i ^ bit) for i in range(lax.axis_size('xy'))])  20.8 us
    all_to_all x1, starting transfers between devices, summed(): lax.all_to_all(total, axes, split_axis=0, concat_axis=0, tiled=True)  15 us
    unnamed x34, local copies, waits for them, and re-layouts  10.4 us
  transfers between devices with their start and end apart: 29, of which 6 were waited for; matrix products, arithmetic and copies ran while one was open for 0% of the time, Pallas kernels for 42%

profile of v2, /device:TPU:0, one launch (start us, length us, event | category | flops | bytes accessed | tf_op | source)
XLA Modules:
  0.0 293.9 jit_solution(3871515704706140015)
XLA Ops:
  1.3 3.8 %core_send.2.refs_1_ = f32[128,8,256]{2,1,0:T(8,128)} custom-call(s32[3]{0:T(128)} %pad_add_fusion.index_ref, f32[256,256]{1,0:T(8,128)} %refs_0_.29, f32[256,64,256]{2,1,0:T(8,128)} %refs_1_.7), custom_call_target="tpu_custom_call" | custom-call | flops 30000001024 | tf_op jit(solution)/shard_map/core_send/pallas_call | solution.py:70
  5.0 3.0 %collective-permute-start.2 = (f32[128,8,256]{2,1,0:T(8,128)}, f32[128,8,256]{2,1,0:T(8,128)}, u32[]{:S(2)}, u32[]{:S(2)}) collective-permute-start(f32[128,8,256]{2,1,0:T(8,128)} %core_send.2.refs_1_), channel_id=1, source_target_pairs={{0,1},{1,0},{2,3},{3,2},{4,5},{5,4},{6,7},{7,6},{8,9},{9,8},{10,11... | collective-permute-start | bytes 3145736 | tf_op jit(solution)/shard_map/ppermute | solution.py:21
  10.2 3.2 %copy.26.refs_1_ = f32[256,8,256]{2,1,0:T(8,128)} custom-call(s32[3]{0:T(128)} %pad_add_fusion.index_ref, f32[256,64,256]{2,1,0:T(8,128)} %refs_1_.7, f32[256,128]{1,0:T(8,128)} %copy.25.refs_1_), custom_call_target="tpu_custom_call" | custom-call | flops 30000001024 | tf_op jit(solution)/shard_map/copy/pallas_call | solution.py:70
  16.1 16.5 %diagonal.1 = (f32[128,256]{1,0:T(8,128)}, f32[128,256]{1,0:T(8,128)}) custom-call(s32[7]{0:T(128)} %concatenate.4.index_ref, f32[256,64,256]{2,1,0:T(8,128)} %refs_1_.7, f32[256,8,256]{2,1,0:T(8,128)} %copy.26.refs_1_), custom_call_target="tpu_custom_call" | custom-call | flops 30000001024 | tf_op jit(solution)/shard_map/diagonal/pallas_call | solution.py:70
  32.6 3.1 %copy.27.refs_2_ = f32[256,8,256]{2,1,0:T(8,128)} custom-call(s32[7]{0:T(128)} %concatenate.4.index_ref, f32[256,64,256]{2,1,0:T(8,128)} %refs_1_.7, f32[128,256]{1,0:T(8,128)} %get-tuple-element.10.refs_1_.refs_0_), custom_call_target="tpu_custom_call" | custom-call | flops 30000001024 | tf_op jit(solution)/shard_map/copy/pallas_call | solution.py:70
  37.0 2.3 small.5.refs_2_.refs_0_
  41.6 2.4 join.2.refs_3_.refs_1_
  44.0 4.0 %core_finish.2.refs_2_.refs_0_ = f32[128,8,256]{2,1,0:T(8,128)} custom-call(s32[7]{0:T(128)} %concatenate.4.index_ref, f32[256,256]{1,0:T(8,128)} %refs_0_.29, f32[256,64,256]{2,1,0:T(8,128)} %refs_1_.7, f32[128,8,256]{2,1,0:T(8,128)} %collective-permute-done.2.refs_2_, f32[256,256]{1,0:T(8,128)} %join.2.refs_3_.refs_1_), custom_call_target="tpu_custom_call" | custom-call | flops 30000001024 | tf_op jit(solution)/shard_map/core_finish/pallas_call | solution.py:70
  48.0 3.2 %collective-permute-start.7 = (f32[128,8,256]{2,1,0:T(8,128)}, f32[128,8,256]{2,1,0:T(8,128)S(1)}, u32[]{:S(2)}, u32[]{:S(2)}) collective-permute-start(f32[128,8,256]{2,1,0:T(8,128)} %core_finish.2.refs_2_.refs_0_), channel_id=1, source_target_pairs={{0,30},{2,0},{4,2},{6,4},{8,6},{10,8},{12,10},{14,12},{16,14},{18,... | collective-permute-start | bytes 3145736 | tf_op jit(solution)/shard_map/ppermute | solution.py:21
  51.9 2.3 small.6.refs_3_.refs_0_
  54.2 11.1 %collective-permute-done.7.refs_2_ = f32[128,8,256]{2,1,0:T(8,128)S(1)} collective-permute-done((f32[128,8,256]{2,1,0:T(8,128)}, f32[128,8,256]{2,1,0:T(8,128)S(1)}, u32[]{:S(2)}, u32[]{:S(2)}) %collective-permute-start.7) | collective-permute-done | bytes 1048608 | tf_op jit(solution)/shard_map/ppermute | solution.py:21
  65.2 4.6 %collective-permute-done.6.refs_1_ = f32[128,8,256]{2,1,0:T(8,128)S(1)} collective-permute-done((f32[128,8,256]{2,1,0:T(8,128)}, f32[128,8,256]{2,1,0:T(8,128)S(1)}, u32[]{:S(2)}, u32[]{:S(2)}) %collective-permute-start.6) | collective-permute-done | bytes 1048608 | tf_op jit(solution)/shard_map/ppermute | solution.py:21
  70.8 3.1 %place.8.refs_2_.refs_3_ = f32[128,64,256]{2,1,0:T(8,128)} custom-call(s32[7]{0:T(128)} %concatenate.4.index_ref, f32[128,8,256]{2,1,0:T(8,128)} %core_finish.2.refs_2_.refs_0_, f32[128,8,256]{2,1,0:T(8,128)} %copy-done.10, f32[128,8,256]{2,1,0:T(8,128)} %copy-done.9, f32[128,256]{1,0:T(8,128)} %small.6.refs_3_.refs_0_), custom_call_target="tpu_custom_call" | custom-call | flops 30000001024 | tf_op jit(solution)/shard_map/place/pallas_call | solution.py:70
  74.5 2.3 small.7.refs_4_.refs_0_
  76.8 3.2 %collective-permute-done.9.refs_3_ = f32[256,8,256]{2,1,0:T(8,128)} collective-permute-done((f32[256,8,256]{2,1,0:T(8,128)}, f32[256,8,256]{2,1,0:T(8,128)}, u32[]{:S(2)}, u32[]{:S(2)}) %collective-permute-start.9) | collective-permute-done | bytes 2097184 | tf_op jit(solution)/shard_map/ppermute | solution.py:21
  80.1 8.3 %received.3 = (f32[256,8,256]{2,1,0:T(8,128)}, f32[256,256]{1,0:T(8,128)}) custom-call(s32[7]{0:T(128)} %concatenate.4.index_ref, f32[256,256]{1,0:T(8,128)} %refs_0_.29, f32[256,256]{1,0:T(8,128)} %join.2.refs_3_.refs_1_, f32[256,64,256]{2,1,0:T(8,128)} %refs_1_.7, f32[256,8,256]{2,1,0:T(8,128)} %collective-permute-done.9.refs_3_, ...), custom_call_target="tpu_custom_call" | custom-call | flops 30000001024 | tf_op jit(solution)/shard_map/received/pallas_call | solution.py:70
  88.4 2.5 collective-permute-start.14
  93.7 2.3 small.8.refs_1_.refs_0_
  96.0 3.1 %copy.28.refs_5_ = f32[256,8,256]{2,1,0:T(8,128)} custom-call(s32[7]{0:T(128)} %concatenate.4.index_ref, f32[256,64,256]{2,1,0:T(8,128)} %refs_1_.7, f32[128,256]{1,0:T(8,128)} %small.8.refs_1_.refs_0_), custom_call_target="tpu_custom_call" | custom-call | flops 30000001024 | tf_op jit(solution)/shard_map/copy/pallas_call | solution.py:70
  100.7 24.3 %collective-permute-done.10.refs_3_ = f32[256,8,256]{2,1,0:T(8,128)} collective-permute-done((f32[256,8,256]{2,1,0:T(8,128)}, f32[256,8,256]{2,1,0:T(8,128)}, u32[]{:S(2)}, u32[]{:S(2)}) %collective-permute-start.10) | collective-permute-done | bytes 2097184 | tf_op jit(solution)/shard_map/ppermute | solution.py:21
  125.0 8.3 %received.4 = (f32[256,8,256]{2,1,0:T(8,128)}, f32[256,256]{1,0:T(8,128)}) custom-call(s32[7]{0:T(128)} %concatenate.4.index_ref, f32[256,256]{1,0:T(8,128)} %refs_0_.29, f32[256,256]{1,0:T(8,128)} %join.2.refs_3_.refs_1_, f32[256,64,256]{2,1,0:T(8,128)} %refs_1_.7, f32[256,8,256]{2,1,0:T(8,128)} %collective-permute-done.10.refs_3_, ...), custom_call_target="tpu_custom_call" | custom-call | flops 30000001024 | tf_op jit(solution)/shard_map/received/pallas_call | solution.py:70
  133.3 2.5 collective-permute-start.12
  135.9 3.1 %place.9.refs_1_.refs_3_ = f32[128,64,256]{2,1,0:T(8,128)} custom-call(s32[7]{0:T(128)} %concatenate.4.index_ref, f32[256,8,256]{2,1,0:T(8,128)} %get-tuple-element.12.refs_2_.refs_0_, f32[256,8,256]{2,1,0:T(8,128)} %collective-permute-done.13.refs_1_, f32[256,8,256]{2,1,0:T(8,128)} %collective-permute-done.14.refs_2_, ...), custom_call_target="tpu_custom_call", output_to_operand_aliasing={{}: (4, {})} | custom-call | flops 8999999488 | tf_op jit(solution)/shard_map/place/pallas_call | solution.py:70
  138.9 3.1 %copy.29.refs_5_ = f32[256,8,256]{2,1,0:T(8,128)} custom-call(s32[7]{0:T(128)} %concatenate.4.index_ref, f32[256,64,256]{2,1,0:T(8,128)} %refs_1_.7, f32[128,64,256]{2,1,0:T(8,128)} %place.9.refs_1_.refs_3_), custom_call_target="tpu_custom_call" | custom-call | flops 8999999488 | tf_op jit(solution)/shard_map/copy/pallas_call | solution.py:70
  143.6 26.3 %collective-permute-done.15.refs_3_ = f32[256,8,256]{2,1,0:T(8,128)} collective-permute-done((f32[256,8,256]{2,1,0:T(8,128)}, f32[256,8,256]{2,1,0:T(8,128)}, u32[]{:S(2)}, u32[]{:S(2)}) %collective-permute-start.15) | collective-permute-done | bytes 2097184 | tf_op jit(solution)/shard_map/ppermute | solution.py:21
  169.9 6.6 %received.5 = (f32[128,8,256]{2,1,0:T(8,128)}, f32[256,256]{1,0:T(8,128)}) custom-call(s32[7]{0:T(128)} %concatenate.4.index_ref, f32[256,256]{1,0:T(8,128)} %refs_0_.29, f32[256,256]{1,0:T(8,128)} %join.2.refs_3_.refs_1_, f32[256,64,256]{2,1,0:T(8,128)} %refs_1_.7, f32[256,8,256]{2,1,0:T(8,128)} %collective-permute-done.15.refs_3_, ...), custom_call_target="tpu_custom_call" | custom-call | flops 30000001024 | tf_op jit(solution)/shard_map/received/pallas_call | solution.py:70
  176.5 2.5 collective-permute-start.19
  180.4 3.1 %place.10.refs_1_.refs_3_ = f32[128,64,256]{2,1,0:T(8,128)} custom-call(s32[7]{0:T(128)} %concatenate.4.index_ref, f32[256,8,256]{2,1,0:T(8,128)} %get-tuple-element.14.refs_4_.refs_0_, f32[256,8,256]{2,1,0:T(8,128)} %collective-permute-done.11.refs_1_, f32[256,8,256]{2,1,0:T(8,128)} %copy-done, ...), custom_call_target="tpu_custom_call", output_to_operand_aliasing={{}: (4, {})} | custom-call | flops 30000001024 | tf_op jit(solution)/shard_map/place/pallas_call | solution.py:70
  183.5 2.2 small.9.refs_2_.refs_0_
  185.7 18.7 %collective-permute-start.16 = (f32[128,256]{1,0:T(8,128)}, f32[128,256]{1,0:T(8,128)S(1)}, u32[]{:S(2)}, u32[]{:S(2)}) collective-permute-start(f32[128,256]{1,0:T(8,128)} %small.9.refs_2_.refs_0_), channel_id=1, source_target_pairs={{0,2},{2,0},{4,6},{6,4},{8,10},{10,8},{12,14},{14,12},{16,18},{18,... | collective-permute-start | bytes 393224 | tf_op jit(solution)/shard_map/ppermute | solution.py:303
  204.4 3.8 %core_send.3.refs_2_ = f32[128,8,256]{2,1,0:T(8,128)} custom-call(s32[7]{0:T(128)} %concatenate.4.index_ref, f32[256,256]{1,0:T(8,128)} %refs_0_.29, f32[256,64,256]{2,1,0:T(8,128)} %refs_1_.7, f32[128,256]{1,0:T(8,128)} %small.9.refs_2_.refs_0_), custom_call_target="tpu_custom_call" | custom-call | flops 30000001024 | tf_op jit(solution)/shard_map/core_send/pallas_call | solution.py:70
  210.4 2.4 join.3.refs_4_.refs_0_
  213.7 3.1 %place.11.refs_4_.refs_3_ = f32[128,64,256]{2,1,0:T(8,128)} custom-call(s32[7]{0:T(128)} %concatenate.4.index_ref, f32[128,8,256]{2,1,0:T(8,128)} %get-tuple-element.16.refs_4_.refs_0_, f32[128,8,256]{2,1,0:T(8,128)} %collective-permute-done.18.refs_1_, f32[128,8,256]{2,1,0:T(8,128)} %copy-done.3, ...), custom_call_target="tpu_custom_call", output_to_operand_aliasing={{}: (4, {})} | custom-call | tf_op jit(solution)/shard_map/place/pallas_call | solution.py:70
  216.8 5.0 %core.1.refs_3_.refs_0_ = f32[128,8,256]{2,1,0:T(8,128)} custom-call(s32[7]{0:T(128)} %concatenate.4.index_ref, f32[256,256]{1,0:T(8,128)} %refs_0_.29, f32[256,256]{1,0:T(8,128)} %join.2.refs_3_.refs_1_, f32[256,64,256]{2,1,0:T(8,128)} %refs_1_.7, f32[256,8,256]{2,1,0:T(8,128)} %collective-permute-done.17.refs_3_.refs_1_, f32[128,64,256]{2,1,0:T(8,128)} %place.11.refs_4_.refs_3_), custom_call_target="tpu_custom_call" | custom-call | flops 30000001024 | tf_op jit(solution)/shard_map/core/pallas_call | solution.py:70
  222.4 4.6 %cross.1.refs_3_ = f32[256,256]{1,0:T(8,128)} custom-call(s32[7]{0:T(128)} %concatenate.4.index_ref, f32[256,64,256]{2,1,0:T(8,128)} %refs_1_.7, f32[256,8,256]{2,1,0:T(8,128)} %collective-permute-done.17.refs_3_.refs_1_, f32[256,256]{1,0:T(8,128)} %get-tuple-element.17.refs_2_, f32[128,8,256]{2,1,0:T(8,128)} %core.1.refs_3_.refs_0_), custom_call_target="tpu_custom_call" | custom-call | flops 30000001024 | tf_op jit(solution)/shard_map/cross/pallas_call | solution.py:70
  227.0 5.9 %all-to-all-start = ((f32[32,8,256]{2,1,0:T(8,128)}), f32[32,8,256]{2,1,0:T(8,128)S(1)}, u32[]{:S(2)}, u32[]{:S(2)}) async-start(f32[32,8,256]{2,1,0:T(8,128)} %bitcast.5), calls=%async_computation | async-start | bytes 524288 | tf_op jit(solution)/shard_map/all_to_all | solution.py:375
  232.9 3.1 %place.12.refs_3_ = f32[128,8,256]{2,1,0:T(8,128)} custom-call(s32[7]{0:T(128)} %concatenate.4.index_ref, f32[256,8,256]{2,1,0:T(8,128)} %get-tuple-element.12.refs_2_.refs_0_, f32[256,8,256]{2,1,0:T(8,128)} %collective-permute-done.13.refs_1_, f32[256,8,256]{2,1,0:T(8,128)} %collective-permute-done.14.refs_2_, f32[256,256]{1,0:T(8,128)} %cross.1.refs_3_), custom_call_target="tpu_custom_call" | custom-call | flops 30000001024 | tf_op jit(solution)/shard_map/place/pallas_call | solution.py:70
  237.7 3.0 %place.13.refs_3_ = f32[128,8,256]{2,1,0:T(8,128)} custom-call(s32[7]{0:T(128)} %concatenate.4.index_ref, f32[256,8,256]{2,1,0:T(8,128)} %get-tuple-element.14.refs_4_.refs_0_, f32[256,8,256]{2,1,0:T(8,128)} %collective-permute-done.11.refs_1_, f32[256,8,256]{2,1,0:T(8,128)} %copy-done, f32[128,8,256]{2,1,0:T(8,128)} %place.12.refs_3_), custom_call_target="tpu_custom_call" | custom-call | tf_op jit(solution)/shard_map/place/pallas_call | solution.py:70
  240.8 4.0 %core_finish.3.refs_4_.refs_0_ = f32[128,8,256]{2,1,0:T(8,128)} custom-call(s32[7]{0:T(128)} %concatenate.4.index_ref, f32[256,256]{1,0:T(8,128)} %refs_0_.29, f32[256,64,256]{2,1,0:T(8,128)} %refs_1_.7, f32[128,8,256]{2,1,0:T(8,128)} %collective-permute-done.22.refs_2_, f32[128,8,256]{2,1,0:T(8,128)} %place.13.refs_3_), custom_call_target="tpu_custom_call" | custom-call | flops 30000001024 | tf_op jit(solution)/shard_map/core_finish/pallas_call | solution.py:70
  244.8 4.4 %collective-permute-start.25 = (f32[128,8,256]{2,1,0:T(8,128)}, f32[128,8,256]{2,1,0:T(8,128)}, u32[]{:S(2)}, u32[]{:S(2)}) collective-permute-start(f32[128,8,256]{2,1,0:T(8,128)} %core_finish.3.refs_4_.refs_0_), channel_id=1, source_target_pairs={{0,30},{2,0},{4,2},{6,4},{8,6},{10,8},{12,10},{14,12},{16,14},{18,... | collective-permute-start | bytes 3145736 | tf_op jit(solution)/shard_map/ppermute | solution.py:21
  251.2 3.1 %place.14.refs_1_ = f32[128,64,256]{2,1,0:T(8,128)} custom-call(s32[7]{0:T(128)} %concatenate.4.index_ref, f32[128,8,256]{2,1,0:T(8,128)} %core.1.refs_3_.refs_0_, f32[128,8,256]{2,1,0:T(8,128)} %copy-done.2, f32[128,8,256]{2,1,0:T(8,128)} %copy-done.1, f32[128,64,256]{2,1,0:T(8,128)} %place.11.refs_4_.refs_3_, ...), custom_call_target="tpu_custom_call", output_to_operand_aliasing={{}: (4, {})} | custom-call | flops 3000000000 | tf_op jit(solution)/shard_map/place/pallas_call | solution.py:70
  254.9 2.4 sum.1.refs_2_
  257.3 15.0 %all-to-all-start.1 = ((f32[32,8,256]{2,1,0:T(8,128)}), f32[32,8,256]{2,1,0:T(8,128)}, u32[]{:S(2)}, u32[]{:S(2)}) async-start(f32[32,8,256]{2,1,0:T(8,128)} %sum.1.refs_2_), calls=%async_computation.1 | async-start | bytes 524288 | tf_op jit(solution)/shard_map/all_to_all | solution.py:381
  273.3 2.6 put.2.refs_3_
  276.0 3.1 %place.15.refs_1_ = f32[128,64,256]{2,1,0:T(8,128)} custom-call(s32[7]{0:T(128)} %concatenate.4.index_ref, f32[128,8,256]{2,1,0:T(8,128)} %core_finish.3.refs_4_.refs_0_, f32[128,8,256]{2,1,0:T(8,128)} %collective-permute-done.24.refs_1_, f32[128,8,256]{2,1,0:T(8,128)} %collective-permute-done.25.refs_2_, ...), custom_call_target="tpu_custom_call", output_to_operand_aliasing={{}: (4, {})} | custom-call | flops 89999998976 | tf_op jit(solution)/shard_map/place/pallas_call | solution.py:70
  279.0 9.7 %collective-permute-done.23.refs_0_ = f32[128,8,256]{2,1,0:T(8,128)} collective-permute-done((f32[128,8,256]{2,1,0:T(8,128)}, f32[128,8,256]{2,1,0:T(8,128)}, u32[]{:S(2)}, u32[]{:S(2)}) %collective-permute-start.23) | collective-permute-done | bytes 1048608 | tf_op jit(solution)/shard_map/ppermute | solution.py:21
  288.7 2.6 put.3.refs_2_
  291.3 2.5 gram.1
  (81 shorter events, 28.1 us)
Async XLA Ops:
  5.0 39.0 %collective-permute-start.2 = (f32[128,8,256]{2,1,0:T(8,128)}, f32[128,8,256]{2,1,0:T(8,128)}, u32[]{:S(2)}, u32[]{:S(2)}) collective-permute-start(f32[128,8,256]{2,1,0:T(8,128)} %core_send.2.refs_1_), channel_id=1, source_target_pairs={{0,1},{1,0},{2,3},{3,2},{4,5},{5,4},{6,7},{7,6},{8,9},{9,8},{10,11... | collective-permute-start | bytes 3145736 | tf_op jit(solution)/shard_map/ppermute | solution.py:21
  10.2 5.2 %copy-start.6 = (s32[32]{0:T(128)S(1)}, s32[32]{0:T(128)}, u32[]{:S(2)}) copy-start(s32[32]{0:T(128)} %param.7) | copy-start | bytes 388
  10.2 5.2 %copy-start.7 = (s32[32]{0:T(128)S(1)}, s32[32]{0:T(128)}, u32[]{:S(2)}) copy-start(s32[32]{0:T(128)} %param.6) | copy-start | bytes 388
  10.2 25.7 %collective-permute-start.3 = (f32[256,128]{1,0:T(8,128)}, f32[256,128]{1,0:T(8,128)S(1)}, u32[]{:S(2)}, u32[]{:S(2)}) collective-permute-start(f32[256,128]{1,0:T(8,128)} %copy.25.refs_1_), channel_id=1, source_target_pairs={{0,1},{1,0},{2,3},{3,2},{4,5},{5,4},{6,7},{7,6},{8,9},{9,8},{10,11... | collective-permute-start | bytes 393224 | tf_op jit(solution)/shard_map/ppermute | solution.py:21
  13.5 66.6 %collective-permute-start.9 = (f32[256,8,256]{2,1,0:T(8,128)}, f32[256,8,256]{2,1,0:T(8,128)}, u32[]{:S(2)}, u32[]{:S(2)}) collective-permute-start(f32[256,8,256]{2,1,0:T(8,128)} %copy.26.refs_1_), channel_id=1, source_target_pairs={{0,1},{1,0},{2,3},{3,2},{4,5},{5,4},{6,7},{7,6},{8,9},{9,8},{10,11... | collective-permute-start | bytes 6291464 | tf_op jit(solution)/shard_map/ppermute | solution.py:21
  32.6 3.8 %collective-permute-start = (f32[128,256]{1,0:T(8,128)}, f32[128,256]{1,0:T(8,128)S(1)}, u32[]{:S(2)}, u32[]{:S(2)}) collective-permute-start(f32[128,256]{1,0:T(8,128)} %get-tuple-element.11), channel_id=1, source_target_pairs={{0,2},{2,0},{4,6},{6,4},{8,10},{10,8},{12,14},{14,12},{16,18},{18,... | collective-permute-start | bytes 393224 | tf_op jit(solution)/shard_map/ppermute | solution.py:303
  35.7 89.3 %collective-permute-start.10 = (f32[256,8,256]{2,1,0:T(8,128)}, f32[256,8,256]{2,1,0:T(8,128)}, u32[]{:S(2)}, u32[]{:S(2)}) collective-permute-start(f32[256,8,256]{2,1,0:T(8,128)} %copy.27.refs_2_), channel_id=1, source_target_pairs={{0,1},{1,0},{2,3},{3,2},{4,5},{5,4},{6,7},{7,6},{8,9},{9,8},{10,11... | collective-permute-start | bytes 6291464 | tf_op jit(solution)/shard_map/ppermute | solution.py:21
  35.9 3.4 %copy-start.11 = (f32[256,128]{1,0:T(8,128)}, f32[256,128]{1,0:T(8,128)S(1)}, u32[]{:S(2)}) copy-start(f32[256,128]{1,0:T(8,128)S(1)} %collective-permute-done.3.refs_0_) | copy-start | bytes 393220
  35.9 5.1 %collective-permute-start.4 = (f32[256,128]{1,0:T(8,128)S(1)}, f32[256,128]{1,0:T(8,128)S(1)}, u32[]{:S(2)}, u32[]{:S(2)}) collective-permute-start(f32[256,128]{1,0:T(8,128)S(1)} %collective-permute-done.3.refs_0_), channel_id=1, source_target_pairs={{0,2},{2,0},{4,6},{6,4},{8,10},{10,8},{12,14},{14,12},{16,18},{18,... | collective-permute-start | bytes 393224 | tf_op jit(solution)/shard_map/ppermute | solution.py:303
  36.4 0.7 copy-start.14
  39.3 11.9 %collective-permute-start.1 = (f32[128,256]{1,0:T(8,128)}, f32[128,256]{1,0:T(8,128)S(1)}, u32[]{:S(2)}, u32[]{:S(2)}) collective-permute-start(f32[128,256]{1,0:T(8,128)} %small.5.refs_2_.refs_0_), channel_id=1, source_target_pairs={{0,4},{2,6},{4,0},{6,2},{8,12},{10,14},{12,8},{14,10},{16,20},{18,... | collective-permute-start | bytes 393224 | tf_op jit(solution)/shard_map/ppermute | solution.py:303
  41.0 0.7 copy-start.15
  48.0 17.2 %collective-permute-start.7 = (f32[128,8,256]{2,1,0:T(8,128)}, f32[128,8,256]{2,1,0:T(8,128)S(1)}, u32[]{:S(2)}, u32[]{:S(2)}) collective-permute-start(f32[128,8,256]{2,1,0:T(8,128)} %core_finish.2.refs_2_.refs_0_), channel_id=1, source_target_pairs={{0,30},{2,0},{4,2},{6,4},{8,6},{10,8},{12,10},{14,12},{16,14},{18,... | collective-permute-start | bytes 3145736 | tf_op jit(solution)/shard_map/ppermute | solution.py:21
  51.2 18.6 %collective-permute-start.6 = (f32[128,8,256]{2,1,0:T(8,128)}, f32[128,8,256]{2,1,0:T(8,128)S(1)}, u32[]{:S(2)}, u32[]{:S(2)}) collective-permute-start(f32[128,8,256]{2,1,0:T(8,128)} %core_finish.2.refs_2_.refs_0_), channel_id=1, source_target_pairs={{0,2},{2,4},{4,6},{6,8},{8,10},{10,12},{12,14},{14,16},{16,18},{18... | collective-permute-start | bytes 3145736 | tf_op jit(solution)/shard_map/ppermute | solution.py:21
  51.2 0.7 copy-start.12
  54.2 19.7 %collective-permute-start.5 = (f32[128,256]{1,0:T(8,128)}, f32[128,256]{1,0:T(8,128)S(1)}, u32[]{:S(2)}, u32[]{:S(2)}) collective-permute-start(f32[128,256]{1,0:T(8,128)} %small.6.refs_3_.refs_0_), channel_id=1, source_target_pairs={{0,8},{2,10},{4,12},{6,14},{8,0},{10,2},{12,4},{14,6},{16,24},{18,... | collective-permute-start | bytes 393224 | tf_op jit(solution)/shard_map/ppermute | solution.py:303
  65.2 4.6 %copy-start.9 = (f32[128,8,256]{2,1,0:T(8,128)}, f32[128,8,256]{2,1,0:T(8,128)S(1)}, u32[]{:S(2)}) copy-start(f32[128,8,256]{2,1,0:T(8,128)S(1)} %collective-permute-done.7.refs_2_) | copy-start | bytes 3145732
  69.8 1.0 copy-start.10
  73.9 0.7 copy-start.16
  76.8 16.2 %collective-permute-start.8 = (f32[128,256]{1,0:T(8,128)}, f32[128,256]{1,0:T(8,128)S(1)}, u32[]{:S(2)}, u32[]{:S(2)}) collective-permute-start(f32[128,256]{1,0:T(8,128)} %small.7.refs_4_.refs_0_), channel_id=1, source_target_pairs={{0,16},{2,18},{4,20},{6,22},{8,24},{10,26},{12,28},{14,30},{16,0},... | collective-permute-start | bytes 393224 | tf_op jit(solution)/shard_map/ppermute | solution.py:303
  88.4 47.5 %collective-permute-start.14 = (f32[256,8,256]{2,1,0:T(8,128)}, f32[256,8,256]{2,1,0:T(8,128)}, u32[]{:S(2)}, u32[]{:S(2)}) collective-permute-start(f32[256,8,256]{2,1,0:T(8,128)} %get-tuple-element.12.refs_2_.refs_0_), channel_id=1, source_target_pairs={{0,30},{2,0},{4,2},{6,4},{8,6},{10,8},{12,10},{14,12},{16,14},{18,... | collective-permute-start | bytes 6291464 | tf_op jit(solution)/shard_map/ppermute | solution.py:21
  90.9 45.0 %collective-permute-start.13 = (f32[256,8,256]{2,1,0:T(8,128)}, f32[256,8,256]{2,1,0:T(8,128)}, u32[]{:S(2)}, u32[]{:S(2)}) collective-permute-start(f32[256,8,256]{2,1,0:T(8,128)} %get-tuple-element.12.refs_2_.refs_0_), channel_id=1, source_target_pairs={{0,2},{2,4},{4,6},{6,8},{8,10},{10,12},{12,14},{14,16},{16,18},{18... | collective-permute-start | bytes 6291464 | tf_op jit(solution)/shard_map/ppermute | solution.py:21
  93.0 0.7 copy-start.13
  99.1 70.8 %collective-permute-start.15 = (f32[256,8,256]{2,1,0:T(8,128)}, f32[256,8,256]{2,1,0:T(8,128)}, u32[]{:S(2)}, u32[]{:S(2)}) collective-permute-start(f32[256,8,256]{2,1,0:T(8,128)} %copy.28.refs_5_), channel_id=1, source_target_pairs={{0,1},{1,0},{2,3},{3,2},{4,5},{5,4},{6,7},{7,6},{8,9},{9,8},{10,11... | collective-permute-start | bytes 6291464 | tf_op jit(solution)/shard_map/ppermute | solution.py:21
  133.3 45.7 %collective-permute-start.12 = (f32[256,8,256]{2,1,0:T(8,128)}, f32[256,8,256]{2,1,0:T(8,128)S(1)}, u32[]{:S(2)}, u32[]{:S(2)}) collective-permute-start(f32[256,8,256]{2,1,0:T(8,128)} %get-tuple-element.14.refs_4_.refs_0_), channel_id=1, source_target_pairs={{0,30},{2,0},{4,2},{6,4},{8,6},{10,8},{12,10},{14,12},{16,14},{18,... | collective-permute-start | bytes 6291464 | tf_op jit(solution)/shard_map/ppermute | solution.py:21
  135.8 43.2 %collective-permute-start.11 = (f32[256,8,256]{2,1,0:T(8,128)}, f32[256,8,256]{2,1,0:T(8,128)}, u32[]{:S(2)}, u32[]{:S(2)}) collective-permute-start(f32[256,8,256]{2,1,0:T(8,128)} %get-tuple-element.14.refs_4_.refs_0_), channel_id=1, source_target_pairs={{0,2},{2,4},{4,6},{6,8},{8,10},{10,12},{12,14},{14,16},{16,18},{18... | collective-permute-start | bytes 6291464 | tf_op jit(solution)/shard_map/ppermute | solution.py:21
  142.0 74.8 %collective-permute-start.17 = (f32[256,8,256]{2,1,0:T(8,128)}, f32[256,8,256]{2,1,0:T(8,128)}, u32[]{:S(2)}, u32[]{:S(2)}) collective-permute-start(f32[256,8,256]{2,1,0:T(8,128)} %copy.29.refs_5_), channel_id=1, source_target_pairs={{0,1},{1,0},{2,3},{3,2},{4,5},{5,4},{6,7},{7,6},{8,9},{9,8},{10,11... | collective-permute-start | bytes 6291464 | tf_op jit(solution)/shard_map/ppermute | solution.py:21
  176.5 36.2 %collective-permute-start.19 = (f32[128,8,256]{2,1,0:T(8,128)}, f32[128,8,256]{2,1,0:T(8,128)S(1)}, u32[]{:S(2)}, u32[]{:S(2)}) collective-permute-start(f32[128,8,256]{2,1,0:T(8,128)} %get-tuple-element.16.refs_4_.refs_0_), channel_id=1, source_target_pairs={{0,30},{2,0},{4,2},{6,4},{8,6},{10,8},{12,10},{14,12},{16,14},{18,... | collective-permute-start | bytes 3145736 | tf_op jit(solution)/shard_map/ppermute | solution.py:21
  179.0 33.7 %collective-permute-start.18 = (f32[128,8,256]{2,1,0:T(8,128)}, f32[128,8,256]{2,1,0:T(8,128)}, u32[]{:S(2)}, u32[]{:S(2)}) collective-permute-start(f32[128,8,256]{2,1,0:T(8,128)} %get-tuple-element.16.refs_4_.refs_0_), channel_id=1, source_target_pairs={{0,2},{2,4},{4,6},{6,8},{8,10},{10,12},{12,14},{14,16},{16,18},{18... | collective-permute-start | bytes 3145736 | tf_op jit(solution)/shard_map/ppermute | solution.py:21
  179.0 1.4 copy-start
  185.7 24.0 %collective-permute-start.16 = (f32[128,256]{1,0:T(8,128)}, f32[128,256]{1,0:T(8,128)S(1)}, u32[]{:S(2)}, u32[]{:S(2)}) collective-permute-start(f32[128,256]{1,0:T(8,128)} %small.9.refs_2_.refs_0_), channel_id=1, source_target_pairs={{0,2},{2,0},{4,6},{6,4},{8,10},{10,8},{12,14},{14,12},{16,18},{18,... | collective-permute-start | bytes 393224 | tf_op jit(solution)/shard_map/ppermute | solution.py:303
  208.2 32.6 %collective-permute-start.22 = (f32[128,8,256]{2,1,0:T(8,128)}, f32[128,8,256]{2,1,0:T(8,128)}, u32[]{:S(2)}, u32[]{:S(2)}) collective-permute-start(f32[128,8,256]{2,1,0:T(8,128)} %core_send.3.refs_2_), channel_id=1, source_target_pairs={{0,1},{1,0},{2,3},{3,2},{4,5},{5,4},{6,7},{7,6},{8,9},{9,8},{10,11... | collective-permute-start | bytes 3145736 | tf_op jit(solution)/shard_map/ppermute | solution.py:21
  209.7 0.7 copy-start.5
  212.7 1.0 copy-start.3
  221.8 27.3 %collective-permute-start.21 = (f32[128,8,256]{2,1,0:T(8,128)}, f32[128,8,256]{2,1,0:T(8,128)S(1)}, u32[]{:S(2)}, u32[]{:S(2)}) collective-permute-start(f32[128,8,256]{2,1,0:T(8,128)} %core.1.refs_3_.refs_0_), channel_id=1, source_target_pairs={{0,30},{2,0},{4,2},{6,4},{8,6},{10,8},{12,10},{14,12},{16,14},{18,... | collective-permute-start | bytes 3145736 | tf_op jit(solution)/shard_map/ppermute | solution.py:21
  222.4 27.4 %collective-permute-start.20 = (f32[128,8,256]{2,1,0:T(8,128)}, f32[128,8,256]{2,1,0:T(8,128)S(1)}, u32[]{:S(2)}, u32[]{:S(2)}) collective-permute-start(f32[128,8,256]{2,1,0:T(8,128)} %core.1.refs_3_.refs_0_), channel_id=1, source_target_pairs={{0,2},{2,4},{4,6},{6,8},{8,10},{10,12},{12,14},{14,16},{16,18},{18... | collective-permute-start | bytes 3145736 | tf_op jit(solution)/shard_map/ppermute | solution.py:21
  227.0 27.2 %all-to-all-start = ((f32[32,8,256]{2,1,0:T(8,128)}), f32[32,8,256]{2,1,0:T(8,128)S(1)}, u32[]{:S(2)}, u32[]{:S(2)}) async-start(f32[32,8,256]{2,1,0:T(8,128)} %bitcast.5), calls=%async_computation | async-start | bytes 524288 | tf_op jit(solution)/shard_map/all_to_all | solution.py:375
  235.9 36.4 %collective-permute-start.26 = (f32[128,8,256]{2,1,0:T(8,128)}, f32[128,8,256]{2,1,0:T(8,128)S(1)}, u32[]{:S(2)}, u32[]{:S(2)}) collective-permute-start(f32[128,8,256]{2,1,0:T(8,128)} %place.12.refs_3_), channel_id=1, source_target_pairs={{0,1},{1,0},{2,3},{3,2},{4,5},{5,4},{6,7},{7,6},{8,9},{9,8},{10,11... | collective-permute-start | bytes 3145736 | tf_op jit(solution)/shard_map/ppermute | solution.py:21
  244.8 31.2 %collective-permute-start.25 = (f32[128,8,256]{2,1,0:T(8,128)}, f32[128,8,256]{2,1,0:T(8,128)}, u32[]{:S(2)}, u32[]{:S(2)}) collective-permute-start(f32[128,8,256]{2,1,0:T(8,128)} %core_finish.3.refs_4_.refs_0_), channel_id=1, source_target_pairs={{0,30},{2,0},{4,2},{6,4},{8,6},{10,8},{12,10},{14,12},{16,14},{18,... | collective-permute-start | bytes 3145736 | tf_op jit(solution)/shard_map/ppermute | solution.py:21
  249.2 26.8 %collective-permute-start.24 = (f32[128,8,256]{2,1,0:T(8,128)}, f32[128,8,256]{2,1,0:T(8,128)}, u32[]{:S(2)}, u32[]{:S(2)}) collective-permute-start(f32[128,8,256]{2,1,0:T(8,128)} %core_finish.3.refs_4_.refs_0_), channel_id=1, source_target_pairs={{0,2},{2,4},{4,6},{6,8},{8,10},{10,12},{12,14},{14,16},{16,18},{18... | collective-permute-start | bytes 3145736 | tf_op jit(solution)/shard_map/ppermute | solution.py:21
  249.2 1.0 copy-start.1
  249.2 39.5 %collective-permute-start.23 = (f32[128,8,256]{2,1,0:T(8,128)}, f32[128,8,256]{2,1,0:T(8,128)}, u32[]{:S(2)}, u32[]{:S(2)}) collective-permute-start(f32[128,8,256]{2,1,0:T(8,128)} %place.13.refs_3_), channel_id=1, source_target_pairs={{0,1},{1,0},{2,3},{3,2},{4,5},{5,4},{6,7},{7,6},{8,9},{9,8},{10,11... | collective-permute-start | bytes 3145736 | tf_op jit(solution)/shard_map/ppermute | solution.py:21
  250.1 1.0 copy-start.2
  254.2 0.7 copy-start.4
  257.3 34.1 %all-to-all-start.1 = ((f32[32,8,256]{2,1,0:T(8,128)}), f32[32,8,256]{2,1,0:T(8,128)}, u32[]{:S(2)}, u32[]{:S(2)}) async-start(f32[32,8,256]{2,1,0:T(8,128)} %sum.1.refs_2_), calls=%async_computation.1 | async-start | bytes 524288 | tf_op jit(solution)/shard_map/all_to_all | solution.py:381
  272.3 1.0 copy-start.8

commit v3 on v2

--- a/solution.py
+++ b/solution.py
@@ -12,7 +12,7 @@
 TILE = 8
 VMEM_LIMIT = 60 * 1024 * 1024
 HEAVY = 3 * 10**10
-WEIGHTS = {15: 0.3, 16: 0.3, 19: 0, 21: 0, 22: 0, 26: 0, 28: 0.1, 29: 0.1, 30: 3, 31: 3, 32: 3}
+WEIGHTS = {15: 0.3, 16: 0.3, 18: 0.2, 19: 0, 20: 0.2, 21: 0, 22: 0, 26: 0, 28: 0.1, 29: 0.1, 30: 3, 31: 3, 32: 3}
 MINE, THEIRS, CORE, SOURCE, SLOT = 0, 1, 2, 3, 3 + BLOCKS_DEV
 
 
@@ -211,20 +211,6 @@
     out_ref[...] = jnp.broadcast_to(total[None], out_ref.shape)
 
 
-def gram_kernel(index_ref, diagonal_ref, cross_ref, out_ref):
-    z = cross_ref.shape[0]
-
-    @pl.when(index_ref[MINE] == 0)
-    def _():
-        out_ref[:, :z] = diagonal_ref[...]
-        out_ref[:, z:] = cross_ref[...]
-
-    @pl.when(index_ref[MINE] == 1)
-    def _():
-        out_ref[:, :z] = cross_ref[...].T
-        out_ref[:, z:] = diagonal_ref[...]
-
-
 def place_kernel(index_ref, here_ref, lower_ref, upper_ref, *rest):
     out_ref = rest[-1]
     source = index_ref[SOURCE + pl.program_id(0)]
@@ -253,6 +239,37 @@
         in_sems,
         out_sems,
     )
+
+
+def last_kernel(
+    i, index_ref, part_ref, diagonal_ref, cross_ref, old_ref, core_ref, gram_ref, *scratch
+):
+    stage_ref, in_sems, out_sems, diagonal_stage, cross_stage, gram_sems = scratch
+    z = cross_ref.shape[0]
+    mine = index_ref[MINE]
+    blocks = [pl.ds(pl.multiple_of(at * z, z), z) for at in (mine, 1 - mine)]
+    loads = [
+        pltpu.make_async_copy(diagonal_ref, diagonal_stage, gram_sems.at[0]),
+        pltpu.make_async_copy(cross_ref, cross_stage, gram_sems.at[1]),
+    ]
+    stores = [
+        pltpu.make_async_copy(diagonal_stage, gram_ref.at[:, blocks[0]], gram_sems.at[2]),
+        pltpu.make_async_copy(cross_stage, gram_ref.at[:, blocks[1]], gram_sems.at[3]),
+    ]
+    for load in loads:
+        load.start()
+    put_kernel(i, index_ref, part_ref, old_ref, core_ref, stage_ref, in_sems, out_sems)
+    loads[0].wait()
+    stores[0].start()
+    loads[1].wait()
+
+    @pl.when(mine == 1)
+    def _():
+        cross_stage[...] = cross_stage[...].T
+
+    stores[1].start()
+    for store in stores:
+        store.wait()
 
 
 def join_kernel(axis, index_ref, keep_ref, other_ref, out_ref):
@@ -288,7 +305,6 @@
     any_space = pl.BlockSpec(memory_space=pl.ANY)
     whole_factor = whole(factor.shape)
     slabs = 4
-    late = (2, 3)
 
     def staging(rows):
         return [pltpu.VMEM((rows, TILE, points), jnp.float32)] + [pltpu.SemaphoreType.DMA((slabs,))] * 2
@@ -311,13 +327,11 @@
     def send_factor():
         out = ((z, rank), whole((z, rank)))
         half = steps.call(copy_kernel, "copy", (1,), [(factor, ranks(z, rank, CORE))], [out], index=places)[0]
-        half = over_gz(half)
-        return half, exchanged(half, 1)
-
-    def core_send(i):
+        return over_gz(half)
+
+    def core_send(i, index=None):
         inputs = [(factor, ranks(z, rank, THEIRS)), (field, field_chunk(z, chunks, MINE, i))]
         out = ((rank, TILE, points), core_chunk(rank))
-        index = places if i == late[0] else None
         return steps.call(core_part_kernel, "core_send", (columns,), inputs, [out], index=index)[0]
 
     def core_finish(i, arrived):
@@ -401,15 +415,16 @@
 
     fields, ready, arrived = {}, {}, {}
     own_ranks = ranks(z, rank, MINE)
-    arrived[2] = over_gz(core_send(2))
-    cross_half = send_factor()
+    arrived[2] = over_gz(core_send(2, places))
+    factor_half = send_factor()
+    other_half = exchanged(factor_half, 1)
     fields[0] = send_field(0)
     diagonal, half = diagonal_gram()
     half = exchanged(half, 1)
     fields[1] = send_field(1)
     diagonal = small(add_kernel, diagonal, half)
     half = exchanged(diagonal, 2)
-    cross_factor = joined(1, *cross_half)
+    cross_factor = joined(1, factor_half, other_half)
     late2 = neighbours(core_finish(2, arrived[2]))
     diagonal = small(add_kernel, diagonal, half)
     half = exchanged(diagonal, 4)
@@ -441,9 +456,11 @@
     cross = summed(cross, ("xy", "gz"))
     core = put(arrived[0], core, 0)
     core = place(late3, None, core, THEIRS, 3)
-    core = put(arrived[1], core, 1)
-    gram_specs = [(diagonal, whole((z, z))), (cross, whole((z, z)))]
-    gram = steps.call(gram_kernel, "gram", (1,), gram_specs, [((z, 2 * z), whole((z, 2 * z)))])[0]
+    inputs = [(array, any_space) for array in (arrived[1], diagonal, cross, core)]
+    outputs = [((rank, count, points), any_space), ((z, 2 * z), any_space)]
+    scratch = staging(rank) + [pltpu.VMEM((z, z), jnp.float32)] * 2 + [pltpu.SemaphoreType.DMA((4,))]
+    kernel = functools.partial(last_kernel, 1)
+    core, gram = steps.call(kernel, "last", (1,), inputs, outputs, {3: 0}, scratch)
     return (gram, core)
 
 

time: 295 us -> 294 us (level)
    pallas_call x34 -> x33, Pallas kernels: 130 us -> 131 us  [call(): pl.pallas_call(body, out_shape=[jax.ShapeDtypeStruct(shape, jnp.float32)...]
  transfers between devices with their start and end apart: 29 -> 29, of which waited for: 6 -> 7; matrix products, arithmetic and copies ran while one was open for 0% -> 0% of each run, Pallas kernels for 42% -> 42%
where the time goes in v3:
time: 294 us; the launch traced here: 293 us
  Pallas kernels  131 us (45%)
  waiting for transfers between devices  78.7 us (27%)
  starting transfers between devices  69.9 us (24%)
  local copies, waits for them, and re-layouts  11.1 us (4%)
    pallas_call x33, Pallas kernels, call(): pl.pallas_call(body, out_shape=[jax.ShapeDtypeStruct(shape, jnp.float32)...  131 us
    ppermute x21, waiting for transfers between devices, shifted(): lax.ppermute(array, axis, [(i, (i + by) % length) for i in range(length)])  78.5 us
    ppermute x21, starting transfers between devices, shifted(): lax.ppermute(array, axis, [(i, (i + by) % length) for i in range(length)])  28.4 us
    ppermute x6, starting transfers between devices, exchanged(): lax.ppermute(part, 'xy', [(i, i ^ bit) for i in range(lax.axis_size('xy'))])  20.2 us
    all_to_all x1, starting transfers between devices, summed(): lax.all_to_all(total, axes, split_axis=0, concat_axis=0, tiled=True)  15.3 us
    unnamed x34, local copies, waits for them, and re-layouts  10.4 us
  transfers between devices with their start and end apart: 29, of which 7 were waited for; matrix products, arithmetic and copies ran while one was open for 0% of the time, Pallas kernels for 42%

profile of v3, /device:TPU:0, one launch (start us, length us, event | category | flops | bytes accessed | tf_op | source)
XLA Modules:
  0.0 292.6 jit_solution(8806526397434260926)
XLA Ops:
  1.2 3.8 %core_send.2.refs_1_ = f32[128,8,256]{2,1,0:T(8,128)} custom-call(s32[3]{0:T(128)} %pad_add_fusion.index_ref, f32[256,256]{1,0:T(8,128)} %refs_0_.29, f32[256,64,256]{2,1,0:T(8,128)} %refs_1_.7), custom_call_target="tpu_custom_call" | custom-call | flops 30000001024 | tf_op jit(solution)/shard_map/core_send/pallas_call | solution.py:70
  5.0 3.0 %collective-permute-start.6 = (f32[128,8,256]{2,1,0:T(8,128)}, f32[128,8,256]{2,1,0:T(8,128)}, u32[]{:S(2)}, u32[]{:S(2)}) collective-permute-start(f32[128,8,256]{2,1,0:T(8,128)} %core_send.2.refs_1_), channel_id=1, source_target_pairs={{0,1},{1,0},{2,3},{3,2},{4,5},{5,4},{6,7},{7,6},{8,9},{9,8},{10,11... | collective-permute-start | bytes 3145736 | tf_op jit(solution)/shard_map/ppermute | solution.py:21
  8.0 2.2 copy.25.refs_1_
  10.2 3.2 %copy.26.refs_1_ = f32[256,8,256]{2,1,0:T(8,128)} custom-call(s32[3]{0:T(128)} %pad_add_fusion.index_ref, f32[256,64,256]{2,1,0:T(8,128)} %refs_1_.7, f32[256,128]{1,0:T(8,128)} %copy.25.refs_1_), custom_call_target="tpu_custom_call" | custom-call | flops 30000001024 | tf_op jit(solution)/shard_map/copy/pallas_call | solution.py:70
  16.2 16.5 %diagonal.1 = (f32[128,256]{1,0:T(8,128)}, f32[128,256]{1,0:T(8,128)}) custom-call(s32[7]{0:T(128)} %concatenate.4.index_ref, f32[256,64,256]{2,1,0:T(8,128)} %refs_1_.7, f32[256,8,256]{2,1,0:T(8,128)} %copy.26.refs_1_), custom_call_target="tpu_custom_call" | custom-call | flops 30000001024 | tf_op jit(solution)/shard_map/diagonal/pallas_call | solution.py:70
  32.6 3.1 %copy.27.refs_2_ = f32[256,8,256]{2,1,0:T(8,128)} custom-call(s32[7]{0:T(128)} %concatenate.4.index_ref, f32[256,64,256]{2,1,0:T(8,128)} %refs_1_.7, f32[128,256]{1,0:T(8,128)} %get-tuple-element.12.refs_1_.refs_0_), custom_call_target="tpu_custom_call" | custom-call | flops 30000001024 | tf_op jit(solution)/shard_map/copy/pallas_call | solution.py:70
  37.1 2.3 small.5.refs_2_.refs_0_
  41.7 2.4 join.2.refs_3_.refs_1_
  44.0 4.0 %core_finish.2.refs_2_.refs_0_ = f32[128,8,256]{2,1,0:T(8,128)} custom-call(s32[7]{0:T(128)} %concatenate.4.index_ref, f32[256,256]{1,0:T(8,128)} %refs_0_.29, f32[256,64,256]{2,1,0:T(8,128)} %refs_1_.7, f32[128,8,256]{2,1,0:T(8,128)} %collective-permute-done.6.refs_2_, f32[256,256]{1,0:T(8,128)} %join.2.refs_3_.refs_1_), custom_call_target="tpu_custom_call" | custom-call | flops 30000001024 | tf_op jit(solution)/shard_map/core_finish/pallas_call | solution.py:70
  48.0 3.2 %collective-permute-start.9 = (f32[128,8,256]{2,1,0:T(8,128)}, f32[128,8,256]{2,1,0:T(8,128)S(1)}, u32[]{:S(2)}, u32[]{:S(2)}) collective-permute-start(f32[128,8,256]{2,1,0:T(8,128)} %core_finish.2.refs_2_.refs_0_), channel_id=1, source_target_pairs={{0,30},{2,0},{4,2},{6,4},{8,6},{10,8},{12,10},{14,12},{16,14},{18,... | collective-permute-start | bytes 3145736 | tf_op jit(solution)/shard_map/ppermute | solution.py:21
  51.9 2.3 small.6.refs_3_.refs_0_
  54.2 11.1 %collective-permute-done.9.refs_2_ = f32[128,8,256]{2,1,0:T(8,128)S(1)} collective-permute-done((f32[128,8,256]{2,1,0:T(8,128)}, f32[128,8,256]{2,1,0:T(8,128)S(1)}, u32[]{:S(2)}, u32[]{:S(2)}) %collective-permute-start.9) | collective-permute-done | bytes 1048608 | tf_op jit(solution)/shard_map/ppermute | solution.py:21
  65.2 4.6 %collective-permute-done.8.refs_1_ = f32[128,8,256]{2,1,0:T(8,128)S(1)} collective-permute-done((f32[128,8,256]{2,1,0:T(8,128)}, f32[128,8,256]{2,1,0:T(8,128)S(1)}, u32[]{:S(2)}, u32[]{:S(2)}) %collective-permute-start.8) | collective-permute-done | bytes 1048608 | tf_op jit(solution)/shard_map/ppermute | solution.py:21
  70.9 3.4 %place.8.refs_2_.refs_3_ = f32[128,64,256]{2,1,0:T(8,128)} custom-call(s32[7]{0:T(128)} %concatenate.4.index_ref, f32[128,8,256]{2,1,0:T(8,128)} %core_finish.2.refs_2_.refs_0_, f32[128,8,256]{2,1,0:T(8,128)} %copy-done.10, f32[128,8,256]{2,1,0:T(8,128)} %copy-done.9, f32[128,256]{1,0:T(8,128)} %small.6.refs_3_.refs_0_), custom_call_target="tpu_custom_call" | custom-call | flops 30000001024 | tf_op jit(solution)/shard_map/place/pallas_call | solution.py:70
  74.9 2.3 small.7.refs_4_.refs_0_
  77.2 2.8 collective-permute-done.4.refs_3_
  80.0 8.3 %received.3 = (f32[256,8,256]{2,1,0:T(8,128)}, f32[256,256]{1,0:T(8,128)}) custom-call(s32[7]{0:T(128)} %concatenate.4.index_ref, f32[256,256]{1,0:T(8,128)} %refs_0_.29, f32[256,256]{1,0:T(8,128)} %join.2.refs_3_.refs_1_, f32[256,64,256]{2,1,0:T(8,128)} %refs_1_.7, f32[256,8,256]{2,1,0:T(8,128)} %collective-permute-done.4.refs_3_, ...), custom_call_target="tpu_custom_call" | custom-call | flops 30000001024 | tf_op jit(solution)/shard_map/received/pallas_call | solution.py:70
  88.3 2.5 collective-permute-start.14
  93.4 2.3 small.8.refs_1_.refs_0_
  95.7 3.1 %copy.28.refs_5_ = f32[256,8,256]{2,1,0:T(8,128)} custom-call(s32[7]{0:T(128)} %concatenate.4.index_ref, f32[256,64,256]{2,1,0:T(8,128)} %refs_1_.7, f32[128,256]{1,0:T(8,128)} %small.8.refs_1_.refs_0_), custom_call_target="tpu_custom_call" | custom-call | flops 30000001024 | tf_op jit(solution)/shard_map/copy/pallas_call | solution.py:70
  100.4 24.6 %collective-permute-done.3.refs_3_ = f32[256,8,256]{2,1,0:T(8,128)} collective-permute-done((f32[256,8,256]{2,1,0:T(8,128)}, f32[256,8,256]{2,1,0:T(8,128)}, u32[]{:S(2)}, u32[]{:S(2)}) %collective-permute-start.3) | collective-permute-done | bytes 2097184 | tf_op jit(solution)/shard_map/ppermute | solution.py:21
  124.9 8.3 %received.4 = (f32[256,8,256]{2,1,0:T(8,128)}, f32[256,256]{1,0:T(8,128)}) custom-call(s32[7]{0:T(128)} %concatenate.4.index_ref, f32[256,256]{1,0:T(8,128)} %refs_0_.29, f32[256,256]{1,0:T(8,128)} %join.2.refs_3_.refs_1_, f32[256,64,256]{2,1,0:T(8,128)} %refs_1_.7, f32[256,8,256]{2,1,0:T(8,128)} %collective-permute-done.3.refs_3_, ...), custom_call_target="tpu_custom_call" | custom-call | flops 30000001024 | tf_op jit(solution)/shard_map/received/pallas_call | solution.py:70
  133.3 2.5 collective-permute-start.12
  135.8 3.4 %place.9.refs_1_.refs_3_ = f32[128,64,256]{2,1,0:T(8,128)} custom-call(s32[7]{0:T(128)} %concatenate.4.index_ref, f32[256,8,256]{2,1,0:T(8,128)} %get-tuple-element.15.refs_2_.refs_0_, f32[256,8,256]{2,1,0:T(8,128)} %collective-permute-done.13.refs_1_, f32[256,8,256]{2,1,0:T(8,128)} %collective-permute-done.14.refs_2_, ...), custom_call_target="tpu_custom_call", output_to_operand_aliasing={{}: (4, {})} | custom-call | flops 8999999488 | tf_op jit(solution)/shard_map/place/pallas_call | solution.py:70
  139.2 3.1 %copy.29.refs_5_ = f32[256,8,256]{2,1,0:T(8,128)} custom-call(s32[7]{0:T(128)} %concatenate.4.index_ref, f32[256,64,256]{2,1,0:T(8,128)} %refs_1_.7, f32[128,64,256]{2,1,0:T(8,128)} %place.9.refs_1_.refs_3_), custom_call_target="tpu_custom_call" | custom-call | flops 8999999488 | tf_op jit(solution)/shard_map/copy/pallas_call | solution.py:70
  143.8 26.1 %collective-permute-done.16.refs_3_ = f32[256,8,256]{2,1,0:T(8,128)} collective-permute-done((f32[256,8,256]{2,1,0:T(8,128)}, f32[256,8,256]{2,1,0:T(8,128)}, u32[]{:S(2)}, u32[]{:S(2)}) %collective-permute-start.16) | collective-permute-done | bytes 2097184 | tf_op jit(solution)/shard_map/ppermute | solution.py:21
  169.9 6.6 %received.5 = (f32[128,8,256]{2,1,0:T(8,128)}, f32[256,256]{1,0:T(8,128)}) custom-call(s32[7]{0:T(128)} %concatenate.4.index_ref, f32[256,256]{1,0:T(8,128)} %refs_0_.29, f32[256,256]{1,0:T(8,128)} %join.2.refs_3_.refs_1_, f32[256,64,256]{2,1,0:T(8,128)} %refs_1_.7, f32[256,8,256]{2,1,0:T(8,128)} %collective-permute-done.16.refs_3_, ...), custom_call_target="tpu_custom_call" | custom-call | flops 30000001024 | tf_op jit(solution)/shard_map/received/pallas_call | solution.py:70
  176.4 2.5 collective-permute-start.18
  180.4 3.4 %place.10.refs_1_.refs_3_ = f32[128,64,256]{2,1,0:T(8,128)} custom-call(s32[7]{0:T(128)} %concatenate.4.index_ref, f32[256,8,256]{2,1,0:T(8,128)} %get-tuple-element.16.refs_4_.refs_0_, f32[256,8,256]{2,1,0:T(8,128)} %collective-permute-done.11.refs_1_, f32[256,8,256]{2,1,0:T(8,128)} %copy-done, ...), custom_call_target="tpu_custom_call", output_to_operand_aliasing={{}: (4, {})} | custom-call | flops 6000000000 | tf_op jit(solution)/shard_map/place/pallas_call | solution.py:70
  183.7 2.2 small.9.refs_2_.refs_0_
  186.0 18.1 %collective-permute-start.19 = (f32[128,256]{1,0:T(8,128)}, f32[128,256]{1,0:T(8,128)S(1)}, u32[]{:S(2)}, u32[]{:S(2)}) collective-permute-start(f32[128,256]{1,0:T(8,128)} %small.9.refs_2_.refs_0_), channel_id=1, source_target_pairs={{0,2},{2,0},{4,6},{6,4},{8,10},{10,8},{12,14},{14,12},{16,18},{18,... | collective-permute-start | bytes 393224 | tf_op jit(solution)/shard_map/ppermute | solution.py:319
  204.1 3.8 %core_send.3.refs_2_ = f32[128,8,256]{2,1,0:T(8,128)} custom-call(s32[7]{0:T(128)} %concatenate.4.index_ref, f32[256,256]{1,0:T(8,128)} %refs_0_.29, f32[256,64,256]{2,1,0:T(8,128)} %refs_1_.7, f32[128,256]{1,0:T(8,128)} %small.9.refs_2_.refs_0_), custom_call_target="tpu_custom_call" | custom-call | flops 6000000000 | tf_op jit(solution)/shard_map/core_send/pallas_call | solution.py:70
  210.1 2.3 join.3.refs_4_.refs_1_
  213.4 3.4 %place.11.refs_4_.refs_3_ = f32[128,64,256]{2,1,0:T(8,128)} custom-call(s32[7]{0:T(128)} %concatenate.4.index_ref, f32[128,8,256]{2,1,0:T(8,128)} %get-tuple-element.19.refs_4_.refs_0_, f32[128,8,256]{2,1,0:T(8,128)} %collective-permute-done.17.refs_1_, f32[128,8,256]{2,1,0:T(8,128)} %copy-done.3, ...), custom_call_target="tpu_custom_call", output_to_operand_aliasing={{}: (4, {})} | custom-call | tf_op jit(solution)/shard_map/place/pallas_call | solution.py:70
  216.8 5.0 %core.1.refs_3_.refs_0_ = f32[128,8,256]{2,1,0:T(8,128)} custom-call(s32[7]{0:T(128)} %concatenate.4.index_ref, f32[256,256]{1,0:T(8,128)} %refs_0_.29, f32[256,256]{1,0:T(8,128)} %join.2.refs_3_.refs_1_, f32[256,64,256]{2,1,0:T(8,128)} %refs_1_.7, f32[256,8,256]{2,1,0:T(8,128)} %collective-permute-done.15.refs_3_.refs_1_, f32[128,64,256]{2,1,0:T(8,128)} %place.11.refs_4_.refs_3_), custom_call_target="tpu_custom_call" | custom-call | flops 30000001024 | tf_op jit(solution)/shard_map/core/pallas_call | solution.py:70
  222.4 4.6 %cross.1.refs_3_ = f32[256,256]{1,0:T(8,128)} custom-call(s32[7]{0:T(128)} %concatenate.4.index_ref, f32[256,64,256]{2,1,0:T(8,128)} %refs_1_.7, f32[256,8,256]{2,1,0:T(8,128)} %collective-permute-done.15.refs_3_.refs_1_, f32[256,256]{1,0:T(8,128)} %get-tuple-element.18.refs_2_, f32[128,8,256]{2,1,0:T(8,128)} %core.1.refs_3_.refs_0_), custom_call_target="tpu_custom_call" | custom-call | flops 30000001024 | tf_op jit(solution)/shard_map/cross/pallas_call | solution.py:70
  227.0 5.9 %all-to-all-start = ((f32[32,8,256]{2,1,0:T(8,128)}), f32[32,8,256]{2,1,0:T(8,128)S(1)}, u32[]{:S(2)}, u32[]{:S(2)}) async-start(f32[32,8,256]{2,1,0:T(8,128)} %bitcast.5), calls=%async_computation | async-start | bytes 524288 | tf_op jit(solution)/shard_map/all_to_all | solution.py:389
  232.8 3.4 %place.12.refs_3_ = f32[128,8,256]{2,1,0:T(8,128)} custom-call(s32[7]{0:T(128)} %concatenate.4.index_ref, f32[256,8,256]{2,1,0:T(8,128)} %get-tuple-element.15.refs_2_.refs_0_, f32[256,8,256]{2,1,0:T(8,128)} %collective-permute-done.13.refs_1_, f32[256,8,256]{2,1,0:T(8,128)} %collective-permute-done.14.refs_2_, f32[256,256]{1,0:T(8,128)} %cross.1.refs_3_), custom_call_target="tpu_custom_call" | custom-call | flops 30000001024 | tf_op jit(solution)/shard_map/place/pallas_call | solution.py:70
  238.0 3.4 %place.13.refs_3_ = f32[128,8,256]{2,1,0:T(8,128)} custom-call(s32[7]{0:T(128)} %concatenate.4.index_ref, f32[256,8,256]{2,1,0:T(8,128)} %get-tuple-element.16.refs_4_.refs_0_, f32[256,8,256]{2,1,0:T(8,128)} %collective-permute-done.11.refs_1_, f32[256,8,256]{2,1,0:T(8,128)} %copy-done, f32[128,8,256]{2,1,0:T(8,128)} %place.12.refs_3_), custom_call_target="tpu_custom_call" | custom-call | tf_op jit(solution)/shard_map/place/pallas_call | solution.py:70
  241.3 4.0 %core_finish.3.refs_4_.refs_0_ = f32[128,8,256]{2,1,0:T(8,128)} custom-call(s32[7]{0:T(128)} %concatenate.4.index_ref, f32[256,256]{1,0:T(8,128)} %refs_0_.29, f32[256,64,256]{2,1,0:T(8,128)} %refs_1_.7, f32[128,8,256]{2,1,0:T(8,128)} %collective-permute-done.23.refs_2_, f32[128,8,256]{2,1,0:T(8,128)} %place.13.refs_3_), custom_call_target="tpu_custom_call" | custom-call | flops 30000001024 | tf_op jit(solution)/shard_map/core_finish/pallas_call | solution.py:70
  245.4 3.1 %collective-permute-start.25 = (f32[128,8,256]{2,1,0:T(8,128)}, f32[128,8,256]{2,1,0:T(8,128)}, u32[]{:S(2)}, u32[]{:S(2)}) collective-permute-start(f32[128,8,256]{2,1,0:T(8,128)} %core_finish.3.refs_4_.refs_0_), channel_id=1, source_target_pairs={{0,30},{2,0},{4,2},{6,4},{8,6},{10,8},{12,10},{14,12},{16,14},{18,... | collective-permute-start | bytes 3145736 | tf_op jit(solution)/shard_map/ppermute | solution.py:21
  250.5 3.4 %place.14.refs_1_ = f32[128,64,256]{2,1,0:T(8,128)} custom-call(s32[7]{0:T(128)} %concatenate.4.index_ref, f32[128,8,256]{2,1,0:T(8,128)} %core.1.refs_3_.refs_0_, f32[128,8,256]{2,1,0:T(8,128)} %copy-done.2, f32[128,8,256]{2,1,0:T(8,128)} %copy-done.1, f32[128,64,256]{2,1,0:T(8,128)} %place.11.refs_4_.refs_3_, ...), custom_call_target="tpu_custom_call", output_to_operand_aliasing={{}: (4, {})} | custom-call | flops 3000000000 | tf_op jit(solution)/shard_map/place/pallas_call | solution.py:70
  254.6 2.4 sum.1.refs_2_
  256.9 15.3 %all-to-all-start.1 = ((f32[32,8,256]{2,1,0:T(8,128)}), f32[32,8,256]{2,1,0:T(8,128)}, u32[]{:S(2)}, u32[]{:S(2)}) async-start(f32[32,8,256]{2,1,0:T(8,128)} %sum.1.refs_2_), calls=%async_computation.1 | async-start | bytes 524288 | tf_op jit(solution)/shard_map/all_to_all | solution.py:395
  273.3 2.6 put.1.refs_3_
  275.9 3.4 %place.15.refs_3_ = f32[128,64,256]{2,1,0:T(8,128)} custom-call(s32[7]{0:T(128)} %concatenate.4.index_ref, f32[128,8,256]{2,1,0:T(8,128)} %core_finish.3.refs_4_.refs_0_, f32[128,8,256]{2,1,0:T(8,128)} %collective-permute-done.24.refs_1_, f32[128,8,256]{2,1,0:T(8,128)} %collective-permute-done.25.refs_2_, ...), custom_call_target="tpu_custom_call", output_to_operand_aliasing={{}: (4, {})} | custom-call | flops 89999998976 | tf_op jit(solution)/shard_map/place/pallas_call | solution.py:70
  279.3 9.3 %collective-permute-done.20.refs_0_ = f32[128,8,256]{2,1,0:T(8,128)} collective-permute-done((f32[128,8,256]{2,1,0:T(8,128)}, f32[128,8,256]{2,1,0:T(8,128)}, u32[]{:S(2)}, u32[]{:S(2)}) %collective-permute-start.20) | collective-permute-done | bytes 1048608 | tf_op jit(solution)/shard_map/ppermute | solution.py:21
  288.8 3.6 %last.1 = (f32[128,64,256]{2,1,0:T(8,128)}, f32[256,512]{1,0:T(8,128)}) custom-call(s32[7]{0:T(128)} %concatenate.4.index_ref, f32[128,8,256]{2,1,0:T(8,128)} %collective-permute-done.20.refs_0_, f32[256,256]{1,0:T(8,128)} %join.3.refs_4_.refs_1_, f32[256,256]{1,0:T(8,128)} %bitcast.4.refs_2_, ...), custom_call_target="tpu_custom_call", output_to_operand_aliasing={{0}: (4, {})} | custom-call | flops 89999998976 | tf_op jit(solution)/shard_map/last/pallas_call | solution.py:70
  (80 shorter events, 25.7 us)
Async XLA Ops:
  5.0 39.0 %collective-permute-start.6 = (f32[128,8,256]{2,1,0:T(8,128)}, f32[128,8,256]{2,1,0:T(8,128)}, u32[]{:S(2)}, u32[]{:S(2)}) collective-permute-start(f32[128,8,256]{2,1,0:T(8,128)} %core_send.2.refs_1_), channel_id=1, source_target_pairs={{0,1},{1,0},{2,3},{3,2},{4,5},{5,4},{6,7},{7,6},{8,9},{9,8},{10,11... | collective-permute-start | bytes 3145736 | tf_op jit(solution)/shard_map/ppermute | solution.py:21
  10.2 5.2 %copy-start.6 = (s32[32]{0:T(128)S(1)}, s32[32]{0:T(128)}, u32[]{:S(2)}) copy-start(s32[32]{0:T(128)} %param.7) | copy-start | bytes 388
  10.2 5.2 %copy-start.7 = (s32[32]{0:T(128)S(1)}, s32[32]{0:T(128)}, u32[]{:S(2)}) copy-start(s32[32]{0:T(128)} %param.6) | copy-start | bytes 388
  10.2 25.8 %collective-permute-start = (f32[256,128]{1,0:T(8,128)}, f32[256,128]{1,0:T(8,128)S(1)}, u32[]{:S(2)}, u32[]{:S(2)}) collective-permute-start(f32[256,128]{1,0:T(8,128)} %copy.25.refs_1_), channel_id=1, source_target_pairs={{0,1},{1,0},{2,3},{3,2},{4,5},{5,4},{6,7},{7,6},{8,9},{9,8},{10,11... | collective-permute-start | bytes 393224 | tf_op jit(solution)/shard_map/ppermute | solution.py:21
  13.4 66.6 %collective-permute-start.4 = (f32[256,8,256]{2,1,0:T(8,128)}, f32[256,8,256]{2,1,0:T(8,128)}, u32[]{:S(2)}, u32[]{:S(2)}) collective-permute-start(f32[256,8,256]{2,1,0:T(8,128)} %copy.26.refs_1_), channel_id=1, source_target_pairs={{0,1},{1,0},{2,3},{3,2},{4,5},{5,4},{6,7},{7,6},{8,9},{9,8},{10,11... | collective-permute-start | bytes 6291464 | tf_op jit(solution)/shard_map/ppermute | solution.py:21
  32.6 3.8 %collective-permute-start.2 = (f32[128,256]{1,0:T(8,128)}, f32[128,256]{1,0:T(8,128)S(1)}, u32[]{:S(2)}, u32[]{:S(2)}) collective-permute-start(f32[128,256]{1,0:T(8,128)} %get-tuple-element.13), channel_id=1, source_target_pairs={{0,2},{2,0},{4,6},{6,4},{8,10},{10,8},{12,14},{14,12},{16,18},{18,... | collective-permute-start | bytes 393224 | tf_op jit(solution)/shard_map/ppermute | solution.py:319
  35.7 89.2 %collective-permute-start.3 = (f32[256,8,256]{2,1,0:T(8,128)}, f32[256,8,256]{2,1,0:T(8,128)}, u32[]{:S(2)}, u32[]{:S(2)}) collective-permute-start(f32[256,8,256]{2,1,0:T(8,128)} %copy.27.refs_2_), channel_id=1, source_target_pairs={{0,1},{1,0},{2,3},{3,2},{4,5},{5,4},{6,7},{7,6},{8,9},{9,8},{10,11... | collective-permute-start | bytes 6291464 | tf_op jit(solution)/shard_map/ppermute | solution.py:21
  36.0 3.4 %copy-start.11 = (f32[256,128]{1,0:T(8,128)}, f32[256,128]{1,0:T(8,128)S(1)}, u32[]{:S(2)}) copy-start(f32[256,128]{1,0:T(8,128)S(1)} %collective-permute-done.refs_0_) | copy-start | bytes 393220
  36.0 5.0 %collective-permute-start.1 = (f32[256,128]{1,0:T(8,128)S(1)}, f32[256,128]{1,0:T(8,128)S(1)}, u32[]{:S(2)}, u32[]{:S(2)}) collective-permute-start(f32[256,128]{1,0:T(8,128)S(1)} %collective-permute-done.refs_0_), channel_id=1, source_target_pairs={{0,2},{2,0},{4,6},{6,4},{8,10},{10,8},{12,14},{14,12},{16,18},{18,... | collective-permute-start | bytes 393224 | tf_op jit(solution)/shard_map/ppermute | solution.py:319
  36.4 0.7 copy-start.14
  39.4 11.8 %collective-permute-start.5 = (f32[128,256]{1,0:T(8,128)}, f32[128,256]{1,0:T(8,128)S(1)}, u32[]{:S(2)}, u32[]{:S(2)}) collective-permute-start(f32[128,256]{1,0:T(8,128)} %small.5.refs_2_.refs_0_), channel_id=1, source_target_pairs={{0,4},{2,6},{4,0},{6,2},{8,12},{10,14},{12,8},{14,10},{16,20},{18,... | collective-permute-start | bytes 393224 | tf_op jit(solution)/shard_map/ppermute | solution.py:319
  41.0 0.7 copy-start.15
  48.0 17.2 %collective-permute-start.9 = (f32[128,8,256]{2,1,0:T(8,128)}, f32[128,8,256]{2,1,0:T(8,128)S(1)}, u32[]{:S(2)}, u32[]{:S(2)}) collective-permute-start(f32[128,8,256]{2,1,0:T(8,128)} %core_finish.2.refs_2_.refs_0_), channel_id=1, source_target_pairs={{0,30},{2,0},{4,2},{6,4},{8,6},{10,8},{12,10},{14,12},{16,14},{18,... | collective-permute-start | bytes 3145736 | tf_op jit(solution)/shard_map/ppermute | solution.py:21
  51.2 18.6 %collective-permute-start.8 = (f32[128,8,256]{2,1,0:T(8,128)}, f32[128,8,256]{2,1,0:T(8,128)S(1)}, u32[]{:S(2)}, u32[]{:S(2)}) collective-permute-start(f32[128,8,256]{2,1,0:T(8,128)} %core_finish.2.refs_2_.refs_0_), channel_id=1, source_target_pairs={{0,2},{2,4},{4,6},{6,8},{8,10},{10,12},{12,14},{14,16},{16,18},{18... | collective-permute-start | bytes 3145736 | tf_op jit(solution)/shard_map/ppermute | solution.py:21
  51.2 0.7 copy-start.12
  54.2 20.0 %collective-permute-start.7 = (f32[128,256]{1,0:T(8,128)}, f32[128,256]{1,0:T(8,128)S(1)}, u32[]{:S(2)}, u32[]{:S(2)}) collective-permute-start(f32[128,256]{1,0:T(8,128)} %small.6.refs_3_.refs_0_), channel_id=1, source_target_pairs={{0,8},{2,10},{4,12},{6,14},{8,0},{10,2},{12,4},{14,6},{16,24},{18,... | collective-permute-start | bytes 393224 | tf_op jit(solution)/shard_map/ppermute | solution.py:319
  65.2 4.6 %copy-start.9 = (f32[128,8,256]{2,1,0:T(8,128)}, f32[128,8,256]{2,1,0:T(8,128)S(1)}, u32[]{:S(2)}) copy-start(f32[128,8,256]{2,1,0:T(8,128)S(1)} %collective-permute-done.9.refs_2_) | copy-start | bytes 3145732
  69.9 1.0 copy-start.10
  74.2 0.6 copy-start.16
  77.2 15.6 %collective-permute-start.10 = (f32[128,256]{1,0:T(8,128)}, f32[128,256]{1,0:T(8,128)S(1)}, u32[]{:S(2)}, u32[]{:S(2)}) collective-permute-start(f32[128,256]{1,0:T(8,128)} %small.7.refs_4_.refs_0_), channel_id=1, source_target_pairs={{0,16},{2,18},{4,20},{6,22},{8,24},{10,26},{12,28},{14,30},{16,0},... | collective-permute-start | bytes 393224 | tf_op jit(solution)/shard_map/ppermute | solution.py:319
  88.3 47.5 %collective-permute-start.14 = (f32[256,8,256]{2,1,0:T(8,128)}, f32[256,8,256]{2,1,0:T(8,128)}, u32[]{:S(2)}, u32[]{:S(2)}) collective-permute-start(f32[256,8,256]{2,1,0:T(8,128)} %get-tuple-element.15.refs_2_.refs_0_), channel_id=1, source_target_pairs={{0,30},{2,0},{4,2},{6,4},{8,6},{10,8},{12,10},{14,12},{16,14},{18,... | collective-permute-start | bytes 6291464 | tf_op jit(solution)/shard_map/ppermute | solution.py:21
  90.8 45.0 %collective-permute-start.13 = (f32[256,8,256]{2,1,0:T(8,128)}, f32[256,8,256]{2,1,0:T(8,128)}, u32[]{:S(2)}, u32[]{:S(2)}) collective-permute-start(f32[256,8,256]{2,1,0:T(8,128)} %get-tuple-element.15.refs_2_.refs_0_), channel_id=1, source_target_pairs={{0,2},{2,4},{4,6},{6,8},{8,10},{10,12},{12,14},{14,16},{16,18},{18... | collective-permute-start | bytes 6291464 | tf_op jit(solution)/shard_map/ppermute | solution.py:21
  92.7 0.6 copy-start.13
  98.8 71.1 %collective-permute-start.16 = (f32[256,8,256]{2,1,0:T(8,128)}, f32[256,8,256]{2,1,0:T(8,128)}, u32[]{:S(2)}, u32[]{:S(2)}) collective-permute-start(f32[256,8,256]{2,1,0:T(8,128)} %copy.28.refs_5_), channel_id=1, source_target_pairs={{0,1},{1,0},{2,3},{3,2},{4,5},{5,4},{6,7},{7,6},{8,9},{9,8},{10,11... | collective-permute-start | bytes 6291464 | tf_op jit(solution)/shard_map/ppermute | solution.py:21
  133.3 45.7 %collective-permute-start.12 = (f32[256,8,256]{2,1,0:T(8,128)}, f32[256,8,256]{2,1,0:T(8,128)S(1)}, u32[]{:S(2)}, u32[]{:S(2)}) collective-permute-start(f32[256,8,256]{2,1,0:T(8,128)} %get-tuple-element.16.refs_4_.refs_0_), channel_id=1, source_target_pairs={{0,30},{2,0},{4,2},{6,4},{8,6},{10,8},{12,10},{14,12},{16,14},{18,... | collective-permute-start | bytes 6291464 | tf_op jit(solution)/shard_map/ppermute | solution.py:21
  135.8 43.2 %collective-permute-start.11 = (f32[256,8,256]{2,1,0:T(8,128)}, f32[256,8,256]{2,1,0:T(8,128)}, u32[]{:S(2)}, u32[]{:S(2)}) collective-permute-start(f32[256,8,256]{2,1,0:T(8,128)} %get-tuple-element.16.refs_4_.refs_0_), channel_id=1, source_target_pairs={{0,2},{2,4},{4,6},{6,8},{8,10},{10,12},{12,14},{14,16},{16,18},{18... | collective-permute-start | bytes 6291464 | tf_op jit(solution)/shard_map/ppermute | solution.py:21
  142.3 74.5 %collective-permute-start.15 = (f32[256,8,256]{2,1,0:T(8,128)}, f32[256,8,256]{2,1,0:T(8,128)}, u32[]{:S(2)}, u32[]{:S(2)}) collective-permute-start(f32[256,8,256]{2,1,0:T(8,128)} %copy.29.refs_5_), channel_id=1, source_target_pairs={{0,1},{1,0},{2,3},{3,2},{4,5},{5,4},{6,7},{7,6},{8,9},{9,8},{10,11... | collective-permute-start | bytes 6291464 | tf_op jit(solution)/shard_map/ppermute | solution.py:21
  176.4 35.9 %collective-permute-start.18 = (f32[128,8,256]{2,1,0:T(8,128)}, f32[128,8,256]{2,1,0:T(8,128)S(1)}, u32[]{:S(2)}, u32[]{:S(2)}) collective-permute-start(f32[128,8,256]{2,1,0:T(8,128)} %get-tuple-element.19.refs_4_.refs_0_), channel_id=1, source_target_pairs={{0,30},{2,0},{4,2},{6,4},{8,6},{10,8},{12,10},{14,12},{16,14},{18,... | collective-permute-start | bytes 3145736 | tf_op jit(solution)/shard_map/ppermute | solution.py:21
  178.9 33.5 %collective-permute-start.17 = (f32[128,8,256]{2,1,0:T(8,128)}, f32[128,8,256]{2,1,0:T(8,128)}, u32[]{:S(2)}, u32[]{:S(2)}) collective-permute-start(f32[128,8,256]{2,1,0:T(8,128)} %get-tuple-element.19.refs_4_.refs_0_), channel_id=1, source_target_pairs={{0,2},{2,4},{4,6},{6,8},{8,10},{10,12},{12,14},{14,16},{16,18},{18... | collective-permute-start | bytes 3145736 | tf_op jit(solution)/shard_map/ppermute | solution.py:21
  178.9 1.4 copy-start
  186.0 23.4 %collective-permute-start.19 = (f32[128,256]{1,0:T(8,128)}, f32[128,256]{1,0:T(8,128)S(1)}, u32[]{:S(2)}, u32[]{:S(2)}) collective-permute-start(f32[128,256]{1,0:T(8,128)} %small.9.refs_2_.refs_0_), channel_id=1, source_target_pairs={{0,2},{2,0},{4,6},{6,4},{8,10},{10,8},{12,14},{14,12},{16,18},{18,... | collective-permute-start | bytes 393224 | tf_op jit(solution)/shard_map/ppermute | solution.py:319
  207.9 33.5 %collective-permute-start.23 = (f32[128,8,256]{2,1,0:T(8,128)}, f32[128,8,256]{2,1,0:T(8,128)}, u32[]{:S(2)}, u32[]{:S(2)}) collective-permute-start(f32[128,8,256]{2,1,0:T(8,128)} %core_send.3.refs_2_), channel_id=1, source_target_pairs={{0,1},{1,0},{2,3},{3,2},{4,5},{5,4},{6,7},{7,6},{8,9},{9,8},{10,11... | collective-permute-start | bytes 3145736 | tf_op jit(solution)/shard_map/ppermute | solution.py:21
  209.4 0.7 copy-start.5
  212.4 1.0 copy-start.3
  221.8 26.7 %collective-permute-start.22 = (f32[128,8,256]{2,1,0:T(8,128)}, f32[128,8,256]{2,1,0:T(8,128)S(1)}, u32[]{:S(2)}, u32[]{:S(2)}) collective-permute-start(f32[128,8,256]{2,1,0:T(8,128)} %core.1.refs_3_.refs_0_), channel_id=1, source_target_pairs={{0,30},{2,0},{4,2},{6,4},{8,6},{10,8},{12,10},{14,12},{16,14},{18,... | collective-permute-start | bytes 3145736 | tf_op jit(solution)/shard_map/ppermute | solution.py:21
  222.4 26.7 %collective-permute-start.21 = (f32[128,8,256]{2,1,0:T(8,128)}, f32[128,8,256]{2,1,0:T(8,128)S(1)}, u32[]{:S(2)}, u32[]{:S(2)}) collective-permute-start(f32[128,8,256]{2,1,0:T(8,128)} %core.1.refs_3_.refs_0_), channel_id=1, source_target_pairs={{0,2},{2,4},{4,6},{6,8},{8,10},{10,12},{12,14},{14,16},{16,18},{18... | collective-permute-start | bytes 3145736 | tf_op jit(solution)/shard_map/ppermute | solution.py:21
  227.0 26.9 %all-to-all-start = ((f32[32,8,256]{2,1,0:T(8,128)}), f32[32,8,256]{2,1,0:T(8,128)S(1)}, u32[]{:S(2)}, u32[]{:S(2)}) async-start(f32[32,8,256]{2,1,0:T(8,128)} %bitcast.5), calls=%async_computation | async-start | bytes 524288 | tf_op jit(solution)/shard_map/all_to_all | solution.py:389
  236.2 36.1 %collective-permute-start.26 = (f32[128,8,256]{2,1,0:T(8,128)}, f32[128,8,256]{2,1,0:T(8,128)S(1)}, u32[]{:S(2)}, u32[]{:S(2)}) collective-permute-start(f32[128,8,256]{2,1,0:T(8,128)} %place.12.refs_3_), channel_id=1, source_target_pairs={{0,1},{1,0},{2,3},{3,2},{4,5},{5,4},{6,7},{7,6},{8,9},{9,8},{10,11... | collective-permute-start | bytes 3145736 | tf_op jit(solution)/shard_map/ppermute | solution.py:21
  245.4 30.5 %collective-permute-start.25 = (f32[128,8,256]{2,1,0:T(8,128)}, f32[128,8,256]{2,1,0:T(8,128)}, u32[]{:S(2)}, u32[]{:S(2)}) collective-permute-start(f32[128,8,256]{2,1,0:T(8,128)} %core_finish.3.refs_4_.refs_0_), channel_id=1, source_target_pairs={{0,30},{2,0},{4,2},{6,4},{8,6},{10,8},{12,10},{14,12},{16,14},{18,... | collective-permute-start | bytes 3145736 | tf_op jit(solution)/shard_map/ppermute | solution.py:21
  248.5 27.4 %collective-permute-start.24 = (f32[128,8,256]{2,1,0:T(8,128)}, f32[128,8,256]{2,1,0:T(8,128)}, u32[]{:S(2)}, u32[]{:S(2)}) collective-permute-start(f32[128,8,256]{2,1,0:T(8,128)} %core_finish.3.refs_4_.refs_0_), channel_id=1, source_target_pairs={{0,2},{2,4},{4,6},{6,8},{8,10},{10,12},{12,14},{14,16},{16,18},{18... | collective-permute-start | bytes 3145736 | tf_op jit(solution)/shard_map/ppermute | solution.py:21
  248.5 1.0 copy-start.1
  248.5 40.1 %collective-permute-start.20 = (f32[128,8,256]{2,1,0:T(8,128)}, f32[128,8,256]{2,1,0:T(8,128)}, u32[]{:S(2)}, u32[]{:S(2)}) collective-permute-start(f32[128,8,256]{2,1,0:T(8,128)} %place.13.refs_3_), channel_id=1, source_target_pairs={{0,1},{1,0},{2,3},{3,2},{4,5},{5,4},{6,7},{7,6},{8,9},{9,8},{10,11... | collective-permute-start | bytes 3145736 | tf_op jit(solution)/shard_map/ppermute | solution.py:21
  249.5 1.0 copy-start.2
  253.9 0.7 copy-start.4
  256.9 31.9 %all-to-all-start.1 = ((f32[32,8,256]{2,1,0:T(8,128)}), f32[32,8,256]{2,1,0:T(8,128)}, u32[]{:S(2)}, u32[]{:S(2)}) async-start(f32[32,8,256]{2,1,0:T(8,128)} %sum.1.refs_2_), calls=%async_computation.1 | async-start | bytes 524288 | tf_op jit(solution)/shard_map/all_to_all | solution.py:395
  272.3 1.0 copy-start.8

commit v4 on v3

--- a/solution.py
+++ b/solution.py
@@ -12,7 +12,7 @@
 TILE = 8
 VMEM_LIMIT = 60 * 1024 * 1024
 HEAVY = 3 * 10**10
-WEIGHTS = {15: 0.3, 16: 0.3, 18: 0.2, 19: 0, 20: 0.2, 21: 0, 22: 0, 26: 0, 28: 0.1, 29: 0.1, 30: 3, 31: 3, 32: 3}
+WEIGHTS = {15: 0.3, 16: 0.3, 18: 0.2, 19: 0, 20: 0.2, 21: 0, 22: 0, 27: 0, 29: 0.1, 30: 0.1, 31: 3, 32: 3, 33: 3}
 MINE, THEIRS, CORE, SOURCE, SLOT = 0, 1, 2, 3, 3 + BLOCKS_DEV
 
 
@@ -148,7 +148,7 @@
         put_species(out_ref, s, species(arrived_ref, s) + dot3(at, halves(species(field_ref, s)), dot))
 
 
-def cross_kernel(first, last, index_ref, mine_ref, theirs_ref, *rest):
+def cross_kernel(first, index_ref, mine_ref, theirs_ref, *rest):
     out_ref = rest[-1]
     step = pl.program_id(0)
 
@@ -161,10 +161,20 @@
         total = total + dot3(halves(species(mine_ref, s)), halves(species(theirs_ref, s)), dot_nt)
     out_ref[...] = total
 
-    if last:
-        @pl.when((step == pl.num_programs(0) - 1) & (index_ref[MINE] == 1))
+
+def cross_last_kernel(index_ref, mine_ref, theirs_ref, sum_ref, keep_ref, send_ref, total_ref):
+    cross_kernel(False, index_ref, mine_ref, theirs_ref, sum_ref, total_ref)
+
+    @pl.when(pl.program_id(0) == pl.num_programs(0) - 1)
+    def _():
+        @pl.when(index_ref[MINE] == 1)
         def _():
-            out_ref[...] = out_ref[...].T
+            total_ref[...] = total_ref[...].T
+
+        half = keep_ref.shape[0]
+        odd = index_ref[CORE]
+        keep_ref[...] = total_ref[pl.ds(pl.multiple_of(odd * half, half), half), :]
+        send_ref[...] = total_ref[pl.ds(pl.multiple_of((1 - odd) * half, half), half), :]
 
 
 def core_kernel(index_ref, factor_ref, cross_factor_ref, mine_ref, theirs_ref, out_ref):
@@ -177,7 +187,7 @@
 def received_kernel(first, index_ref, factor_ref, cross_factor_ref, mine_ref, theirs_ref, *rest):
     core_ref, cross_ref = rest[-2:]
     core_kernel(index_ref, factor_ref, cross_factor_ref, mine_ref, theirs_ref, core_ref)
-    cross_kernel(first, False, index_ref, mine_ref, theirs_ref, *rest[:-2], cross_ref)
+    cross_kernel(first, index_ref, mine_ref, theirs_ref, *rest[:-2], cross_ref)
 
 
 def diagonal_kernel(scale, index_ref, field_ref, keep_ref, send_ref, high_ref, mixed_ref):
@@ -206,9 +216,22 @@
         send_ref[...] = high_ref[pl.ds(pl.multiple_of((1 - odd) * half, half), half), :]
 
 
+def tiles(count, rows, columns):
+    across = columns // POINTS
+    high = rows * across // count
+    return [(t, slice(t // across * high, (t // across + 1) * high), slice(t % across * POINTS, (t % across + 1) * POINTS)) for t in range(count)]
+
+
+def cut_kernel(index_ref, keep_ref, other_ref, out_ref):
+    for t, rows, columns in tiles(out_ref.shape[0], *keep_ref.shape):
+        out_ref[t] = keep_ref[rows, columns] + other_ref[rows, columns]
+
+
 def sum_kernel(scale, index_ref, pieces_ref, out_ref):
-    total = jnp.sum(pieces_ref[...], axis=0) * scale
-    out_ref[...] = jnp.broadcast_to(total[None], out_ref.shape)
+    count, high, _ = pieces_ref.shape
+    for odd in range(2):
+        total = functools.reduce(jnp.add, [pieces_ref[s] for s in range(count) if s // 2 % 2 == odd]) * scale
+        out_ref[:, odd * high : (odd + 1) * high, :] = jnp.broadcast_to(total[None], (count,) + total.shape)
 
 
 def place_kernel(index_ref, here_ref, lower_ref, upper_ref, *rest):
@@ -244,13 +267,13 @@
 def last_kernel(
     i, index_ref, part_ref, diagonal_ref, cross_ref, old_ref, core_ref, gram_ref, *scratch
 ):
-    stage_ref, in_sems, out_sems, diagonal_stage, cross_stage, gram_sems = scratch
-    z = cross_ref.shape[0]
+    stage_ref, in_sems, out_sems, diagonal_stage, cross_stage, pieces_stage, gram_sems = scratch
+    z = diagonal_ref.shape[0]
     mine = index_ref[MINE]
     blocks = [pl.ds(pl.multiple_of(at * z, z), z) for at in (mine, 1 - mine)]
     loads = [
         pltpu.make_async_copy(diagonal_ref, diagonal_stage, gram_sems.at[0]),
-        pltpu.make_async_copy(cross_ref, cross_stage, gram_sems.at[1]),
+        pltpu.make_async_copy(cross_ref, pieces_stage, gram_sems.at[1]),
     ]
     stores = [
         pltpu.make_async_copy(diagonal_stage, gram_ref.at[:, blocks[0]], gram_sems.at[2]),
@@ -262,6 +285,11 @@
     loads[0].wait()
     stores[0].start()
     loads[1].wait()
+    count, high, _ = pieces_stage.shape
+    for odd in range(2):
+        for t, rows, columns in tiles(count, z // 2, z):
+            place = slice(odd * z // 2 + rows.start, odd * z // 2 + rows.stop)
+            cross_stage[place, columns] = pieces_stage[t, odd * high // 2 : (odd + 1) * high // 2, :]
 
     @pl.when(mine == 1)
     def _():
@@ -305,6 +333,7 @@
     any_space = pl.BlockSpec(memory_space=pl.ANY)
     whole_factor = whole(factor.shape)
     slabs = 4
+    axes = ("xy", "gz")
 
     def staging(rows):
         return [pltpu.VMEM((rows, TILE, points), jnp.float32)] + [pltpu.SemaphoreType.DMA((slabs,))] * 2
@@ -347,10 +376,11 @@
         received = pl.BlockSpec((z, TILE, POINTS), lambda p, w: (0, 0, p))
         return [(field, field_chunk(z, chunks, MINE, i)), (theirs, received)]
 
-    def add_cross(i, theirs, cross):
-        inputs = both_halves(i, theirs) + ([] if cross is None else [(cross, whole((z, z)))])
-        kernel = functools.partial(cross_kernel, cross is None, i == chunks - 1)
-        return steps.call(kernel, "cross", (columns,), inputs, [((z, z), whole((z, z)))])[0]
+    def add_last_cross(i, theirs, cross):
+        inputs = both_halves(i, theirs) + [(cross, whole((z, z)))]
+        half = ((z // 2, z), whole((z // 2, z)))
+        scratch = [pltpu.VMEM((z, z), jnp.float32)]
+        return steps.call(cross_last_kernel, "cross", (columns,), inputs, [half, half], None, scratch)
 
     def core_of(i, theirs, cross_factor, ranks_spec, out_rank):
         inputs = [(factor, ranks_spec), (cross_factor, ranks_spec)] + both_halves(i, theirs)
@@ -383,16 +413,18 @@
         kernel = functools.partial(join_kernel, axis)
         return steps.call(kernel, "join", (1,), [(keep, spec), (other, spec)], [(shape, whole(shape))])[0]
 
-    def spread(matrix, axes):
-        parts = lax.axis_size(axes)
-        pieces = matrix.reshape(parts, z // parts, z)
+    def spread(keep, other):
+        shape = (lax.axis_size(axes), z // 2 * z // lax.axis_size(axes) // POINTS, POINTS)
+        inputs = [(keep, whole(keep.shape)), (other, whole(other.shape))]
+        pieces = steps.call(cut_kernel, "cut", (1,), inputs, [(shape, whole(shape))])[0]
         return lax.all_to_all(pieces, axes, split_axis=0, concat_axis=0, tiled=True)
 
-    def summed(pieces, axes):
-        spec = whole(pieces.shape)
+    def summed(pieces):
+        count, high, _ = pieces.shape
+        shape = (count, 2 * high, POINTS)
         kernel = functools.partial(sum_kernel, scale)
-        total = steps.call(kernel, "sum", (1,), [(pieces, spec)], [(pieces.shape, spec)])[0]
-        return lax.all_to_all(total, axes, split_axis=0, concat_axis=0, tiled=True).reshape(z, z)
+        total = steps.call(kernel, "sum", (1,), [(pieces, whole(pieces.shape))], [(shape, whole(shape))])[0]
+        return lax.all_to_all(total, axes, split_axis=0, concat_axis=0, tiled=True)
 
     def place(parts, half=None, core=None, at=MINE, i=0):
         rows = (lambda w: 0) if half is None else (lambda w: w[half])
@@ -448,17 +480,20 @@
     diagonal = joined(0, diagonal, half)
     core = place(ready[2], None, core, MINE, 2)
     ready[3] = neighbours(core_of(3, fields[3], cross_factor, own_ranks, rank))
-    cross = spread(add_cross(3, fields[3], cross), ("xy", "gz"))
+    keep, send = add_last_cross(3, fields[3], cross)
+    half = exchanged(send, 1)
     arrived[0] = over_gz(place(ready[0], THEIRS))
+    cross = spread(keep, half)
     arrived[1] = over_gz(place(ready[1], THEIRS))
     late3 = neighbours(core_finish(3, arrived[3]))
     core = place(ready[3], None, core, MINE, 3)
-    cross = summed(cross, ("xy", "gz"))
+    cross = summed(cross)
     core = put(arrived[0], core, 0)
     core = place(late3, None, core, THEIRS, 3)
     inputs = [(array, any_space) for array in (arrived[1], diagonal, cross, core)]
     outputs = [((rank, count, points), any_space), ((z, 2 * z), any_space)]
-    scratch = staging(rank) + [pltpu.VMEM((z, z), jnp.float32)] * 2 + [pltpu.SemaphoreType.DMA((4,))]
+    scratch = staging(rank) + [pltpu.VMEM((z, z), jnp.float32)] * 2
+    scratch += [pltpu.VMEM(cross.shape, jnp.float32), pltpu.SemaphoreType.DMA((4,))]
     kernel = functools.partial(last_kernel, 1)
     core, gram = steps.call(kernel, "last", (1,), inputs, outputs, {3: 0}, scratch)
     return (gram, core)

time: 294 us -> 291 us (0.990)
  starting transfers between devices: 69.9 us -> 62 us
  Pallas kernels: 131 us -> 134 us
    all_to_all x1, starting transfers between devices: 15.3 us -> 6.43 us  [summed(): return lax.all_to_all(total, axes, split_axis=0, concat_axis=0, tiled=True)]
    all_to_all x1, waiting for transfers between devices: 0.01 us -> 3.91 us  [spread(): return lax.all_to_all(pieces, axes, split_axis=0, concat_axis=0, tiled=True)]
    pallas_call x33 -> x34, Pallas kernels: 131 us -> 134 us  [call(): pl.pallas_call(body, out_shape=[jax.ShapeDtypeStruct(shape, jnp.float32)...]
    ppermute x6 -> x7, starting transfers between devices: 20.2 us -> 21.8 us  [exchanged(): lax.ppermute(part, 'xy', [(i, i ^ bit) for i in range(lax.axis_size('xy'))])]
    unnamed x34 -> x36, local copies, waits for them, and re-layouts: 10.4 us -> 10.6 us
  transfers between devices with their start and end apart: 29 -> 30, of which waited for: 7 -> 8; matrix products, arithmetic and copies ran while one was open for 0% -> 0% of each run, Pallas kernels for 42% -> 44%
where the time goes in v4:
time: 291 us; the launch traced here: 289 us
  Pallas kernels  134 us (46%)
  waiting for transfers between devices  80.8 us (28%)
  starting transfers between devices  62 us (21%)
  local copies, waits for them, and re-layouts  11.3 us (4%)
    pallas_call x34, Pallas kernels, call(): pl.pallas_call(body, out_shape=[jax.ShapeDtypeStruct(shape, jnp.float32)...  134 us
    ppermute x21, waiting for transfers between devices, shifted(): lax.ppermute(array, axis, [(i, (i + by) % length) for i in range(length)])  76.7 us
    ppermute x21, starting transfers between devices, shifted(): lax.ppermute(array, axis, [(i, (i + by) % length) for i in range(length)])  29.4 us
    ppermute x7, starting transfers between devices, exchanged(): lax.ppermute(part, 'xy', [(i, i ^ bit) for i in range(lax.axis_size('xy'))])  21.8 us
    unnamed x36, local copies, waits for them, and re-layouts  10.6 us
    all_to_all x1, starting transfers between devices, summed(): return lax.all_to_all(total, axes, split_axis=0, concat_axis=0, tiled=True)  6.43 us
  transfers between devices with their start and end apart: 30, of which 8 were waited for; matrix products, arithmetic and copies ran while one was open for 0% of the time, Pallas kernels for 44%

profile of v4, /device:TPU:0, one launch (start us, length us, event | category | flops | bytes accessed | tf_op | source)
XLA Modules:
  0.0 289.4 jit_solution(11727252618688467586)
XLA Ops:
  1.2 3.8 %core_send.2.refs_1_ = f32[128,8,256]{2,1,0:T(8,128)} custom-call(s32[3]{0:T(128)} %pad_add_fusion.index_ref, f32[256,256]{1,0:T(8,128)} %refs_0_.29, f32[256,64,256]{2,1,0:T(8,128)} %refs_1_.7), custom_call_target="tpu_custom_call" | custom-call | flops 30000001024 | tf_op jit(solution)/shard_map/core_send/pallas_call | solution.py:70
  5.0 3.0 %collective-permute-start.6 = (f32[128,8,256]{2,1,0:T(8,128)}, f32[128,8,256]{2,1,0:T(8,128)}, u32[]{:S(2)}, u32[]{:S(2)}) collective-permute-start(f32[128,8,256]{2,1,0:T(8,128)} %core_send.2.refs_1_), channel_id=1, source_target_pairs={{0,1},{1,0},{2,3},{3,2},{4,5},{5,4},{6,7},{7,6},{8,9},{9,8},{10,11... | collective-permute-start | bytes 3145736 | tf_op jit(solution)/shard_map/ppermute | solution.py:21
  10.2 3.3 %copy.26.refs_1_ = f32[256,8,256]{2,1,0:T(8,128)} custom-call(s32[3]{0:T(128)} %pad_add_fusion.index_ref, f32[256,64,256]{2,1,0:T(8,128)} %refs_1_.7, f32[256,128]{1,0:T(8,128)} %copy.25.refs_1_), custom_call_target="tpu_custom_call" | custom-call | flops 30000001024 | tf_op jit(solution)/shard_map/copy/pallas_call | solution.py:70
  16.2 16.5 %diagonal.1 = (f32[128,256]{1,0:T(8,128)}, f32[128,256]{1,0:T(8,128)}) custom-call(s32[7]{0:T(128)} %concatenate.4.index_ref, f32[256,64,256]{2,1,0:T(8,128)} %refs_1_.7, f32[256,8,256]{2,1,0:T(8,128)} %copy.26.refs_1_), custom_call_target="tpu_custom_call" | custom-call | flops 30000001024 | tf_op jit(solution)/shard_map/diagonal/pallas_call | solution.py:70
  32.7 3.2 %copy.27.refs_2_ = f32[256,8,256]{2,1,0:T(8,128)} custom-call(s32[7]{0:T(128)} %concatenate.4.index_ref, f32[256,64,256]{2,1,0:T(8,128)} %refs_1_.7, f32[128,256]{1,0:T(8,128)} %get-tuple-element.14.refs_1_.refs_0_), custom_call_target="tpu_custom_call" | custom-call | flops 30000001024 | tf_op jit(solution)/shard_map/copy/pallas_call | solution.py:70
  37.2 2.3 small.5.refs_2_.refs_0_
  41.7 2.4 join.2.refs_3_.refs_1_
  44.1 4.0 %core_finish.2.refs_2_.refs_0_ = f32[128,8,256]{2,1,0:T(8,128)} custom-call(s32[7]{0:T(128)} %concatenate.4.index_ref, f32[256,256]{1,0:T(8,128)} %refs_0_.29, f32[256,64,256]{2,1,0:T(8,128)} %refs_1_.7, f32[128,8,256]{2,1,0:T(8,128)} %collective-permute-done.6.refs_2_, f32[256,256]{1,0:T(8,128)} %join.2.refs_3_.refs_1_), custom_call_target="tpu_custom_call" | custom-call | flops 30000001024 | tf_op jit(solution)/shard_map/core_finish/pallas_call | solution.py:70
  48.1 3.2 %collective-permute-start.9 = (f32[128,8,256]{2,1,0:T(8,128)}, f32[128,8,256]{2,1,0:T(8,128)S(1)}, u32[]{:S(2)}, u32[]{:S(2)}) collective-permute-start(f32[128,8,256]{2,1,0:T(8,128)} %core_finish.2.refs_2_.refs_0_), channel_id=1, source_target_pairs={{0,30},{2,0},{4,2},{6,4},{8,6},{10,8},{12,10},{14,12},{16,14},{18,... | collective-permute-start | bytes 3145736 | tf_op jit(solution)/shard_map/ppermute | solution.py:21
  52.0 2.3 small.6.refs_3_.refs_0_
  54.3 11.1 %collective-permute-done.9.refs_2_ = f32[128,8,256]{2,1,0:T(8,128)S(1)} collective-permute-done((f32[128,8,256]{2,1,0:T(8,128)}, f32[128,8,256]{2,1,0:T(8,128)S(1)}, u32[]{:S(2)}, u32[]{:S(2)}) %collective-permute-start.9) | collective-permute-done | bytes 1048608 | tf_op jit(solution)/shard_map/ppermute | solution.py:21
  65.3 4.6 %collective-permute-done.8.refs_1_ = f32[128,8,256]{2,1,0:T(8,128)S(1)} collective-permute-done((f32[128,8,256]{2,1,0:T(8,128)}, f32[128,8,256]{2,1,0:T(8,128)S(1)}, u32[]{:S(2)}, u32[]{:S(2)}) %collective-permute-start.8) | collective-permute-done | bytes 1048608 | tf_op jit(solution)/shard_map/ppermute | solution.py:21
  70.9 3.4 %place.8.refs_2_.refs_3_ = f32[128,64,256]{2,1,0:T(8,128)} custom-call(s32[7]{0:T(128)} %concatenate.4.index_ref, f32[128,8,256]{2,1,0:T(8,128)} %core_finish.2.refs_2_.refs_0_, f32[128,8,256]{2,1,0:T(8,128)} %copy-done.10, f32[128,8,256]{2,1,0:T(8,128)} %copy-done.9, f32[128,256]{1,0:T(8,128)} %small.6.refs_3_.refs_0_), custom_call_target="tpu_custom_call" | custom-call | flops 30000001024 | tf_op jit(solution)/shard_map/place/pallas_call | solution.py:70
  77.2 2.8 collective-permute-done.4.refs_3_
  80.0 8.3 %received.3 = (f32[256,8,256]{2,1,0:T(8,128)}, f32[256,256]{1,0:T(8,128)}) custom-call(s32[7]{0:T(128)} %concatenate.4.index_ref, f32[256,256]{1,0:T(8,128)} %refs_0_.29, f32[256,256]{1,0:T(8,128)} %join.2.refs_3_.refs_1_, f32[256,64,256]{2,1,0:T(8,128)} %refs_1_.7, f32[256,8,256]{2,1,0:T(8,128)} %collective-permute-done.4.refs_3_, ...), custom_call_target="tpu_custom_call" | custom-call | flops 30000001024 | tf_op jit(solution)/shard_map/received/pallas_call | solution.py:70
  88.3 2.5 collective-permute-start.14
  90.8 2.3 collective-permute-start.13
  93.8 2.3 small.8.refs_1_.refs_0_
  96.1 3.1 %copy.28.refs_5_ = f32[256,8,256]{2,1,0:T(8,128)} custom-call(s32[7]{0:T(128)} %concatenate.4.index_ref, f32[256,64,256]{2,1,0:T(8,128)} %refs_1_.7, f32[128,256]{1,0:T(8,128)} %small.8.refs_1_.refs_0_), custom_call_target="tpu_custom_call" | custom-call | flops 30000001024 | tf_op jit(solution)/shard_map/copy/pallas_call | solution.py:70
  100.8 24.2 %collective-permute-done.3.refs_3_ = f32[256,8,256]{2,1,0:T(8,128)} collective-permute-done((f32[256,8,256]{2,1,0:T(8,128)}, f32[256,8,256]{2,1,0:T(8,128)}, u32[]{:S(2)}, u32[]{:S(2)}) %collective-permute-start.3) | collective-permute-done | bytes 2097184 | tf_op jit(solution)/shard_map/ppermute | solution.py:21
  125.0 8.3 %received.4 = (f32[256,8,256]{2,1,0:T(8,128)}, f32[256,256]{1,0:T(8,128)}) custom-call(s32[7]{0:T(128)} %concatenate.4.index_ref, f32[256,256]{1,0:T(8,128)} %refs_0_.29, f32[256,256]{1,0:T(8,128)} %join.2.refs_3_.refs_1_, f32[256,64,256]{2,1,0:T(8,128)} %refs_1_.7, f32[256,8,256]{2,1,0:T(8,128)} %collective-permute-done.3.refs_3_, ...), custom_call_target="tpu_custom_call" | custom-call | flops 30000001024 | tf_op jit(solution)/shard_map/received/pallas_call | solution.py:70
  133.3 2.5 collective-permute-start.12
  135.8 3.4 %place.9.refs_1_.refs_3_ = f32[128,64,256]{2,1,0:T(8,128)} custom-call(s32[7]{0:T(128)} %concatenate.4.index_ref, f32[256,8,256]{2,1,0:T(8,128)} %get-tuple-element.17.refs_2_.refs_0_, f32[256,8,256]{2,1,0:T(8,128)} %collective-permute-done.13.refs_1_, f32[256,8,256]{2,1,0:T(8,128)} %collective-permute-done.14.refs_2_, ...), custom_call_target="tpu_custom_call", output_to_operand_aliasing={{}: (4, {})} | custom-call | flops 8999999488 | tf_op jit(solution)/shard_map/place/pallas_call | solution.py:70
  139.2 3.1 %copy.29.refs_5_ = f32[256,8,256]{2,1,0:T(8,128)} custom-call(s32[7]{0:T(128)} %concatenate.4.index_ref, f32[256,64,256]{2,1,0:T(8,128)} %refs_1_.7, f32[128,64,256]{2,1,0:T(8,128)} %place.9.refs_1_.refs_3_), custom_call_target="tpu_custom_call" | custom-call | flops 8999999488 | tf_op jit(solution)/shard_map/copy/pallas_call | solution.py:70
  143.9 26.0 %collective-permute-done.16.refs_3_ = f32[256,8,256]{2,1,0:T(8,128)} collective-permute-done((f32[256,8,256]{2,1,0:T(8,128)}, f32[256,8,256]{2,1,0:T(8,128)}, u32[]{:S(2)}, u32[]{:S(2)}) %collective-permute-start.16) | collective-permute-done | bytes 2097184 | tf_op jit(solution)/shard_map/ppermute | solution.py:21
  169.9 6.6 %received.5 = (f32[128,8,256]{2,1,0:T(8,128)}, f32[256,256]{1,0:T(8,128)}) custom-call(s32[7]{0:T(128)} %concatenate.4.index_ref, f32[256,256]{1,0:T(8,128)} %refs_0_.29, f32[256,256]{1,0:T(8,128)} %join.2.refs_3_.refs_1_, f32[256,64,256]{2,1,0:T(8,128)} %refs_1_.7, f32[256,8,256]{2,1,0:T(8,128)} %collective-permute-done.16.refs_3_, ...), custom_call_target="tpu_custom_call" | custom-call | flops 30000001024 | tf_op jit(solution)/shard_map/received/pallas_call | solution.py:70
  176.5 2.5 collective-permute-start.18
  180.4 3.4 %place.10.refs_1_.refs_3_ = f32[128,64,256]{2,1,0:T(8,128)} custom-call(s32[7]{0:T(128)} %concatenate.4.index_ref, f32[256,8,256]{2,1,0:T(8,128)} %get-tuple-element.18.refs_4_.refs_0_, f32[256,8,256]{2,1,0:T(8,128)} %collective-permute-done.11.refs_1_, f32[256,8,256]{2,1,0:T(8,128)} %copy-done, ...), custom_call_target="tpu_custom_call", output_to_operand_aliasing={{}: (4, {})} | custom-call | flops 6000000000 | tf_op jit(solution)/shard_map/place/pallas_call | solution.py:70
  186.0 18.8 %collective-permute-start.19 = (f32[128,256]{1,0:T(8,128)}, f32[128,256]{1,0:T(8,128)S(1)}, u32[]{:S(2)}, u32[]{:S(2)}) collective-permute-start(f32[128,256]{1,0:T(8,128)} %small.9.refs_2_.refs_0_), channel_id=1, source_target_pairs={{0,2},{2,0},{4,6},{6,4},{8,10},{10,8},{12,14},{14,12},{16,18},{18,... | collective-permute-start | bytes 393224 | tf_op jit(solution)/shard_map/ppermute | solution.py:348
  204.8 3.8 %core_send.3.refs_2_ = f32[128,8,256]{2,1,0:T(8,128)} custom-call(s32[7]{0:T(128)} %concatenate.4.index_ref, f32[256,256]{1,0:T(8,128)} %refs_0_.29, f32[256,64,256]{2,1,0:T(8,128)} %refs_1_.7, f32[128,256]{1,0:T(8,128)} %small.9.refs_2_.refs_0_), custom_call_target="tpu_custom_call" | custom-call | flops 6000000000 | tf_op jit(solution)/shard_map/core_send/pallas_call | solution.py:70
  210.8 2.3 join.3.refs_4_.refs_1_
  214.1 3.4 %place.11.refs_4_.refs_3_ = f32[128,64,256]{2,1,0:T(8,128)} custom-call(s32[7]{0:T(128)} %concatenate.4.index_ref, f32[128,8,256]{2,1,0:T(8,128)} %get-tuple-element.21.refs_4_.refs_0_, f32[128,8,256]{2,1,0:T(8,128)} %collective-permute-done.17.refs_1_, f32[128,8,256]{2,1,0:T(8,128)} %copy-done.3, ...), custom_call_target="tpu_custom_call", output_to_operand_aliasing={{}: (4, {})} | custom-call | tf_op jit(solution)/shard_map/place/pallas_call | solution.py:70
  217.5 5.0 %core.1.refs_3_.refs_0_ = f32[128,8,256]{2,1,0:T(8,128)} custom-call(s32[7]{0:T(128)} %concatenate.4.index_ref, f32[256,256]{1,0:T(8,128)} %refs_0_.29, f32[256,256]{1,0:T(8,128)} %join.2.refs_3_.refs_1_, f32[256,64,256]{2,1,0:T(8,128)} %refs_1_.7, f32[256,8,256]{2,1,0:T(8,128)} %collective-permute-done.15.refs_3_.refs_1_, f32[128,64,256]{2,1,0:T(8,128)} %place.11.refs_4_.refs_3_), custom_call_target="tpu_custom_call" | custom-call | flops 30000001024 | tf_op jit(solution)/shard_map/core/pallas_call | solution.py:70
  223.0 4.6 %cross.1 = (f32[128,256]{1,0:T(8,128)}, f32[128,256]{1,0:T(8,128)}) custom-call(s32[7]{0:T(128)} %concatenate.4.index_ref, f32[256,64,256]{2,1,0:T(8,128)} %refs_1_.7, f32[256,8,256]{2,1,0:T(8,128)} %collective-permute-done.15.refs_3_.refs_1_, f32[256,256]{1,0:T(8,128)} %get-tuple-element.20.refs_2_, f32[128,8,256]{2,1,0:T(8,128)} %core.1.refs_3_.refs_0_), custom_call_target="tpu_custom_call" | custom-call | flops 30000001024 | tf_op jit(solution)/shard_map/cross/pallas_call | solution.py:70
  228.6 3.4 %place.12.refs_2_ = f32[128,8,256]{2,1,0:T(8,128)} custom-call(s32[7]{0:T(128)} %concatenate.4.index_ref, f32[256,8,256]{2,1,0:T(8,128)} %get-tuple-element.17.refs_2_.refs_0_, f32[256,8,256]{2,1,0:T(8,128)} %collective-permute-done.13.refs_1_, f32[256,8,256]{2,1,0:T(8,128)} %collective-permute-done.14.refs_2_, f32[128,256]{1,0:T(8,128)} %get-tuple-element.22.refs_3_.refs_0_), custom_call_target="tpu_custom_call" | custom-call | flops 30000001024 | tf_op jit(solution)/shard_map/place/pallas_call | solution.py:70
  233.3 2.3 cut.1.refs_3_
  235.6 4.3 %all-to-all-start = ((f32[32,8,128]{2,1,0:T(8,128)}), f32[32,8,128]{2,1,0:T(8,128)S(1)}, u32[]{:S(2)}, u32[]{:S(2)}) async-start(f32[32,8,128]{2,1,0:T(8,128)} %cut.1.refs_3_), calls=%async_computation | async-start | bytes 262144 | tf_op jit(solution)/shard_map/all_to_all | solution.py:420
  239.9 3.4 %place.13.refs_3_ = f32[128,8,256]{2,1,0:T(8,128)} custom-call(s32[7]{0:T(128)} %concatenate.4.index_ref, f32[256,8,256]{2,1,0:T(8,128)} %get-tuple-element.18.refs_4_.refs_0_, f32[256,8,256]{2,1,0:T(8,128)} %collective-permute-done.11.refs_1_, f32[256,8,256]{2,1,0:T(8,128)} %copy-done, f32[32,8,128]{2,1,0:T(8,128)} %cut.1.refs_3_), custom_call_target="tpu_custom_call" | custom-call | tf_op jit(solution)/shard_map/place/pallas_call | solution.py:70
  243.3 4.0 %core_finish.3.refs_4_.refs_0_ = f32[128,8,256]{2,1,0:T(8,128)} custom-call(s32[7]{0:T(128)} %concatenate.4.index_ref, f32[256,256]{1,0:T(8,128)} %refs_0_.29, f32[256,64,256]{2,1,0:T(8,128)} %refs_1_.7, f32[128,8,256]{2,1,0:T(8,128)} %collective-permute-done.24.refs_2_, f32[128,8,256]{2,1,0:T(8,128)} %place.13.refs_3_), custom_call_target="tpu_custom_call" | custom-call | flops 30000001024 | tf_op jit(solution)/shard_map/core_finish/pallas_call | solution.py:70
  247.3 4.0 %collective-permute-start.26 = (f32[128,8,256]{2,1,0:T(8,128)}, f32[128,8,256]{2,1,0:T(8,128)}, u32[]{:S(2)}, u32[]{:S(2)}) collective-permute-start(f32[128,8,256]{2,1,0:T(8,128)} %core_finish.3.refs_4_.refs_0_), channel_id=1, source_target_pairs={{0,30},{2,0},{4,2},{6,4},{8,6},{10,8},{12,10},{14,12},{16,14},{18,... | collective-permute-start | bytes 3145736 | tf_op jit(solution)/shard_map/ppermute | solution.py:21
  253.8 3.4 %place.14.refs_1_ = f32[128,64,256]{2,1,0:T(8,128)} custom-call(s32[7]{0:T(128)} %concatenate.4.index_ref, f32[128,8,256]{2,1,0:T(8,128)} %core.1.refs_3_.refs_0_, f32[128,8,256]{2,1,0:T(8,128)} %copy-done.2, f32[128,8,256]{2,1,0:T(8,128)} %copy-done.1, f32[128,64,256]{2,1,0:T(8,128)} %place.11.refs_4_.refs_3_, ...), custom_call_target="tpu_custom_call", output_to_operand_aliasing={{}: (4, {})} | custom-call | flops 3000000000 | tf_op jit(solution)/shard_map/place/pallas_call | solution.py:70
  257.2 3.9 %all-to-all-done.refs_0_ = f32[32,8,128]{2,1,0:T(8,128)S(1)} async-done(((f32[32,8,128]{2,1,0:T(8,128)}), f32[32,8,128]{2,1,0:T(8,128)S(1)}, u32[]{:S(2)}, u32[]{:S(2)}) %all-to-all-start) | async-done | bytes 131104 | tf_op jit(solution)/shard_map/all_to_all | solution.py:420
  261.8 2.3 sum.1.refs_2_
  264.1 6.4 %all-to-all-start.1 = ((f32[32,16,128]{2,1,0:T(8,128)}), f32[32,16,128]{2,1,0:T(8,128)}, u32[]{:S(2)}, u32[]{:S(2)}) async-start(f32[32,16,128]{2,1,0:T(8,128)} %sum.1.refs_2_), calls=%async_computation.1 | async-start | bytes 524288 | tf_op jit(solution)/shard_map/all_to_all | solution.py:427
  271.5 2.6 put.1.refs_3_
  274.2 3.4 %place.15.refs_3_ = f32[128,64,256]{2,1,0:T(8,128)} custom-call(s32[7]{0:T(128)} %concatenate.4.index_ref, f32[128,8,256]{2,1,0:T(8,128)} %core_finish.3.refs_4_.refs_0_, f32[128,8,256]{2,1,0:T(8,128)} %collective-permute-done.25.refs_1_, f32[128,8,256]{2,1,0:T(8,128)} %collective-permute-done.26.refs_2_, ...), custom_call_target="tpu_custom_call", output_to_operand_aliasing={{}: (4, {})} | custom-call | flops 89999998976 | tf_op jit(solution)/shard_map/place/pallas_call | solution.py:70
  277.5 7.9 %collective-permute-done.21.refs_0_ = f32[128,8,256]{2,1,0:T(8,128)} collective-permute-done((f32[128,8,256]{2,1,0:T(8,128)}, f32[128,8,256]{2,1,0:T(8,128)}, u32[]{:S(2)}, u32[]{:S(2)}) %collective-permute-start.21) | collective-permute-done | bytes 1048608 | tf_op jit(solution)/shard_map/ppermute | solution.py:21
  285.7 3.6 %last.1 = (f32[128,64,256]{2,1,0:T(8,128)}, f32[256,512]{1,0:T(8,128)}) custom-call(s32[7]{0:T(128)} %concatenate.4.index_ref, f32[128,8,256]{2,1,0:T(8,128)} %collective-permute-done.21.refs_0_, f32[256,256]{1,0:T(8,128)} %join.3.refs_4_.refs_1_, f32[32,16,128]{2,1,0:T(8,128)} %all-to-all-done.1.refs_2_, ...), custom_call_target="tpu_custom_call", output_to_operand_aliasing={{0}: (4, {})} | custom-call | flops 89999998976 | tf_op jit(solution)/shard_map/last/pallas_call | solution.py:70
  (85 shorter events, 31.6 us)
Async XLA Ops:
  5.0 39.1 %collective-permute-start.6 = (f32[128,8,256]{2,1,0:T(8,128)}, f32[128,8,256]{2,1,0:T(8,128)}, u32[]{:S(2)}, u32[]{:S(2)}) collective-permute-start(f32[128,8,256]{2,1,0:T(8,128)} %core_send.2.refs_1_), channel_id=1, source_target_pairs={{0,1},{1,0},{2,3},{3,2},{4,5},{5,4},{6,7},{7,6},{8,9},{9,8},{10,11... | collective-permute-start | bytes 3145736 | tf_op jit(solution)/shard_map/ppermute | solution.py:21
  10.2 5.2 %copy-start.6 = (s32[32]{0:T(128)S(1)}, s32[32]{0:T(128)}, u32[]{:S(2)}) copy-start(s32[32]{0:T(128)} %param.7) | copy-start | bytes 388
  10.2 5.2 %copy-start.7 = (s32[32]{0:T(128)S(1)}, s32[32]{0:T(128)}, u32[]{:S(2)}) copy-start(s32[32]{0:T(128)} %param.6) | copy-start | bytes 388
  10.2 25.8 %collective-permute-start = (f32[256,128]{1,0:T(8,128)}, f32[256,128]{1,0:T(8,128)S(1)}, u32[]{:S(2)}, u32[]{:S(2)}) collective-permute-start(f32[256,128]{1,0:T(8,128)} %copy.25.refs_1_), channel_id=1, source_target_pairs={{0,1},{1,0},{2,3},{3,2},{4,5},{5,4},{6,7},{7,6},{8,9},{9,8},{10,11... | collective-permute-start | bytes 393224 | tf_op jit(solution)/shard_map/ppermute | solution.py:21
  13.5 66.5 %collective-permute-start.4 = (f32[256,8,256]{2,1,0:T(8,128)}, f32[256,8,256]{2,1,0:T(8,128)}, u32[]{:S(2)}, u32[]{:S(2)}) collective-permute-start(f32[256,8,256]{2,1,0:T(8,128)} %copy.26.refs_1_), channel_id=1, source_target_pairs={{0,1},{1,0},{2,3},{3,2},{4,5},{5,4},{6,7},{7,6},{8,9},{9,8},{10,11... | collective-permute-start | bytes 6291464 | tf_op jit(solution)/shard_map/ppermute | solution.py:21
  32.7 3.8 %collective-permute-start.2 = (f32[128,256]{1,0:T(8,128)}, f32[128,256]{1,0:T(8,128)S(1)}, u32[]{:S(2)}, u32[]{:S(2)}) collective-permute-start(f32[128,256]{1,0:T(8,128)} %get-tuple-element.15), channel_id=1, source_target_pairs={{0,2},{2,0},{4,6},{6,4},{8,10},{10,8},{12,14},{14,12},{16,18},{18,... | collective-permute-start | bytes 393224 | tf_op jit(solution)/shard_map/ppermute | solution.py:348
  35.9 89.1 %collective-permute-start.3 = (f32[256,8,256]{2,1,0:T(8,128)}, f32[256,8,256]{2,1,0:T(8,128)}, u32[]{:S(2)}, u32[]{:S(2)}) collective-permute-start(f32[256,8,256]{2,1,0:T(8,128)} %copy.27.refs_2_), channel_id=1, source_target_pairs={{0,1},{1,0},{2,3},{3,2},{4,5},{5,4},{6,7},{7,6},{8,9},{9,8},{10,11... | collective-permute-start | bytes 6291464 | tf_op jit(solution)/shard_map/ppermute | solution.py:21
  36.1 3.4 %copy-start.11 = (f32[256,128]{1,0:T(8,128)}, f32[256,128]{1,0:T(8,128)S(1)}, u32[]{:S(2)}) copy-start(f32[256,128]{1,0:T(8,128)S(1)} %collective-permute-done.refs_0_) | copy-start | bytes 393220
  36.1 5.0 %collective-permute-start.1 = (f32[256,128]{1,0:T(8,128)S(1)}, f32[256,128]{1,0:T(8,128)S(1)}, u32[]{:S(2)}, u32[]{:S(2)}) collective-permute-start(f32[256,128]{1,0:T(8,128)S(1)} %collective-permute-done.refs_0_), channel_id=1, source_target_pairs={{0,2},{2,0},{4,6},{6,4},{8,10},{10,8},{12,14},{14,12},{16,18},{18,... | collective-permute-start | bytes 393224 | tf_op jit(solution)/shard_map/ppermute | solution.py:348
  36.5 0.7 copy-start.14
  39.5 11.8 %collective-permute-start.5 = (f32[128,256]{1,0:T(8,128)}, f32[128,256]{1,0:T(8,128)S(1)}, u32[]{:S(2)}, u32[]{:S(2)}) collective-permute-start(f32[128,256]{1,0:T(8,128)} %small.5.refs_2_.refs_0_), channel_id=1, source_target_pairs={{0,4},{2,6},{4,0},{6,2},{8,12},{10,14},{12,8},{14,10},{16,20},{18,... | collective-permute-start | bytes 393224 | tf_op jit(solution)/shard_map/ppermute | solution.py:348
  41.1 0.7 copy-start.15
  48.1 17.2 %collective-permute-start.9 = (f32[128,8,256]{2,1,0:T(8,128)}, f32[128,8,256]{2,1,0:T(8,128)S(1)}, u32[]{:S(2)}, u32[]{:S(2)}) collective-permute-start(f32[128,8,256]{2,1,0:T(8,128)} %core_finish.2.refs_2_.refs_0_), channel_id=1, source_target_pairs={{0,30},{2,0},{4,2},{6,4},{8,6},{10,8},{12,10},{14,12},{16,14},{18,... | collective-permute-start | bytes 3145736 | tf_op jit(solution)/shard_map/ppermute | solution.py:21
  51.3 18.6 %collective-permute-start.8 = (f32[128,8,256]{2,1,0:T(8,128)}, f32[128,8,256]{2,1,0:T(8,128)S(1)}, u32[]{:S(2)}, u32[]{:S(2)}) collective-permute-start(f32[128,8,256]{2,1,0:T(8,128)} %core_finish.2.refs_2_.refs_0_), channel_id=1, source_target_pairs={{0,2},{2,4},{4,6},{6,8},{8,10},{10,12},{12,14},{14,16},{16,18},{18... | collective-permute-start | bytes 3145736 | tf_op jit(solution)/shard_map/ppermute | solution.py:21
  51.3 0.7 copy-start.12
  54.3 20.0 %collective-permute-start.7 = (f32[128,256]{1,0:T(8,128)}, f32[128,256]{1,0:T(8,128)S(1)}, u32[]{:S(2)}, u32[]{:S(2)}) collective-permute-start(f32[128,256]{1,0:T(8,128)} %small.6.refs_3_.refs_0_), channel_id=1, source_target_pairs={{0,8},{2,10},{4,12},{6,14},{8,0},{10,2},{12,4},{14,6},{16,24},{18,... | collective-permute-start | bytes 393224 | tf_op jit(solution)/shard_map/ppermute | solution.py:348
  65.3 4.6 %copy-start.9 = (f32[128,8,256]{2,1,0:T(8,128)}, f32[128,8,256]{2,1,0:T(8,128)S(1)}, u32[]{:S(2)}) copy-start(f32[128,8,256]{2,1,0:T(8,128)S(1)} %collective-permute-done.9.refs_2_) | copy-start | bytes 3145732
  69.9 1.0 copy-start.10
  74.3 0.7 copy-start.16
  77.2 15.9 %collective-permute-start.10 = (f32[128,256]{1,0:T(8,128)}, f32[128,256]{1,0:T(8,128)S(1)}, u32[]{:S(2)}, u32[]{:S(2)}) collective-permute-start(f32[128,256]{1,0:T(8,128)} %small.7.refs_4_.refs_0_), channel_id=1, source_target_pairs={{0,16},{2,18},{4,20},{6,22},{8,24},{10,26},{12,28},{14,30},{16,0},... | collective-permute-start | bytes 393224 | tf_op jit(solution)/shard_map/ppermute | solution.py:348
  88.3 47.5 %collective-permute-start.14 = (f32[256,8,256]{2,1,0:T(8,128)}, f32[256,8,256]{2,1,0:T(8,128)}, u32[]{:S(2)}, u32[]{:S(2)}) collective-permute-start(f32[256,8,256]{2,1,0:T(8,128)} %get-tuple-element.17.refs_2_.refs_0_), channel_id=1, source_target_pairs={{0,30},{2,0},{4,2},{6,4},{8,6},{10,8},{12,10},{14,12},{16,14},{18,... | collective-permute-start | bytes 6291464 | tf_op jit(solution)/shard_map/ppermute | solution.py:21
  90.8 45.0 %collective-permute-start.13 = (f32[256,8,256]{2,1,0:T(8,128)}, f32[256,8,256]{2,1,0:T(8,128)}, u32[]{:S(2)}, u32[]{:S(2)}) collective-permute-start(f32[256,8,256]{2,1,0:T(8,128)} %get-tuple-element.17.refs_2_.refs_0_), channel_id=1, source_target_pairs={{0,2},{2,4},{4,6},{6,8},{8,10},{10,12},{12,14},{14,16},{16,18},{18... | collective-permute-start | bytes 6291464 | tf_op jit(solution)/shard_map/ppermute | solution.py:21
  93.1 0.7 copy-start.13
  99.2 70.7 %collective-permute-start.16 = (f32[256,8,256]{2,1,0:T(8,128)}, f32[256,8,256]{2,1,0:T(8,128)}, u32[]{:S(2)}, u32[]{:S(2)}) collective-permute-start(f32[256,8,256]{2,1,0:T(8,128)} %copy.28.refs_5_), channel_id=1, source_target_pairs={{0,1},{1,0},{2,3},{3,2},{4,5},{5,4},{6,7},{7,6},{8,9},{9,8},{10,11... | collective-permute-start | bytes 6291464 | tf_op jit(solution)/shard_map/ppermute | solution.py:21
  133.3 45.7 %collective-permute-start.12 = (f32[256,8,256]{2,1,0:T(8,128)}, f32[256,8,256]{2,1,0:T(8,128)S(1)}, u32[]{:S(2)}, u32[]{:S(2)}) collective-permute-start(f32[256,8,256]{2,1,0:T(8,128)} %get-tuple-element.18.refs_4_.refs_0_), channel_id=1, source_target_pairs={{0,30},{2,0},{4,2},{6,4},{8,6},{10,8},{12,10},{14,12},{16,14},{18,... | collective-permute-start | bytes 6291464 | tf_op jit(solution)/shard_map/ppermute | solution.py:21
  135.8 43.2 %collective-permute-start.11 = (f32[256,8,256]{2,1,0:T(8,128)}, f32[256,8,256]{2,1,0:T(8,128)}, u32[]{:S(2)}, u32[]{:S(2)}) collective-permute-start(f32[256,8,256]{2,1,0:T(8,128)} %get-tuple-element.18.refs_4_.refs_0_), channel_id=1, source_target_pairs={{0,2},{2,4},{4,6},{6,8},{8,10},{10,12},{12,14},{14,16},{16,18},{18... | collective-permute-start | bytes 6291464 | tf_op jit(solution)/shard_map/ppermute | solution.py:21
  142.3 75.2 %collective-permute-start.15 = (f32[256,8,256]{2,1,0:T(8,128)}, f32[256,8,256]{2,1,0:T(8,128)}, u32[]{:S(2)}, u32[]{:S(2)}) collective-permute-start(f32[256,8,256]{2,1,0:T(8,128)} %copy.29.refs_5_), channel_id=1, source_target_pairs={{0,1},{1,0},{2,3},{3,2},{4,5},{5,4},{6,7},{7,6},{8,9},{9,8},{10,11... | collective-permute-start | bytes 6291464 | tf_op jit(solution)/shard_map/ppermute | solution.py:21
  176.5 36.6 %collective-permute-start.18 = (f32[128,8,256]{2,1,0:T(8,128)}, f32[128,8,256]{2,1,0:T(8,128)S(1)}, u32[]{:S(2)}, u32[]{:S(2)}) collective-permute-start(f32[128,8,256]{2,1,0:T(8,128)} %get-tuple-element.21.refs_4_.refs_0_), channel_id=1, source_target_pairs={{0,30},{2,0},{4,2},{6,4},{8,6},{10,8},{12,10},{14,12},{16,14},{18,... | collective-permute-start | bytes 3145736 | tf_op jit(solution)/shard_map/ppermute | solution.py:21
  179.0 34.1 %collective-permute-start.17 = (f32[128,8,256]{2,1,0:T(8,128)}, f32[128,8,256]{2,1,0:T(8,128)}, u32[]{:S(2)}, u32[]{:S(2)}) collective-permute-start(f32[128,8,256]{2,1,0:T(8,128)} %get-tuple-element.21.refs_4_.refs_0_), channel_id=1, source_target_pairs={{0,2},{2,4},{4,6},{6,8},{8,10},{10,12},{12,14},{14,16},{16,18},{18... | collective-permute-start | bytes 3145736 | tf_op jit(solution)/shard_map/ppermute | solution.py:21
  179.0 1.4 copy-start
  186.0 24.1 %collective-permute-start.19 = (f32[128,256]{1,0:T(8,128)}, f32[128,256]{1,0:T(8,128)S(1)}, u32[]{:S(2)}, u32[]{:S(2)}) collective-permute-start(f32[128,256]{1,0:T(8,128)} %small.9.refs_2_.refs_0_), channel_id=1, source_target_pairs={{0,2},{2,0},{4,6},{6,4},{8,10},{10,8},{12,14},{14,12},{16,18},{18,... | collective-permute-start | bytes 393224 | tf_op jit(solution)/shard_map/ppermute | solution.py:348
  208.6 34.7 %collective-permute-start.24 = (f32[128,8,256]{2,1,0:T(8,128)}, f32[128,8,256]{2,1,0:T(8,128)}, u32[]{:S(2)}, u32[]{:S(2)}) collective-permute-start(f32[128,8,256]{2,1,0:T(8,128)} %core_send.3.refs_2_), channel_id=1, source_target_pairs={{0,1},{1,0},{2,3},{3,2},{4,5},{5,4},{6,7},{7,6},{8,9},{9,8},{10,11... | collective-permute-start | bytes 3145736 | tf_op jit(solution)/shard_map/ppermute | solution.py:21
  210.1 0.7 copy-start.4
  213.1 1.0 copy-start.3
  222.5 28.8 %collective-permute-start.23 = (f32[128,8,256]{2,1,0:T(8,128)}, f32[128,8,256]{2,1,0:T(8,128)S(1)}, u32[]{:S(2)}, u32[]{:S(2)}) collective-permute-start(f32[128,8,256]{2,1,0:T(8,128)} %core.1.refs_3_.refs_0_), channel_id=1, source_target_pairs={{0,30},{2,0},{4,2},{6,4},{8,6},{10,8},{12,10},{14,12},{16,14},{18,... | collective-permute-start | bytes 3145736 | tf_op jit(solution)/shard_map/ppermute | solution.py:21
  222.5 30.3 %collective-permute-start.22 = (f32[128,8,256]{2,1,0:T(8,128)}, f32[128,8,256]{2,1,0:T(8,128)S(1)}, u32[]{:S(2)}, u32[]{:S(2)}) collective-permute-start(f32[128,8,256]{2,1,0:T(8,128)} %core.1.refs_3_.refs_0_), channel_id=1, source_target_pairs={{0,2},{2,4},{4,6},{6,8},{8,10},{10,12},{12,14},{14,16},{16,18},{18... | collective-permute-start | bytes 3145736 | tf_op jit(solution)/shard_map/ppermute | solution.py:21
  227.6 5.0 %collective-permute-start.20 = (f32[128,256]{1,0:T(8,128)}, f32[128,256]{1,0:T(8,128)S(1)}, u32[]{:S(2)}, u32[]{:S(2)}) collective-permute-start(f32[128,256]{1,0:T(8,128)} %get-tuple-element.23), channel_id=1, source_target_pairs={{0,2},{2,0},{4,6},{6,4},{8,10},{10,8},{12,14},{14,12},{16,18},{18,... | collective-permute-start | bytes 393224 | tf_op jit(solution)/shard_map/ppermute | solution.py:348
  232.0 38.5 %collective-permute-start.27 = (f32[128,8,256]{2,1,0:T(8,128)}, f32[128,8,256]{2,1,0:T(8,128)S(1)}, u32[]{:S(2)}, u32[]{:S(2)}) collective-permute-start(f32[128,8,256]{2,1,0:T(8,128)} %place.12.refs_2_), channel_id=1, source_target_pairs={{0,1},{1,0},{2,3},{3,2},{4,5},{5,4},{6,7},{7,6},{8,9},{9,8},{10,11... | collective-permute-start | bytes 3145736 | tf_op jit(solution)/shard_map/ppermute | solution.py:21
  232.6 0.7 copy-start.17
  235.6 25.6 %all-to-all-start = ((f32[32,8,128]{2,1,0:T(8,128)}), f32[32,8,128]{2,1,0:T(8,128)S(1)}, u32[]{:S(2)}, u32[]{:S(2)}) async-start(f32[32,8,128]{2,1,0:T(8,128)} %cut.1.refs_3_), calls=%async_computation | async-start | bytes 262144 | tf_op jit(solution)/shard_map/all_to_all | solution.py:420
  247.3 26.9 %collective-permute-start.26 = (f32[128,8,256]{2,1,0:T(8,128)}, f32[128,8,256]{2,1,0:T(8,128)}, u32[]{:S(2)}, u32[]{:S(2)}) collective-permute-start(f32[128,8,256]{2,1,0:T(8,128)} %core_finish.3.refs_4_.refs_0_), channel_id=1, source_target_pairs={{0,30},{2,0},{4,2},{6,4},{8,6},{10,8},{12,10},{14,12},{16,14},{18,... | collective-permute-start | bytes 3145736 | tf_op jit(solution)/shard_map/ppermute | solution.py:21
  251.3 22.9 %collective-permute-start.25 = (f32[128,8,256]{2,1,0:T(8,128)}, f32[128,8,256]{2,1,0:T(8,128)}, u32[]{:S(2)}, u32[]{:S(2)}) collective-permute-start(f32[128,8,256]{2,1,0:T(8,128)} %core_finish.3.refs_4_.refs_0_), channel_id=1, source_target_pairs={{0,2},{2,4},{4,6},{6,8},{8,10},{10,12},{12,14},{14,16},{16,18},{18... | collective-permute-start | bytes 3145736 | tf_op jit(solution)/shard_map/ppermute | solution.py:21
  251.3 1.6 copy-start.1
  251.3 34.2 %collective-permute-start.21 = (f32[128,8,256]{2,1,0:T(8,128)}, f32[128,8,256]{2,1,0:T(8,128)}, u32[]{:S(2)}, u32[]{:S(2)}) collective-permute-start(f32[128,8,256]{2,1,0:T(8,128)} %place.13.refs_3_), channel_id=1, source_target_pairs={{0,1},{1,0},{2,3},{3,2},{4,5},{5,4},{6,7},{7,6},{8,9},{9,8},{10,11... | collective-permute-start | bytes 3145736 | tf_op jit(solution)/shard_map/ppermute | solution.py:21
  252.8 1.0 copy-start.2
  261.1 0.7 copy-start.5
  264.1 21.6 %all-to-all-start.1 = ((f32[32,16,128]{2,1,0:T(8,128)}), f32[32,16,128]{2,1,0:T(8,128)}, u32[]{:S(2)}, u32[]{:S(2)}) async-start(f32[32,16,128]{2,1,0:T(8,128)} %sum.1.refs_2_), calls=%async_computation.1 | async-start | bytes 524288 | tf_op jit(solution)/shard_map/all_to_all | solution.py:427
  270.5 1.0 copy-start.8

commit v5 on v4

--- a/solution.py
+++ b/solution.py
@@ -102,7 +102,7 @@
     return pl.BlockSpec((z, rank), lambda p, w: (0, w[at]))
 
 
-def staged(sources, stages, targets, in_sems, out_sems):
+def staged(sources, stages, targets, in_sems, out_sems, meanwhile=None):
     loads = [pltpu.make_async_copy(a, b, in_sems.at[k]) for k, (a, b) in enumerate(zip(sources, stages))]
     stores = [pltpu.make_async_copy(a, b, out_sems.at[k]) for k, (a, b) in enumerate(zip(stages, targets))]
     for load in loads:
@@ -110,6 +110,8 @@
     for load, store in zip(loads, stores):
         load.wait()
         store.start()
+    if meanwhile is not None:
+        meanwhile()
     for store in stores:
         store.wait()
 
@@ -251,7 +253,7 @@
         out_ref[...] = upper_ref[...]
 
 
-def put_kernel(i, index_ref, part_ref, old_ref, core_ref, stage_ref, in_sems, out_sems):
+def put_kernel(i, index_ref, part_ref, old_ref, core_ref, stage_ref, in_sems, out_sems, meanwhile=None):
     count = in_sems.shape[0]
     slab = part_ref.shape[0] // count
     first = pl.multiple_of((index_ref[THEIRS] * (core_ref.shape[1] // (2 * TILE)) + i) * TILE, TILE)
@@ -261,6 +263,7 @@
         [core_ref.at[pl.ds(k * slab, slab), pl.ds(first, TILE), :] for k in range(count)],
         in_sems,
         out_sems,
+        meanwhile,
     )
 
 
@@ -281,21 +284,23 @@
     ]
     for load in loads:
         load.start()
-    put_kernel(i, index_ref, part_ref, old_ref, core_ref, stage_ref, in_sems, out_sems)
-    loads[0].wait()
-    stores[0].start()
-    loads[1].wait()
-    count, high, _ = pieces_stage.shape
-    for odd in range(2):
-        for t, rows, columns in tiles(count, z // 2, z):
-            place = slice(odd * z // 2 + rows.start, odd * z // 2 + rows.stop)
-            cross_stage[place, columns] = pieces_stage[t, odd * high // 2 : (odd + 1) * high // 2, :]
-
-    @pl.when(mine == 1)
-    def _():
-        cross_stage[...] = cross_stage[...].T
-
-    stores[1].start()
+    def gram():
+        loads[0].wait()
+        stores[0].start()
+        loads[1].wait()
+        count, high, _ = pieces_stage.shape
+        for odd in range(2):
+            for t, rows, columns in tiles(count, z // 2, z):
+                place = slice(odd * z // 2 + rows.start, odd * z // 2 + rows.stop)
+                cross_stage[place, columns] = pieces_stage[t, odd * high // 2 : (odd + 1) * high // 2, :]
+
+        @pl.when(mine == 1)
+        def _():
+            cross_stage[...] = cross_stage[...].T
+
+        stores[1].start()
+
+    put_kernel(i, index_ref, part_ref, old_ref, core_ref, stage_ref, in_sems, out_sems, gram)
     for store in stores:
         store.wait()
 

time: 291 us -> 290 us (level)
  Pallas kernels: 134 us -> 131 us
    pallas_call x34, Pallas kernels: 134 us -> 131 us  [call(): pl.pallas_call(body, out_shape=[jax.ShapeDtypeStruct(shape, jnp.float32)...]
  transfers between devices with their start and end apart: 30 -> 30, of which waited for: 8 -> 8; matrix products, arithmetic and copies ran while one was open for 0% -> 0% of each run, Pallas kernels for 44% -> 43%
where the time goes in v5:
time: 290 us; the launch traced here: 289 us
  Pallas kernels  131 us (45%)
  waiting for transfers between devices  81.7 us (28%)
  starting transfers between devices  63.6 us (22%)
  local copies, waits for them, and re-layouts  11.3 us (4%)
    pallas_call x34, Pallas kernels, call(): pl.pallas_call(body, out_shape=[jax.ShapeDtypeStruct(shape, jnp.float32)...  131 us
    ppermute x21, waiting for transfers between devices, shifted(): lax.ppermute(array, axis, [(i, (i + by) % length) for i in range(length)])  77.9 us
    ppermute x21, starting transfers between devices, shifted(): lax.ppermute(array, axis, [(i, (i + by) % length) for i in range(length)])  30.5 us
    ppermute x7, starting transfers between devices, exchanged(): lax.ppermute(part, 'xy', [(i, i ^ bit) for i in range(lax.axis_size('xy'))])  21.2 us
    unnamed x36, local copies, waits for them, and re-layouts  10.6 us
    all_to_all x1, starting transfers between devices, summed(): return lax.all_to_all(total, axes, split_axis=0, concat_axis=0, tiled=True)  6.43 us
  transfers between devices with their start and end apart: 30, of which 8 were waited for; matrix products, arithmetic and copies ran while one was open for 0% of the time, Pallas kernels for 43%

profile of v5, /device:TPU:0, one launch (start us, length us, event | category | flops | bytes accessed | tf_op | source)
XLA Modules:
  0.0 288.8 jit_solution(1701618496631169238)
XLA Ops:
  1.2 3.8 %core_send.2.refs_1_ = f32[128,8,256]{2,1,0:T(8,128)} custom-call(s32[3]{0:T(128)} %pad_add_fusion.index_ref, f32[256,256]{1,0:T(8,128)} %refs_0_.29, f32[256,64,256]{2,1,0:T(8,128)} %refs_1_.7), custom_call_target="tpu_custom_call" | custom-call | flops 30000001024 | tf_op jit(solution)/shard_map/core_send/pallas_call | solution.py:70
  5.0 3.0 %collective-permute-start.6 = (f32[128,8,256]{2,1,0:T(8,128)}, f32[128,8,256]{2,1,0:T(8,128)}, u32[]{:S(2)}, u32[]{:S(2)}) collective-permute-start(f32[128,8,256]{2,1,0:T(8,128)} %core_send.2.refs_1_), channel_id=1, source_target_pairs={{0,1},{1,0},{2,3},{3,2},{4,5},{5,4},{6,7},{7,6},{8,9},{9,8},{10,11... | collective-permute-start | bytes 3145736 | tf_op jit(solution)/shard_map/ppermute | solution.py:21
  10.2 3.3 %copy.26.refs_1_ = f32[256,8,256]{2,1,0:T(8,128)} custom-call(s32[3]{0:T(128)} %pad_add_fusion.index_ref, f32[256,64,256]{2,1,0:T(8,128)} %refs_1_.7, f32[256,128]{1,0:T(8,128)} %copy.25.refs_1_), custom_call_target="tpu_custom_call" | custom-call | flops 30000001024 | tf_op jit(solution)/shard_map/copy/pallas_call | solution.py:70
  16.2 16.5 %diagonal.1 = (f32[128,256]{1,0:T(8,128)}, f32[128,256]{1,0:T(8,128)}) custom-call(s32[7]{0:T(128)} %concatenate.4.index_ref, f32[256,64,256]{2,1,0:T(8,128)} %refs_1_.7, f32[256,8,256]{2,1,0:T(8,128)} %copy.26.refs_1_), custom_call_target="tpu_custom_call" | custom-call | flops 30000001024 | tf_op jit(solution)/shard_map/diagonal/pallas_call | solution.py:70
  32.7 3.2 %copy.27.refs_2_ = f32[256,8,256]{2,1,0:T(8,128)} custom-call(s32[7]{0:T(128)} %concatenate.4.index_ref, f32[256,64,256]{2,1,0:T(8,128)} %refs_1_.7, f32[128,256]{1,0:T(8,128)} %get-tuple-element.14.refs_1_.refs_0_), custom_call_target="tpu_custom_call" | custom-call | flops 30000001024 | tf_op jit(solution)/shard_map/copy/pallas_call | solution.py:70
  37.2 2.3 small.5.refs_2_.refs_0_
  41.7 2.4 join.2.refs_3_.refs_1_
  44.1 4.0 %core_finish.2.refs_2_.refs_0_ = f32[128,8,256]{2,1,0:T(8,128)} custom-call(s32[7]{0:T(128)} %concatenate.4.index_ref, f32[256,256]{1,0:T(8,128)} %refs_0_.29, f32[256,64,256]{2,1,0:T(8,128)} %refs_1_.7, f32[128,8,256]{2,1,0:T(8,128)} %collective-permute-done.6.refs_2_, f32[256,256]{1,0:T(8,128)} %join.2.refs_3_.refs_1_), custom_call_target="tpu_custom_call" | custom-call | flops 30000001024 | tf_op jit(solution)/shard_map/core_finish/pallas_call | solution.py:70
  48.1 3.2 %collective-permute-start.9 = (f32[128,8,256]{2,1,0:T(8,128)}, f32[128,8,256]{2,1,0:T(8,128)S(1)}, u32[]{:S(2)}, u32[]{:S(2)}) collective-permute-start(f32[128,8,256]{2,1,0:T(8,128)} %core_finish.2.refs_2_.refs_0_), channel_id=1, source_target_pairs={{0,30},{2,0},{4,2},{6,4},{8,6},{10,8},{12,10},{14,12},{16,14},{18,... | collective-permute-start | bytes 3145736 | tf_op jit(solution)/shard_map/ppermute | solution.py:21
  52.0 2.3 small.6.refs_3_.refs_0_
  54.3 11.1 %collective-permute-done.9.refs_2_ = f32[128,8,256]{2,1,0:T(8,128)S(1)} collective-permute-done((f32[128,8,256]{2,1,0:T(8,128)}, f32[128,8,256]{2,1,0:T(8,128)S(1)}, u32[]{:S(2)}, u32[]{:S(2)}) %collective-permute-start.9) | collective-permute-done | bytes 1048608 | tf_op jit(solution)/shard_map/ppermute | solution.py:21
  65.3 4.6 %collective-permute-done.8.refs_1_ = f32[128,8,256]{2,1,0:T(8,128)S(1)} collective-permute-done((f32[128,8,256]{2,1,0:T(8,128)}, f32[128,8,256]{2,1,0:T(8,128)S(1)}, u32[]{:S(2)}, u32[]{:S(2)}) %collective-permute-start.8) | collective-permute-done | bytes 1048608 | tf_op jit(solution)/shard_map/ppermute | solution.py:21
  70.9 3.1 %place.8.refs_2_.refs_3_ = f32[128,64,256]{2,1,0:T(8,128)} custom-call(s32[7]{0:T(128)} %concatenate.4.index_ref, f32[128,8,256]{2,1,0:T(8,128)} %core_finish.2.refs_2_.refs_0_, f32[128,8,256]{2,1,0:T(8,128)} %copy-done.10, f32[128,8,256]{2,1,0:T(8,128)} %copy-done.9, f32[128,256]{1,0:T(8,128)} %small.6.refs_3_.refs_0_), custom_call_target="tpu_custom_call" | custom-call | flops 30000001024 | tf_op jit(solution)/shard_map/place/pallas_call | solution.py:70
  74.6 2.3 small.7.refs_4_.refs_0_
  76.9 3.1 %collective-permute-done.4.refs_3_ = f32[256,8,256]{2,1,0:T(8,128)} collective-permute-done((f32[256,8,256]{2,1,0:T(8,128)}, f32[256,8,256]{2,1,0:T(8,128)}, u32[]{:S(2)}, u32[]{:S(2)}) %collective-permute-start.4) | collective-permute-done | bytes 2097184 | tf_op jit(solution)/shard_map/ppermute | solution.py:21
  80.0 8.3 %received.3 = (f32[256,8,256]{2,1,0:T(8,128)}, f32[256,256]{1,0:T(8,128)}) custom-call(s32[7]{0:T(128)} %concatenate.4.index_ref, f32[256,256]{1,0:T(8,128)} %refs_0_.29, f32[256,256]{1,0:T(8,128)} %join.2.refs_3_.refs_1_, f32[256,64,256]{2,1,0:T(8,128)} %refs_1_.7, f32[256,8,256]{2,1,0:T(8,128)} %collective-permute-done.4.refs_3_, ...), custom_call_target="tpu_custom_call" | custom-call | flops 30000001024 | tf_op jit(solution)/shard_map/received/pallas_call | solution.py:70
  88.3 2.5 collective-permute-start.14
  93.5 2.3 small.8.refs_1_.refs_0_
  95.8 3.1 %copy.28.refs_5_ = f32[256,8,256]{2,1,0:T(8,128)} custom-call(s32[7]{0:T(128)} %concatenate.4.index_ref, f32[256,64,256]{2,1,0:T(8,128)} %refs_1_.7, f32[128,256]{1,0:T(8,128)} %small.8.refs_1_.refs_0_), custom_call_target="tpu_custom_call" | custom-call | flops 30000001024 | tf_op jit(solution)/shard_map/copy/pallas_call | solution.py:70
  100.5 24.5 %collective-permute-done.3.refs_3_ = f32[256,8,256]{2,1,0:T(8,128)} collective-permute-done((f32[256,8,256]{2,1,0:T(8,128)}, f32[256,8,256]{2,1,0:T(8,128)}, u32[]{:S(2)}, u32[]{:S(2)}) %collective-permute-start.3) | collective-permute-done | bytes 2097184 | tf_op jit(solution)/shard_map/ppermute | solution.py:21
  125.0 8.3 %received.4 = (f32[256,8,256]{2,1,0:T(8,128)}, f32[256,256]{1,0:T(8,128)}) custom-call(s32[7]{0:T(128)} %concatenate.4.index_ref, f32[256,256]{1,0:T(8,128)} %refs_0_.29, f32[256,256]{1,0:T(8,128)} %join.2.refs_3_.refs_1_, f32[256,64,256]{2,1,0:T(8,128)} %refs_1_.7, f32[256,8,256]{2,1,0:T(8,128)} %collective-permute-done.3.refs_3_, ...), custom_call_target="tpu_custom_call" | custom-call | flops 30000001024 | tf_op jit(solution)/shard_map/received/pallas_call | solution.py:70
  133.3 2.5 collective-permute-start.12
  135.8 3.1 %place.9.refs_1_.refs_3_ = f32[128,64,256]{2,1,0:T(8,128)} custom-call(s32[7]{0:T(128)} %concatenate.4.index_ref, f32[256,8,256]{2,1,0:T(8,128)} %get-tuple-element.17.refs_2_.refs_0_, f32[256,8,256]{2,1,0:T(8,128)} %collective-permute-done.13.refs_1_, f32[256,8,256]{2,1,0:T(8,128)} %collective-permute-done.14.refs_2_, ...), custom_call_target="tpu_custom_call", output_to_operand_aliasing={{}: (4, {})} | custom-call | flops 8999999488 | tf_op jit(solution)/shard_map/place/pallas_call | solution.py:70
  138.9 3.1 %copy.29.refs_5_ = f32[256,8,256]{2,1,0:T(8,128)} custom-call(s32[7]{0:T(128)} %concatenate.4.index_ref, f32[256,64,256]{2,1,0:T(8,128)} %refs_1_.7, f32[128,64,256]{2,1,0:T(8,128)} %place.9.refs_1_.refs_3_), custom_call_target="tpu_custom_call" | custom-call | flops 8999999488 | tf_op jit(solution)/shard_map/copy/pallas_call | solution.py:70
  143.6 26.4 %collective-permute-done.16.refs_3_ = f32[256,8,256]{2,1,0:T(8,128)} collective-permute-done((f32[256,8,256]{2,1,0:T(8,128)}, f32[256,8,256]{2,1,0:T(8,128)}, u32[]{:S(2)}, u32[]{:S(2)}) %collective-permute-start.16) | collective-permute-done | bytes 2097184 | tf_op jit(solution)/shard_map/ppermute | solution.py:21
  169.9 6.6 %received.5 = (f32[128,8,256]{2,1,0:T(8,128)}, f32[256,256]{1,0:T(8,128)}) custom-call(s32[7]{0:T(128)} %concatenate.4.index_ref, f32[256,256]{1,0:T(8,128)} %refs_0_.29, f32[256,256]{1,0:T(8,128)} %join.2.refs_3_.refs_1_, f32[256,64,256]{2,1,0:T(8,128)} %refs_1_.7, f32[256,8,256]{2,1,0:T(8,128)} %collective-permute-done.16.refs_3_, ...), custom_call_target="tpu_custom_call" | custom-call | flops 30000001024 | tf_op jit(solution)/shard_map/received/pallas_call | solution.py:70
  176.5 2.5 collective-permute-start.18
  180.4 3.1 %place.10.refs_1_.refs_3_ = f32[128,64,256]{2,1,0:T(8,128)} custom-call(s32[7]{0:T(128)} %concatenate.4.index_ref, f32[256,8,256]{2,1,0:T(8,128)} %get-tuple-element.18.refs_4_.refs_0_, f32[256,8,256]{2,1,0:T(8,128)} %collective-permute-done.11.refs_1_, f32[256,8,256]{2,1,0:T(8,128)} %copy-done, ...), custom_call_target="tpu_custom_call", output_to_operand_aliasing={{}: (4, {})} | custom-call | flops 6000000000 | tf_op jit(solution)/shard_map/place/pallas_call | solution.py:70
  185.7 18.4 %collective-permute-start.19 = (f32[128,256]{1,0:T(8,128)}, f32[128,256]{1,0:T(8,128)S(1)}, u32[]{:S(2)}, u32[]{:S(2)}) collective-permute-start(f32[128,256]{1,0:T(8,128)} %small.9.refs_2_.refs_0_), channel_id=1, source_target_pairs={{0,2},{2,0},{4,6},{6,4},{8,10},{10,8},{12,14},{14,12},{16,18},{18,... | collective-permute-start | bytes 393224 | tf_op jit(solution)/shard_map/ppermute | solution.py:353
  204.2 3.8 %core_send.3.refs_2_ = f32[128,8,256]{2,1,0:T(8,128)} custom-call(s32[7]{0:T(128)} %concatenate.4.index_ref, f32[256,256]{1,0:T(8,128)} %refs_0_.29, f32[256,64,256]{2,1,0:T(8,128)} %refs_1_.7, f32[128,256]{1,0:T(8,128)} %small.9.refs_2_.refs_0_), custom_call_target="tpu_custom_call" | custom-call | flops 6000000000 | tf_op jit(solution)/shard_map/core_send/pallas_call | solution.py:70
  210.1 2.3 join.3.refs_4_.refs_1_
  213.5 3.1 %place.11.refs_4_.refs_3_ = f32[128,64,256]{2,1,0:T(8,128)} custom-call(s32[7]{0:T(128)} %concatenate.4.index_ref, f32[128,8,256]{2,1,0:T(8,128)} %get-tuple-element.21.refs_4_.refs_0_, f32[128,8,256]{2,1,0:T(8,128)} %collective-permute-done.17.refs_1_, f32[128,8,256]{2,1,0:T(8,128)} %copy-done.3, ...), custom_call_target="tpu_custom_call", output_to_operand_aliasing={{}: (4, {})} | custom-call | tf_op jit(solution)/shard_map/place/pallas_call | solution.py:70
  216.5 5.0 %core.1.refs_3_.refs_0_ = f32[128,8,256]{2,1,0:T(8,128)} custom-call(s32[7]{0:T(128)} %concatenate.4.index_ref, f32[256,256]{1,0:T(8,128)} %refs_0_.29, f32[256,256]{1,0:T(8,128)} %join.2.refs_3_.refs_1_, f32[256,64,256]{2,1,0:T(8,128)} %refs_1_.7, f32[256,8,256]{2,1,0:T(8,128)} %collective-permute-done.15.refs_3_.refs_1_, f32[128,64,256]{2,1,0:T(8,128)} %place.11.refs_4_.refs_3_), custom_call_target="tpu_custom_call" | custom-call | flops 30000001024 | tf_op jit(solution)/shard_map/core/pallas_call | solution.py:70
  222.4 4.6 %cross.1 = (f32[128,256]{1,0:T(8,128)}, f32[128,256]{1,0:T(8,128)}) custom-call(s32[7]{0:T(128)} %concatenate.4.index_ref, f32[256,64,256]{2,1,0:T(8,128)} %refs_1_.7, f32[256,8,256]{2,1,0:T(8,128)} %collective-permute-done.15.refs_3_.refs_1_, f32[256,256]{1,0:T(8,128)} %get-tuple-element.20.refs_2_, f32[128,8,256]{2,1,0:T(8,128)} %core.1.refs_3_.refs_0_), custom_call_target="tpu_custom_call" | custom-call | flops 30000001024 | tf_op jit(solution)/shard_map/cross/pallas_call | solution.py:70
  227.7 3.1 %place.12.refs_2_ = f32[128,8,256]{2,1,0:T(8,128)} custom-call(s32[7]{0:T(128)} %concatenate.4.index_ref, f32[256,8,256]{2,1,0:T(8,128)} %get-tuple-element.17.refs_2_.refs_0_, f32[256,8,256]{2,1,0:T(8,128)} %collective-permute-done.13.refs_1_, f32[256,8,256]{2,1,0:T(8,128)} %collective-permute-done.14.refs_2_, f32[128,256]{1,0:T(8,128)} %get-tuple-element.22.refs_3_.refs_0_), custom_call_target="tpu_custom_call" | custom-call | flops 30000001024 | tf_op jit(solution)/shard_map/place/pallas_call | solution.py:70
  232.4 2.3 cut.1.refs_3_
  234.7 5.5 %all-to-all-start = ((f32[32,8,128]{2,1,0:T(8,128)}), f32[32,8,128]{2,1,0:T(8,128)S(1)}, u32[]{:S(2)}, u32[]{:S(2)}) async-start(f32[32,8,128]{2,1,0:T(8,128)} %cut.1.refs_3_), calls=%async_computation | async-start | bytes 262144 | tf_op jit(solution)/shard_map/all_to_all | solution.py:425
  240.2 3.1 %place.13.refs_3_ = f32[128,8,256]{2,1,0:T(8,128)} custom-call(s32[7]{0:T(128)} %concatenate.4.index_ref, f32[256,8,256]{2,1,0:T(8,128)} %get-tuple-element.18.refs_4_.refs_0_, f32[256,8,256]{2,1,0:T(8,128)} %collective-permute-done.11.refs_1_, f32[256,8,256]{2,1,0:T(8,128)} %copy-done, f32[32,8,128]{2,1,0:T(8,128)} %cut.1.refs_3_), custom_call_target="tpu_custom_call" | custom-call | tf_op jit(solution)/shard_map/place/pallas_call | solution.py:70
  243.3 4.0 %core_finish.3.refs_4_.refs_0_ = f32[128,8,256]{2,1,0:T(8,128)} custom-call(s32[7]{0:T(128)} %concatenate.4.index_ref, f32[256,256]{1,0:T(8,128)} %refs_0_.29, f32[256,64,256]{2,1,0:T(8,128)} %refs_1_.7, f32[128,8,256]{2,1,0:T(8,128)} %collective-permute-done.24.refs_2_, f32[128,8,256]{2,1,0:T(8,128)} %place.13.refs_3_), custom_call_target="tpu_custom_call" | custom-call | flops 30000001024 | tf_op jit(solution)/shard_map/core_finish/pallas_call | solution.py:70
  247.3 4.6 %collective-permute-start.26 = (f32[128,8,256]{2,1,0:T(8,128)}, f32[128,8,256]{2,1,0:T(8,128)}, u32[]{:S(2)}, u32[]{:S(2)}) collective-permute-start(f32[128,8,256]{2,1,0:T(8,128)} %core_finish.3.refs_4_.refs_0_), channel_id=1, source_target_pairs={{0,30},{2,0},{4,2},{6,4},{8,6},{10,8},{12,10},{14,12},{16,14},{18,... | collective-permute-start | bytes 3145736 | tf_op jit(solution)/shard_map/ppermute | solution.py:21
  254.5 3.1 %place.14.refs_1_ = f32[128,64,256]{2,1,0:T(8,128)} custom-call(s32[7]{0:T(128)} %concatenate.4.index_ref, f32[128,8,256]{2,1,0:T(8,128)} %core.1.refs_3_.refs_0_, f32[128,8,256]{2,1,0:T(8,128)} %copy-done.2, f32[128,8,256]{2,1,0:T(8,128)} %copy-done.1, f32[128,64,256]{2,1,0:T(8,128)} %place.11.refs_4_.refs_3_, ...), custom_call_target="tpu_custom_call", output_to_operand_aliasing={{}: (4, {})} | custom-call | flops 3000000000 | tf_op jit(solution)/shard_map/place/pallas_call | solution.py:70
  257.5 3.6 %all-to-all-done.refs_0_ = f32[32,8,128]{2,1,0:T(8,128)S(1)} async-done(((f32[32,8,128]{2,1,0:T(8,128)}), f32[32,8,128]{2,1,0:T(8,128)S(1)}, u32[]{:S(2)}, u32[]{:S(2)}) %all-to-all-start) | async-done | bytes 131104 | tf_op jit(solution)/shard_map/all_to_all | solution.py:425
  261.8 2.3 sum.1.refs_2_
  264.1 6.4 %all-to-all-start.1 = ((f32[32,16,128]{2,1,0:T(8,128)}), f32[32,16,128]{2,1,0:T(8,128)}, u32[]{:S(2)}, u32[]{:S(2)}) async-start(f32[32,16,128]{2,1,0:T(8,128)} %sum.1.refs_2_), calls=%async_computation.1 | async-start | bytes 524288 | tf_op jit(solution)/shard_map/all_to_all | solution.py:432
  271.5 2.6 put.1.refs_3_
  274.2 3.1 %place.15.refs_3_ = f32[128,64,256]{2,1,0:T(8,128)} custom-call(s32[7]{0:T(128)} %concatenate.4.index_ref, f32[128,8,256]{2,1,0:T(8,128)} %core_finish.3.refs_4_.refs_0_, f32[128,8,256]{2,1,0:T(8,128)} %collective-permute-done.25.refs_1_, f32[128,8,256]{2,1,0:T(8,128)} %collective-permute-done.26.refs_2_, ...), custom_call_target="tpu_custom_call", output_to_operand_aliasing={{}: (4, {})} | custom-call | flops 89999998976 | tf_op jit(solution)/shard_map/place/pallas_call | solution.py:70
  277.2 8.2 %collective-permute-done.21.refs_0_ = f32[128,8,256]{2,1,0:T(8,128)} collective-permute-done((f32[128,8,256]{2,1,0:T(8,128)}, f32[128,8,256]{2,1,0:T(8,128)}, u32[]{:S(2)}, u32[]{:S(2)}) %collective-permute-start.21) | collective-permute-done | bytes 1048608 | tf_op jit(solution)/shard_map/ppermute | solution.py:21
  285.7 3.0 %last.1 = (f32[128,64,256]{2,1,0:T(8,128)}, f32[256,512]{1,0:T(8,128)}) custom-call(s32[7]{0:T(128)} %concatenate.4.index_ref, f32[128,8,256]{2,1,0:T(8,128)} %collective-permute-done.21.refs_0_, f32[256,256]{1,0:T(8,128)} %join.3.refs_4_.refs_1_, f32[32,16,128]{2,1,0:T(8,128)} %all-to-all-done.1.refs_2_, ...), custom_call_target="tpu_custom_call", output_to_operand_aliasing={{0}: (4, {})} | custom-call | flops 89999998976 | tf_op jit(solution)/shard_map/last/pallas_call | solution.py:70
  (85 shorter events, 31.6 us)
Async XLA Ops:
  5.0 39.1 %collective-permute-start.6 = (f32[128,8,256]{2,1,0:T(8,128)}, f32[128,8,256]{2,1,0:T(8,128)}, u32[]{:S(2)}, u32[]{:S(2)}) collective-permute-start(f32[128,8,256]{2,1,0:T(8,128)} %core_send.2.refs_1_), channel_id=1, source_target_pairs={{0,1},{1,0},{2,3},{3,2},{4,5},{5,4},{6,7},{7,6},{8,9},{9,8},{10,11... | collective-permute-start | bytes 3145736 | tf_op jit(solution)/shard_map/ppermute | solution.py:21
  10.2 5.2 %copy-start.6 = (s32[32]{0:T(128)S(1)}, s32[32]{0:T(128)}, u32[]{:S(2)}) copy-start(s32[32]{0:T(128)} %param.7) | copy-start | bytes 388
  10.2 5.2 %copy-start.7 = (s32[32]{0:T(128)S(1)}, s32[32]{0:T(128)}, u32[]{:S(2)}) copy-start(s32[32]{0:T(128)} %param.6) | copy-start | bytes 388
  10.2 25.8 %collective-permute-start = (f32[256,128]{1,0:T(8,128)}, f32[256,128]{1,0:T(8,128)S(1)}, u32[]{:S(2)}, u32[]{:S(2)}) collective-permute-start(f32[256,128]{1,0:T(8,128)} %copy.25.refs_1_), channel_id=1, source_target_pairs={{0,1},{1,0},{2,3},{3,2},{4,5},{5,4},{6,7},{7,6},{8,9},{9,8},{10,11... | collective-permute-start | bytes 393224 | tf_op jit(solution)/shard_map/ppermute | solution.py:21
  13.5 66.5 %collective-permute-start.4 = (f32[256,8,256]{2,1,0:T(8,128)}, f32[256,8,256]{2,1,0:T(8,128)}, u32[]{:S(2)}, u32[]{:S(2)}) collective-permute-start(f32[256,8,256]{2,1,0:T(8,128)} %copy.26.refs_1_), channel_id=1, source_target_pairs={{0,1},{1,0},{2,3},{3,2},{4,5},{5,4},{6,7},{7,6},{8,9},{9,8},{10,11... | collective-permute-start | bytes 6291464 | tf_op jit(solution)/shard_map/ppermute | solution.py:21
  32.7 3.8 %collective-permute-start.2 = (f32[128,256]{1,0:T(8,128)}, f32[128,256]{1,0:T(8,128)S(1)}, u32[]{:S(2)}, u32[]{:S(2)}) collective-permute-start(f32[128,256]{1,0:T(8,128)} %get-tuple-element.15), channel_id=1, source_target_pairs={{0,2},{2,0},{4,6},{6,4},{8,10},{10,8},{12,14},{14,12},{16,18},{18,... | collective-permute-start | bytes 393224 | tf_op jit(solution)/shard_map/ppermute | solution.py:353
  35.9 89.1 %collective-permute-start.3 = (f32[256,8,256]{2,1,0:T(8,128)}, f32[256,8,256]{2,1,0:T(8,128)}, u32[]{:S(2)}, u32[]{:S(2)}) collective-permute-start(f32[256,8,256]{2,1,0:T(8,128)} %copy.27.refs_2_), channel_id=1, source_target_pairs={{0,1},{1,0},{2,3},{3,2},{4,5},{5,4},{6,7},{7,6},{8,9},{9,8},{10,11... | collective-permute-start | bytes 6291464 | tf_op jit(solution)/shard_map/ppermute | solution.py:21
  36.1 3.4 %copy-start.11 = (f32[256,128]{1,0:T(8,128)}, f32[256,128]{1,0:T(8,128)S(1)}, u32[]{:S(2)}) copy-start(f32[256,128]{1,0:T(8,128)S(1)} %collective-permute-done.refs_0_) | copy-start | bytes 393220
  36.1 5.0 %collective-permute-start.1 = (f32[256,128]{1,0:T(8,128)S(1)}, f32[256,128]{1,0:T(8,128)S(1)}, u32[]{:S(2)}, u32[]{:S(2)}) collective-permute-start(f32[256,128]{1,0:T(8,128)S(1)} %collective-permute-done.refs_0_), channel_id=1, source_target_pairs={{0,2},{2,0},{4,6},{6,4},{8,10},{10,8},{12,14},{14,12},{16,18},{18,... | collective-permute-start | bytes 393224 | tf_op jit(solution)/shard_map/ppermute | solution.py:353
  36.5 0.7 copy-start.14
  39.5 11.8 %collective-permute-start.5 = (f32[128,256]{1,0:T(8,128)}, f32[128,256]{1,0:T(8,128)S(1)}, u32[]{:S(2)}, u32[]{:S(2)}) collective-permute-start(f32[128,256]{1,0:T(8,128)} %small.5.refs_2_.refs_0_), channel_id=1, source_target_pairs={{0,4},{2,6},{4,0},{6,2},{8,12},{10,14},{12,8},{14,10},{16,20},{18,... | collective-permute-start | bytes 393224 | tf_op jit(solution)/shard_map/ppermute | solution.py:353
  41.1 0.7 copy-start.15
  48.1 17.2 %collective-permute-start.9 = (f32[128,8,256]{2,1,0:T(8,128)}, f32[128,8,256]{2,1,0:T(8,128)S(1)}, u32[]{:S(2)}, u32[]{:S(2)}) collective-permute-start(f32[128,8,256]{2,1,0:T(8,128)} %core_finish.2.refs_2_.refs_0_), channel_id=1, source_target_pairs={{0,30},{2,0},{4,2},{6,4},{8,6},{10,8},{12,10},{14,12},{16,14},{18,... | collective-permute-start | bytes 3145736 | tf_op jit(solution)/shard_map/ppermute | solution.py:21
  51.3 18.6 %collective-permute-start.8 = (f32[128,8,256]{2,1,0:T(8,128)}, f32[128,8,256]{2,1,0:T(8,128)S(1)}, u32[]{:S(2)}, u32[]{:S(2)}) collective-permute-start(f32[128,8,256]{2,1,0:T(8,128)} %core_finish.2.refs_2_.refs_0_), channel_id=1, source_target_pairs={{0,2},{2,4},{4,6},{6,8},{8,10},{10,12},{12,14},{14,16},{16,18},{18... | collective-permute-start | bytes 3145736 | tf_op jit(solution)/shard_map/ppermute | solution.py:21
  51.3 0.7 copy-start.12
  54.3 19.7 %collective-permute-start.7 = (f32[128,256]{1,0:T(8,128)}, f32[128,256]{1,0:T(8,128)S(1)}, u32[]{:S(2)}, u32[]{:S(2)}) collective-permute-start(f32[128,256]{1,0:T(8,128)} %small.6.refs_3_.refs_0_), channel_id=1, source_target_pairs={{0,8},{2,10},{4,12},{6,14},{8,0},{10,2},{12,4},{14,6},{16,24},{18,... | collective-permute-start | bytes 393224 | tf_op jit(solution)/shard_map/ppermute | solution.py:353
  65.3 4.6 %copy-start.9 = (f32[128,8,256]{2,1,0:T(8,128)}, f32[128,8,256]{2,1,0:T(8,128)S(1)}, u32[]{:S(2)}) copy-start(f32[128,8,256]{2,1,0:T(8,128)S(1)} %collective-permute-done.9.refs_2_) | copy-start | bytes 3145732
  69.9 1.0 copy-start.10
  74.0 0.7 copy-start.16
  76.9 15.9 %collective-permute-start.10 = (f32[128,256]{1,0:T(8,128)}, f32[128,256]{1,0:T(8,128)S(1)}, u32[]{:S(2)}, u32[]{:S(2)}) collective-permute-start(f32[128,256]{1,0:T(8,128)} %small.7.refs_4_.refs_0_), channel_id=1, source_target_pairs={{0,16},{2,18},{4,20},{6,22},{8,24},{10,26},{12,28},{14,30},{16,0},... | collective-permute-start | bytes 393224 | tf_op jit(solution)/shard_map/ppermute | solution.py:353
  88.3 47.5 %collective-permute-start.14 = (f32[256,8,256]{2,1,0:T(8,128)}, f32[256,8,256]{2,1,0:T(8,128)}, u32[]{:S(2)}, u32[]{:S(2)}) collective-permute-start(f32[256,8,256]{2,1,0:T(8,128)} %get-tuple-element.17.refs_2_.refs_0_), channel_id=1, source_target_pairs={{0,30},{2,0},{4,2},{6,4},{8,6},{10,8},{12,10},{14,12},{16,14},{18,... | collective-permute-start | bytes 6291464 | tf_op jit(solution)/shard_map/ppermute | solution.py:21
  90.8 45.0 %collective-permute-start.13 = (f32[256,8,256]{2,1,0:T(8,128)}, f32[256,8,256]{2,1,0:T(8,128)}, u32[]{:S(2)}, u32[]{:S(2)}) collective-permute-start(f32[256,8,256]{2,1,0:T(8,128)} %get-tuple-element.17.refs_2_.refs_0_), channel_id=1, source_target_pairs={{0,2},{2,4},{4,6},{6,8},{8,10},{10,12},{12,14},{14,16},{16,18},{18... | collective-permute-start | bytes 6291464 | tf_op jit(solution)/shard_map/ppermute | solution.py:21
  92.8 0.7 copy-start.13
  98.9 71.0 %collective-permute-start.16 = (f32[256,8,256]{2,1,0:T(8,128)}, f32[256,8,256]{2,1,0:T(8,128)}, u32[]{:S(2)}, u32[]{:S(2)}) collective-permute-start(f32[256,8,256]{2,1,0:T(8,128)} %copy.28.refs_5_), channel_id=1, source_target_pairs={{0,1},{1,0},{2,3},{3,2},{4,5},{5,4},{6,7},{7,6},{8,9},{9,8},{10,11... | collective-permute-start | bytes 6291464 | tf_op jit(solution)/shard_map/ppermute | solution.py:21
  133.3 45.7 %collective-permute-start.12 = (f32[256,8,256]{2,1,0:T(8,128)}, f32[256,8,256]{2,1,0:T(8,128)S(1)}, u32[]{:S(2)}, u32[]{:S(2)}) collective-permute-start(f32[256,8,256]{2,1,0:T(8,128)} %get-tuple-element.18.refs_4_.refs_0_), channel_id=1, source_target_pairs={{0,30},{2,0},{4,2},{6,4},{8,6},{10,8},{12,10},{14,12},{16,14},{18,... | collective-permute-start | bytes 6291464 | tf_op jit(solution)/shard_map/ppermute | solution.py:21
  135.8 43.2 %collective-permute-start.11 = (f32[256,8,256]{2,1,0:T(8,128)}, f32[256,8,256]{2,1,0:T(8,128)}, u32[]{:S(2)}, u32[]{:S(2)}) collective-permute-start(f32[256,8,256]{2,1,0:T(8,128)} %get-tuple-element.18.refs_4_.refs_0_), channel_id=1, source_target_pairs={{0,2},{2,4},{4,6},{6,8},{8,10},{10,12},{12,14},{14,16},{16,18},{18... | collective-permute-start | bytes 6291464 | tf_op jit(solution)/shard_map/ppermute | solution.py:21
  142.0 74.6 %collective-permute-start.15 = (f32[256,8,256]{2,1,0:T(8,128)}, f32[256,8,256]{2,1,0:T(8,128)}, u32[]{:S(2)}, u32[]{:S(2)}) collective-permute-start(f32[256,8,256]{2,1,0:T(8,128)} %copy.29.refs_5_), channel_id=1, source_target_pairs={{0,1},{1,0},{2,3},{3,2},{4,5},{5,4},{6,7},{7,6},{8,9},{9,8},{10,11... | collective-permute-start | bytes 6291464 | tf_op jit(solution)/shard_map/ppermute | solution.py:21
  176.5 36.0 %collective-permute-start.18 = (f32[128,8,256]{2,1,0:T(8,128)}, f32[128,8,256]{2,1,0:T(8,128)S(1)}, u32[]{:S(2)}, u32[]{:S(2)}) collective-permute-start(f32[128,8,256]{2,1,0:T(8,128)} %get-tuple-element.21.refs_4_.refs_0_), channel_id=1, source_target_pairs={{0,30},{2,0},{4,2},{6,4},{8,6},{10,8},{12,10},{14,12},{16,14},{18,... | collective-permute-start | bytes 3145736 | tf_op jit(solution)/shard_map/ppermute | solution.py:21
  179.0 33.5 %collective-permute-start.17 = (f32[128,8,256]{2,1,0:T(8,128)}, f32[128,8,256]{2,1,0:T(8,128)}, u32[]{:S(2)}, u32[]{:S(2)}) collective-permute-start(f32[128,8,256]{2,1,0:T(8,128)} %get-tuple-element.21.refs_4_.refs_0_), channel_id=1, source_target_pairs={{0,2},{2,4},{4,6},{6,8},{8,10},{10,12},{12,14},{14,16},{16,18},{18... | collective-permute-start | bytes 3145736 | tf_op jit(solution)/shard_map/ppermute | solution.py:21
  179.0 1.4 copy-start
  185.7 23.8 %collective-permute-start.19 = (f32[128,256]{1,0:T(8,128)}, f32[128,256]{1,0:T(8,128)S(1)}, u32[]{:S(2)}, u32[]{:S(2)}) collective-permute-start(f32[128,256]{1,0:T(8,128)} %small.9.refs_2_.refs_0_), channel_id=1, source_target_pairs={{0,2},{2,0},{4,6},{6,4},{8,10},{10,8},{12,14},{14,12},{16,18},{18,... | collective-permute-start | bytes 393224 | tf_op jit(solution)/shard_map/ppermute | solution.py:353
  208.0 35.3 %collective-permute-start.24 = (f32[128,8,256]{2,1,0:T(8,128)}, f32[128,8,256]{2,1,0:T(8,128)}, u32[]{:S(2)}, u32[]{:S(2)}) collective-permute-start(f32[128,8,256]{2,1,0:T(8,128)} %core_send.3.refs_2_), channel_id=1, source_target_pairs={{0,1},{1,0},{2,3},{3,2},{4,5},{5,4},{6,7},{7,6},{8,9},{9,8},{10,11... | collective-permute-start | bytes 3145736 | tf_op jit(solution)/shard_map/ppermute | solution.py:21
  209.5 0.7 copy-start.4
  212.5 1.0 copy-start.3
  221.6 30.3 %collective-permute-start.23 = (f32[128,8,256]{2,1,0:T(8,128)}, f32[128,8,256]{2,1,0:T(8,128)S(1)}, u32[]{:S(2)}, u32[]{:S(2)}) collective-permute-start(f32[128,8,256]{2,1,0:T(8,128)} %core.1.refs_3_.refs_0_), channel_id=1, source_target_pairs={{0,30},{2,0},{4,2},{6,4},{8,6},{10,8},{12,10},{14,12},{16,14},{18,... | collective-permute-start | bytes 3145736 | tf_op jit(solution)/shard_map/ppermute | solution.py:21
  222.4 31.1 %collective-permute-start.22 = (f32[128,8,256]{2,1,0:T(8,128)}, f32[128,8,256]{2,1,0:T(8,128)S(1)}, u32[]{:S(2)}, u32[]{:S(2)}) collective-permute-start(f32[128,8,256]{2,1,0:T(8,128)} %core.1.refs_3_.refs_0_), channel_id=1, source_target_pairs={{0,2},{2,4},{4,6},{6,8},{8,10},{10,12},{12,14},{14,16},{16,18},{18... | collective-permute-start | bytes 3145736 | tf_op jit(solution)/shard_map/ppermute | solution.py:21
  227.0 4.7 %collective-permute-start.20 = (f32[128,256]{1,0:T(8,128)}, f32[128,256]{1,0:T(8,128)S(1)}, u32[]{:S(2)}, u32[]{:S(2)}) collective-permute-start(f32[128,256]{1,0:T(8,128)} %get-tuple-element.23), channel_id=1, source_target_pairs={{0,2},{2,0},{4,6},{6,4},{8,10},{10,8},{12,14},{14,12},{16,18},{18,... | collective-permute-start | bytes 393224 | tf_op jit(solution)/shard_map/ppermute | solution.py:353
  230.7 39.8 %collective-permute-start.27 = (f32[128,8,256]{2,1,0:T(8,128)}, f32[128,8,256]{2,1,0:T(8,128)S(1)}, u32[]{:S(2)}, u32[]{:S(2)}) collective-permute-start(f32[128,8,256]{2,1,0:T(8,128)} %place.12.refs_2_), channel_id=1, source_target_pairs={{0,1},{1,0},{2,3},{3,2},{4,5},{5,4},{6,7},{7,6},{8,9},{9,8},{10,11... | collective-permute-start | bytes 3145736 | tf_op jit(solution)/shard_map/ppermute | solution.py:21
  231.7 0.7 copy-start.17
  234.7 26.4 %all-to-all-start = ((f32[32,8,128]{2,1,0:T(8,128)}), f32[32,8,128]{2,1,0:T(8,128)S(1)}, u32[]{:S(2)}, u32[]{:S(2)}) async-start(f32[32,8,128]{2,1,0:T(8,128)} %cut.1.refs_3_), calls=%async_computation | async-start | bytes 262144 | tf_op jit(solution)/shard_map/all_to_all | solution.py:425
  247.3 26.9 %collective-permute-start.26 = (f32[128,8,256]{2,1,0:T(8,128)}, f32[128,8,256]{2,1,0:T(8,128)}, u32[]{:S(2)}, u32[]{:S(2)}) collective-permute-start(f32[128,8,256]{2,1,0:T(8,128)} %core_finish.3.refs_4_.refs_0_), channel_id=1, source_target_pairs={{0,30},{2,0},{4,2},{6,4},{8,6},{10,8},{12,10},{14,12},{16,14},{18,... | collective-permute-start | bytes 3145736 | tf_op jit(solution)/shard_map/ppermute | solution.py:21
  251.9 22.3 %collective-permute-start.25 = (f32[128,8,256]{2,1,0:T(8,128)}, f32[128,8,256]{2,1,0:T(8,128)}, u32[]{:S(2)}, u32[]{:S(2)}) collective-permute-start(f32[128,8,256]{2,1,0:T(8,128)} %core_finish.3.refs_4_.refs_0_), channel_id=1, source_target_pairs={{0,2},{2,4},{4,6},{6,8},{8,10},{10,12},{12,14},{14,16},{16,18},{18... | collective-permute-start | bytes 3145736 | tf_op jit(solution)/shard_map/ppermute | solution.py:21
  251.9 1.6 copy-start.1
  251.9 33.6 %collective-permute-start.21 = (f32[128,8,256]{2,1,0:T(8,128)}, f32[128,8,256]{2,1,0:T(8,128)}, u32[]{:S(2)}, u32[]{:S(2)}) collective-permute-start(f32[128,8,256]{2,1,0:T(8,128)} %place.13.refs_3_), channel_id=1, source_target_pairs={{0,1},{1,0},{2,3},{3,2},{4,5},{5,4},{6,7},{7,6},{8,9},{9,8},{10,11... | collective-permute-start | bytes 3145736 | tf_op jit(solution)/shard_map/ppermute | solution.py:21
  253.5 1.0 copy-start.2
  261.1 0.7 copy-start.5
  264.1 21.6 %all-to-all-start.1 = ((f32[32,16,128]{2,1,0:T(8,128)}), f32[32,16,128]{2,1,0:T(8,128)}, u32[]{:S(2)}, u32[]{:S(2)}) async-start(f32[32,16,128]{2,1,0:T(8,128)} %sum.1.refs_2_), calls=%async_computation.1 | async-start | bytes 524288 | tf_op jit(solution)/shard_map/all_to_all | solution.py:432
  270.5 1.0 copy-start.8
